TPU v7x, 128 devices: a whole 4x4x4 slice. The times are simulated.
128 devices in a mesh: dp: 4 (over y), ctx: 32 (over z, x, core).
Axes of the slice: x: 4, y: 4, z: 4, core: 2. Of those that a mesh axis runs over, the one named last changes fastest.
Arguments:
- tokens: bfloat16 [4, 20480, 4096], P('dp', 'ctx'), may hold values from -400 to 400
- w_query: bfloat16 [4096, 1024], P(('dp', 'ctx')), may hold values from -0.09375 to 0.09375
- w_key: bfloat16 [4096, 1024], P(('dp', 'ctx')), may hold values from -0.09375 to 0.09375
- w_value: bfloat16 [4096, 2048], P(('dp', 'ctx')), may hold values from -0.09375 to 0.09375
- w_gates: bfloat16 [4096, 8], P(('dp', 'ctx')), may hold values from -0.09375 to 0.09375
- forget_bias: float32 [4], replicated, may hold values from 2 to 15
- doc_lengths: int32 [4, 16], P('dp'), may hold values from 1 to 10240, 20480 in all within a row
Outputs:
- head_out: bfloat16 [4, 20480, 2048], P('dp', 'ctx')
Inputs may be any that keep to these rules, and one draw needn't show every extreme that they name: `doc_lengths`: each sequence's 16 lengths sum to 20480; the longest is exactly 10240.
All inputs are finite; a program needn't handle non-finite values.
Results may differ from a plain program's by a relative error of at most 0.025.
Values may be sent and summed in bfloat16 or wider, within the bound.
No kernel may reach another device: no remote copies, remote signals or barrier semaphores. Data moves between devices by JAX's collectives and lax.ppermute only.
A program may use at most 128 MiB of HBM per device.

v0:
```python
import functools
import itertools

import jax
import jax.numpy as jnp
from jax import lax
from jax.experimental import pallas as pl
from jax.experimental.pallas import tpu as pltpu
from jax.sharding import Mesh, PartitionSpec as P

ROWS = 640
DQK = 256
DV = 512
OWN = 32
PIECE = 64
EXTRA = 16
WIDE = 512
BF = jnp.bfloat16
F32 = jnp.float32
COST = pl.CostEstimate(flops=0, bytes_accessed=1 << 10, transcendentals=0)
SMALL = pltpu.CompilerParams(vmem_limit_bytes=20 * 1024 * 1024)
PARAMS = pltpu.CompilerParams(vmem_limit_bytes=20 * 1024 * 1024)


def swap(value):
    return lax.ppermute(value, "core", [(0, 1), (1, 0)])


def shift(value, axis, by):
    return lax.ppermute(value, axis, [(i, (i + by) % 4) for i in range(4)])


def hop(value, axes, by):
    names, pairs = ("y", "z", "x", "core"), []
    for source in itertools.product(range(4), range(4), range(4), range(2)):
        target = list(source)
        at = names.index(axes[source[3]])
        target[at] = (target[at] + by) % 4
        flat = [((p[0] * 4 + p[1]) * 4 + p[2]) * 2 + p[3] for p in (source, target)]
        pairs.append(tuple(flat))
    return lax.ppermute(value, names, pairs)


def around(value, axes):
    return (value,) + tuple(hop(value, axes, by) for by in (3, 2, 1))


def places(at):
    return jnp.stack([at, (at + 1) % 4, (at + 2) % 4, (at + 3) % 4]).astype(jnp.int32)


def normalize_kernel(places, own_ref, mate_ref, w_gates_ref, gates_ref, out_ref, *refs):
    chunks, by_y, scratch = refs[:4], refs[4:8], refs[8]
    raw = jnp.where(pl.program_id(0) == 0, own_ref[...], mate_ref[...])
    values = raw.astype(F32)
    scale = lax.rsqrt(jnp.mean(values * values, axis=-1, keepdims=True) + 1e-06)
    normed = (values * scale).astype(BF)
    out_ref[...] = normed
    gates_ref[...] = lax.dot_general(
        w_gates_ref[...], normed, (((1,), (1,)), ((), ())), preferred_element_type=F32
    )

    def reorder(last_step, other_step):
        for last in range(4):
            for other in range(4):
                for pair in range(2):
                    halves = []
                    for y in (2 * pair, 2 * pair + 1):
                        start = y * 1024 + last * last_step + other * other_step
                        halves.append(out_ref[:, start : start + 64])
                    start = last * 1024 + other * 256 + pair * 128
                    scratch[:, start : start + 128] = jnp.concatenate(halves, axis=1)

    pl.when(places[4] == 0)(lambda: reorder(64, 256))
    pl.when(places[4] == 1)(lambda: reorder(256, 64))
    for which in range(4):
        start = pl.multiple_of(places[which] * 1024, 1024)
        chunks[which][...] = scratch[:, pl.ds(start, 1024)]
        start = pl.multiple_of(places[5 + which] * 1024, 1024)
        by_y[which][...] = out_ref[:, pl.ds(start, 1024)]


def normalize(places, own, mate, w_gates):
    tile = 128
    steps = ROWS // tile
    return pl.pallas_call(
        normalize_kernel,
        grid_spec=pltpu.PrefetchScalarGridSpec(
            num_scalar_prefetch=1,
            grid=(2, steps),
            in_specs=[
                pl.BlockSpec((tile, 4096), lambda s, i, p: (jnp.where(s == 0, i, steps - 1), 0)),
                pl.BlockSpec((tile, 4096), lambda s, i, p: (jnp.where(s == 0, 0, i), 0)),
                pl.BlockSpec((EXTRA, 4096), lambda s, i, p: (0, 0)),
            ],
            out_specs=[pl.BlockSpec((EXTRA, tile), lambda s, i, p: (0, s * steps + i))]
            + [pl.BlockSpec((tile, 4096), lambda s, i, p: (s * steps + i, 0))]
            + [pl.BlockSpec((tile, 1024), lambda s, i, p: (s * steps + i, 0))] * 8,
            scratch_shapes=[pltpu.VMEM((tile, 4096), BF)],
        ),
        out_shape=[
            jax.ShapeDtypeStruct((EXTRA, 2 * ROWS), F32),
            jax.ShapeDtypeStruct((2 * ROWS, 4096), BF),
        ]
        + [jax.ShapeDtypeStruct((2 * ROWS, 1024), BF)] * 8,
        compiler_params=PARAMS,
        cost_estimate=pl.CostEstimate(flops=0, bytes_accessed=32 << 20, transcendentals=0),
        name="normalize",
    )(places, own, mate, w_gates)


def prepare_kernel(
    core_ref, query, key, value, mate_query, mate_key, mate_value, region, held_ref, q_ref, rest_ref
):
    core = core_ref[0]
    narrow = pl.ds(pl.multiple_of(core * WIDE, WIDE), WIDE)
    wide = pl.ds(pl.multiple_of(core * 2 * WIDE, WIDE), 2 * WIDE)
    for source, rows in (((query, key, value), core), ((mate_query, mate_key, mate_value), 1 - core)):
        rows = pl.ds(pl.multiple_of(rows * OWN, OWN), OWN)
        q_ref[rows, :] = source[0][:, narrow]
        held_ref[rows, :] = source[1][:, narrow]
        rest_ref[rows, :] = source[2][:, wide]
    held_ref[PIECE:, :] = region[...]


def prepare(core, own, mate, region):
    vmem = pl.BlockSpec(memory_space=pltpu.VMEM)
    return pl.pallas_call(
        prepare_kernel,
        in_specs=[pl.BlockSpec(memory_space=pltpu.SMEM)] + [vmem] * 7,
        out_specs=[vmem] * 3,
        out_shape=[
            jax.ShapeDtypeStruct((PIECE + EXTRA, WIDE), BF),
            jax.ShapeDtypeStruct((PIECE, WIDE), BF),
            jax.ShapeDtypeStruct((PIECE, 2 * WIDE), BF),
        ],
        compiler_params=PARAMS,
        cost_estimate=COST,
        name="prepare",
    )(core, *own, *mate, region)


def weave_kernel(groups, places, *refs):
    blocks, out, held, sems_in, sem_out = refs[:4], *refs[4:]

    def run(target):
        copies = [
            pltpu.make_async_copy(block, target(places[which]), sems_in.at[which])
            for which, block in enumerate(blocks)
        ]
        for copy in copies:
            copy.start()
        for copy in copies:
            copy.wait()

    if groups:
        pl.when(places[4] == 0)(lambda: run(lambda place: held.at[:, place]))
        pl.when(places[4] == 1)(lambda: run(lambda place: held.at[place]))
    else:
        run(lambda place: held.at[place])
    store = pltpu.make_async_copy(held, out, sem_out)
    store.start()
    store.wait()


def weave(places, blocks, groups):
    hbm = pl.BlockSpec(memory_space=pl.ANY)
    shape = (4, 4, PIECE, WIDE) if groups else (4, PIECE, WIDE)
    blocks = [block.reshape(shape[1:]) for block in blocks]
    return pl.pallas_call(
        functools.partial(weave_kernel, groups),
        in_specs=[pl.BlockSpec(memory_space=pltpu.SMEM)] + [hbm] * 4,
        out_specs=hbm,
        out_shape=jax.ShapeDtypeStruct(shape, BF),
        scratch_shapes=[
            pltpu.VMEM(shape, BF),
            pltpu.SemaphoreType.DMA((4,)),
            pltpu.SemaphoreType.DMA,
        ],
        compiler_params=PARAMS,
        cost_estimate=COST,
        name="weave",
    )(places, *blocks).reshape(-1, WIDE)


def assemble_kernel(rows, final, places, *refs):
    blocks, out, held, regions, sems_in, sems_more, sems_out = refs[:4], refs[4:-5], *refs[-5:]
    loads, extras = [], []
    for which, block in enumerate(blocks):
        start = pl.multiple_of(places[which] * rows, PIECE)
        loads.append(
            pltpu.make_async_copy(
                block.at[pl.ds(0, rows), :], held.at[pl.ds(start, rows), :], sems_in.at[which]
            )
        )
        extras.append(
            pltpu.make_async_copy(
                block.at[pl.ds(rows, EXTRA), :], regions.at[which], sems_more.at[which]
            )
        )
    for copy in extras + loads:
        copy.start()
    for copy in extras:
        copy.wait()
    held[4 * rows :, :] = (regions[0] + regions[1]) + (regions[2] + regions[3])
    for copy in loads:
        copy.wait()
    if final:
        stores = [
            pltpu.make_async_copy(held.at[pl.ds(0, 4 * rows), :], out[0], sems_out.at[0]),
            pltpu.make_async_copy(held.at[pl.ds(4 * rows, EXTRA), :], out[1], sems_out.at[1]),
        ]
    else:
        stores = [pltpu.make_async_copy(held, out[0], sems_out.at[0])]
    for copy in stores:
        copy.start()
    for copy in stores:
        copy.wait()


def assemble(places, blocks, rows, final):
    hbm = pl.BlockSpec(memory_space=pl.ANY)
    if final:
        shapes = [(4 * rows, WIDE), (EXTRA, WIDE)]
    else:
        shapes = [(4 * rows + EXTRA, WIDE)]
    return pl.pallas_call(
        functools.partial(assemble_kernel, rows, final),
        in_specs=[pl.BlockSpec(memory_space=pltpu.SMEM)] + [hbm] * 4,
        out_specs=[hbm] * len(shapes),
        out_shape=[jax.ShapeDtypeStruct(shape, BF) for shape in shapes],
        scratch_shapes=[
            pltpu.VMEM((4 * rows + EXTRA, WIDE), BF),
            pltpu.VMEM((4, EXTRA, WIDE), BF),
            pltpu.SemaphoreType.DMA((4,)),
            pltpu.SemaphoreType.DMA((4,)),
            pltpu.SemaphoreType.DMA((2,)),
        ],
        compiler_params=PARAMS,
        cost_estimate=COST,
        name="assemble",
    )(places, *blocks)


def together(*values):
    return lax.optimization_barrier(values)


def project(chunks, weights, total=None):
    for chunk, weight in zip(chunks, weights):
        term = jnp.dot(chunk, weight, preferred_element_type=F32)
        total = term if total is None else total + term
    return total


def state_kernel(cols_ref, key_ref, left_ref, right_ref, out_ref):
    for head, value_ref in enumerate((left_ref, right_ref)):
        weight = cols_ref[0, :, 4 + head : 5 + head]
        keys = key_ref[:, head * DQK : (head + 1) * DQK]
        scaled = (keys.astype(F32) * weight).astype(BF)
        out_ref[0, head] = lax.dot_general(
            scaled, value_ref[...], (((0,), (0,)), ((), ())), preferred_element_type=F32
        ).astype(BF)


def states(cols, key, value):
    parts = [pl.BlockSpec((ROWS, WIDE), lambda s, n=n: (s, n)) for n in (0, 0, 1)]
    return pl.pallas_call(
        state_kernel,
        grid=(2,),
        in_specs=[pl.BlockSpec((1, ROWS, 8), lambda s: (s, 0, 0)), *parts],
        out_specs=pl.BlockSpec((1, 2, DQK, DV), lambda s: (s, 0, 0, 0)),
        out_shape=jax.ShapeDtypeStruct((2, 2, DQK, DV), BF),
        compiler_params=SMALL,
        cost_estimate=COST,
        name="states",
    )(cols, key, value, value)


def intra_kernel(cols_ref, rows_ref, query_ref, key_ref, left_ref, right_ref, out_ref):
    segment = cols_ref[0, :, 6:7]
    segment_row = rows_ref[0, 4:5, :]
    for head, value_ref in enumerate((left_ref, right_ref)):
        cumul = cols_ref[0, :, head : head + 1]
        cumul_row = rows_ref[0, head : head + 1, :]
        gate_row = rows_ref[0, 2 + head : 3 + head, :]
        features = slice(head * DQK, (head + 1) * DQK)
        for start, size in ((0, 256), (256, 384)):
            reach = start + size
            scores = lax.dot_general(
                query_ref[start:reach, features],
                key_ref[:reach, features],
                (((1,), (1,)), ((), ())),
                preferred_element_type=F32,
            ) * (DQK**-0.5)
            later = start + lax.broadcasted_iota(jnp.int32, (size, reach), 0)
            earlier = lax.broadcasted_iota(jnp.int32, (size, reach), 1)
            keep = (later >= earlier) & (segment[start:reach] == segment_row[:, :reach])
            diff = cumul[start:reach] - cumul_row[:, :reach] + gate_row[:, :reach]
            mixed = (scores * jnp.exp(jnp.where(keep, diff, -1e30))).astype(BF)
            out_ref[start:reach, head * DV : (head + 1) * DV] = jnp.dot(
                mixed, value_ref[:reach, :], preferred_element_type=F32
            )


def intra(cols, rows, query, key, value):
    parts = [pl.BlockSpec((ROWS, WIDE), lambda s, n=n: (s, n)) for n in (0, 0, 0, 1)]
    return pl.pallas_call(
        intra_kernel,
        grid=(2,),
        in_specs=[
            pl.BlockSpec((1, ROWS, 8), lambda s: (s, 0, 0)),
            pl.BlockSpec((1, 8, ROWS), lambda s: (s, 0, 0)),
            *parts,
        ],
        out_specs=pl.BlockSpec((ROWS, 2 * DV), lambda s: (s, 0)),
        out_shape=jax.ShapeDtypeStruct((2 * ROWS, 2 * DV), F32),
        compiler_params=SMALL,
        cost_estimate=COST,
        name="intra",
    )(cols, rows, query, key, value, value)


def readout_kernel(cols_ref, query_ref, intra_ref, carried_ref, out_ref):
    head = pl.program_id(0)
    reach = jnp.where(head == 0, cols_ref[0, :, 2:3], cols_ref[0, :, 3:4])
    between = jnp.dot(query_ref[...], carried_ref[0], preferred_element_type=F32) * reach
    readout = intra_ref[...] + between
    scale = lax.rsqrt(jnp.mean(readout * readout, axis=-1, keepdims=True) + 1e-05)
    out_ref[...] = (readout * scale).astype(BF)


def readout(slot, cols, qkv, inner, carried):
    return pl.pallas_call(
        readout_kernel,
        grid=(2,),
        in_specs=[
            pl.BlockSpec((1, ROWS, 8), lambda h: (slot, 0, 0)),
            pl.BlockSpec((ROWS, DQK), lambda h: (slot, h)),
            pl.BlockSpec((ROWS, DV), lambda h: (slot, h)),
            pl.BlockSpec((1, DQK, DV), lambda h: (h, 0, 0)),
        ],
        out_specs=pl.BlockSpec((ROWS, DV), lambda h: (0, h)),
        out_shape=jax.ShapeDtypeStruct((ROWS, 2 * DV), BF),
        compiler_params=SMALL,
        cost_estimate=COST,
        name="readout",
    )(cols, qkv, inner, carried)


def join(decay, earlier, later):
    return (decay.astype(F32)[:, None, None] * earlier.astype(F32) + later.astype(F32)).astype(BF)


def times(left, right):
    return (left.astype(F32) * right.astype(F32)).astype(BF)


def pack(state, decay):
    tail = jnp.broadcast_to(decay[:, None, None], (2, 8, DV))
    return jnp.concatenate([state, tail], axis=1)


def unpack(message):
    return message[:, :-8], message[:, -1, 0]


def in_order(mine, axis, send):
    place = lax.axis_index(axis)
    blocks = [mine] + [shift(send(by), axis, by) for by in (1, 2, 3)]
    stacked = jnp.stack(blocks)
    return [lax.dynamic_index_in_dim(stacked, (place - j) % 4, 0, False) for j in range(4)]


def carry_in(decay, state, beside):
    x, z = lax.axis_index("x"), lax.axis_index("z")
    quarters = state.reshape(2, 4, DQK // 4, DV)

    def piece(by):
        return pack(lax.dynamic_index_in_dim(quarters, (x + by) % 4, 1, False), decay)

    line = [unpack(block) for block in in_order(piece(0), "x", piece)]
    prior = jnp.zeros_like(line[0][0])
    reach = jnp.ones_like(decay)
    priors, reaches = [], []
    for block, fade in line:
        priors.append(prior)
        reaches.append(reach)
        prior = join(fade, prior, block)
        reach = times(fade, reach)
    whole, done = together(pack(prior, reach), beside[0]())
    before = jnp.zeros_like(prior)
    for j, message in enumerate(in_order(whole, "z", lambda by: whole)):
        block, fade = unpack(message)
        before = jnp.where(j < z, join(fade, before, block), before)
    backs = jnp.stack([join(reaches[j], before, priors[j]) for j in range(4)])
    backs, done = together(backs, beside[1](done))

    def back(by):
        return lax.dynamic_index_in_dim(backs, (x + by) % 4, 0, False)

    inner = beside[2](done)
    carried, inner = together(jnp.stack(in_order(back(0), "x", back), axis=1), inner)
    return carried.reshape(2, DQK, DV), done, inner


def gate_rows(w_gates, core, place):
    gates = w_gates.T.reshape(2, 2, 2, OWN).transpose(1, 0, 2, 3).reshape(2, 4, OWN)
    mate = swap(gates)
    gates = jnp.where(
        core == 0,
        jnp.concatenate([gates[0], mate[0]], axis=1),
        jnp.concatenate([mate[1], gates[1]], axis=1),
    )
    gates = jnp.pad(gates.reshape(1, 4 * PIECE), ((0, 0), (0, WIDE - 4 * PIECE)))
    row = lax.broadcasted_iota(jnp.int32, (EXTRA, WIDE), 0)
    return jnp.where(row == place, gates, jnp.zeros_like(gates))


def per_device(tokens, w_query, w_key, w_value, w_gates, forget_bias, doc_lengths):
    core = lax.axis_index("core")
    y, z, x = lax.axis_index("y"), lax.axis_index("z"), lax.axis_index("x")
    chip = z * 4 + x
    last, middle = jnp.where(core == 0, x, z), jnp.where(core == 0, z, x)
    core_scalar = core[None].astype(jnp.int32)
    restore_places = jnp.concatenate([places(last), core_scalar])
    q_places = jnp.concatenate([places(middle), core_scalar])

    own = (w_query, w_key, w_value)
    mate = tuple(swap(weight) for weight in own)
    held, columns, rest = prepare(core_scalar, own, mate, gate_rows(w_gates, core, middle * 4 + y))
    rest = lax.all_gather(rest, ("y", "z", "x"), axis=0, tiled=True)
    tokens = together(tokens[0], held)[0]
    mate_tokens = swap(tokens)

    (held,) = assemble(places(y), together(*around(held, "yy")), PIECE, False)
    held, columns = together(held, columns)
    columns = weave(q_places, together(*around(columns, "zx")), False)
    held, region = assemble(places(middle), together(*around(held, "zx")), 4 * PIECE, True)
    columns = weave(restore_places, together(*around(columns, "xz")), True)
    regions = jnp.stack(together(*around(region, "xz")))
    regions = jnp.stack([lax.dynamic_index_in_dim(regions, (j - last) % 4, 0, False) for j in range(4)])
    regions = regions[:, :, : 4 * PIECE].reshape(4, 4, 4, 4, PIECE)
    w_gates = jnp.where(
        core == 0, regions.transpose(3, 2, 1, 0, 4), regions.transpose(3, 2, 0, 1, 4)
    ).reshape(4, 4096)
    w_gates = jnp.pad(w_gates, ((0, EXTRA - 4), (0, 0)))
    gates, normed, *chunks = normalize(
        jnp.concatenate([restore_places, places(y)]), tokens, mate_tokens, w_gates
    )
    chunks, by_y = chunks[:4], chunks[4:]
    gates = gates[:4].T
    gates = gates.reshape(2, ROWS, 4)
    lengths = doc_lengths[0]
    starts = jnp.cumsum(lengths) - lengths
    shard = chip * 2 + jnp.stack([core, 1 - core])
    positions = shard[:, None] * ROWS + jnp.arange(ROWS, dtype=jnp.int32)[None, :]
    resets = jnp.any(positions[:, :, None] == starts[None, None, :], axis=-1)
    bias = lax.dynamic_slice_in_dim(forget_bias, core * 2, 2)
    in_gate = gates[:, :, :2]
    cumul = jnp.cumsum(jax.nn.log_sigmoid(gates[:, :, 2:] + bias), axis=1)
    segment = jnp.cumsum(resets.astype(jnp.int32), axis=1)
    last = cumul[:, -1]
    same = (segment == segment[:, -1:])[:, :, None]
    weight = jnp.exp(jnp.where(same, last[:, None, :] - cumul + in_gate, -1e30))
    decay = (jnp.exp(last) * (segment[:, -1:] == 0).astype(F32)).astype(BF)
    reach = jnp.exp(cumul) * (segment == 0).astype(F32)[:, :, None] * (DQK**-0.5)
    seg = segment.astype(F32)[:, :, None]
    cols = jnp.concatenate([cumul, reach, weight, seg, jnp.zeros_like(seg)], axis=2)
    rows = jnp.concatenate([cumul, in_gate, seg, jnp.zeros_like(seg), weight], axis=2)
    rows = rows.transpose(0, 2, 1)

    key = project(chunks[:1], [held])
    held, columns, rest, key, cols, rows, decay = together(
        held, columns, rest, key, cols, rows, decay
    )
    blocks = around(held, "xz")
    columns = around(columns, "yy")
    value = jnp.dot(normed, rest, preferred_element_type=F32).astype(BF)
    key = project(chunks[1:], blocks[1:], key).astype(BF)
    state = states(cols, key, value)
    first = lax.dynamic_index_in_dim(state, core, 0, False)
    second = lax.dynamic_index_in_dim(state, 1 - core, 0, False)
    fade_first = lax.dynamic_index_in_dim(decay, core, 0, False)
    fade_second = lax.dynamic_index_in_dim(decay, 1 - core, 0, False)
    chip_state = join(fade_second, first, second)
    carried, query, inner = carry_in(
        times(fade_first, fade_second),
        chip_state,
        (
            lambda: project(by_y[:2], columns[:2]),
            lambda total: project(by_y[2:], columns[2:], total).astype(BF),
            lambda query: intra(cols, rows, query, key, value),
        ),
    )
    carried_second = join(fade_first, carried, first)
    mine = jnp.where(core == 0, carried, carried_second)
    other = jnp.where(core == 0, carried_second, carried)
    outgoing = readout(1, cols, query, inner, other)
    incoming = swap(outgoing)
    kept = readout(0, cols, query, inner, mine)
    result = jnp.where(
        core == 0,
        jnp.concatenate([kept, incoming], axis=1),
        jnp.concatenate([incoming, kept], axis=1),
    )
    return result.reshape(1, ROWS, 2048)


def solution(mesh):
    split = Mesh(mesh.devices.reshape(4, 4, 4, 2), ("y", "z", "x", "core"))
    weight_spec = P(("y", "z", "x", "core"), None)
    in_specs = (
        P("y", ("z", "x", "core"), None),
        weight_spec,
        weight_spec,
        weight_spec,
        weight_spec,
        P(),
        P("y", None),
    )
    out_specs = P("y", ("z", "x", "core"), None)
    return jax.shard_map(
        per_device, mesh=split, in_specs=in_specs, out_specs=out_specs, check_vma=False
    )
```

profile of v0, /device:TPU:25, one launch (start us, length us, event | category | flops | bytes accessed | tf_op | source)
XLA Modules:
  0.0 195.9 jit_solution(3734859150250021180)
XLA Ops:
  17.4 2.0 %collective-permute-start.6 = (bf16[80,512]{1,0:T(8,128)(2,1)S(1)}, bf16[80,512]{1,0:T(8,128)(2,1)S(1)}, u32[]{:S(2)}, u32[]{:S(2)}) collective-permute-start(bf16[80,512]{1,0:T(8,128)(2,1)S(1)} %get-tuple-element.57.refs_0_), channel_id=1, source_target_pairs={{0,32},{1,33},{2,34},{3,35},{4,36},{5,37},{6,38},{7,39},{8,40},{9,... | collective-permute-start | bytes 245768 | tf_op jit(solution)/shard_map/ppermute | solution.py:41
  19.5 2.7 %collective-permute-done.4.refs_1_ = bf16[80,512]{1,0:T(8,128)(2,1)S(1)} collective-permute-done((bf16[80,512]{1,0:T(8,128)(2,1)S(1)}, bf16[80,512]{1,0:T(8,128)(2,1)S(1)}, u32[]{:S(2)}, u32[]{:S(2)}) %collective-permute-start.4) | collective-permute-done | bytes 81952 | tf_op jit(solution)/shard_map/ppermute | solution.py:41
  24.4 2.5 %collective-permute-start.7 = (bf16[272,512]{1,0:T(8,128)(2,1)S(1)}, bf16[272,512]{1,0:T(8,128)(2,1)S(1)}, u32[]{:S(2)}, u32[]{:S(2)}) collective-permute-start(bf16[272,512]{1,0:T(8,128)(2,1)S(1)} %assemble.2.refs_0_), channel_id=1, source_target_pairs={{0,24},{1,7},{2,26},{3,1},{4,28},{5,3},{6,30},{7,5},{8,0},{9,15},{... | collective-permute-start | bytes 835592 | tf_op jit(solution)/shard_map/ppermute | solution.py:41
  28.4 2.1 %collective-permute-start.10 = (bf16[64,512]{1,0:T(8,128)(2,1)S(1)}, bf16[64,512]{1,0:T(8,128)(2,1)S(1)}, u32[]{:S(2)}, u32[]{:S(2)}) collective-permute-start(bf16[64,512]{1,0:T(8,128)(2,1)S(1)} %get-tuple-element.69.refs_0_), channel_id=1, source_target_pairs={{0,24},{1,7},{2,26},{3,1},{4,28},{5,3},{6,30},{7,5},{8,0},{9,15},{... | collective-permute-start | bytes 196616 | tf_op jit(solution)/shard_map/ppermute | solution.py:41
  30.5 3.4 %collective-permute-done.7.refs_1_ = bf16[272,512]{1,0:T(8,128)(2,1)S(1)} collective-permute-done((bf16[272,512]{1,0:T(8,128)(2,1)S(1)}, bf16[272,512]{1,0:T(8,128)(2,1)S(1)}, u32[]{:S(2)}, u32[]{:S(2)}) %collective-permute-start.7) | collective-permute-done | bytes 278560 | tf_op jit(solution)/shard_map/ppermute | solution.py:41
  34.5 3.5 %collective-permute-start.12 = (bf16[64,512]{1,0:T(8,128)(2,1)S(1)}, bf16[64,512]{1,0:T(8,128)(2,1)S(1)}, u32[]{:S(2)}, u32[]{:S(2)}) collective-permute-start(bf16[64,512]{1,0:T(8,128)(2,1)S(1)} %get-tuple-element.69.refs_0_), channel_id=1, source_target_pairs={{0,8},{1,3},{2,10},{3,5},{4,12},{5,7},{6,14},{7,1},{8,16},{9,11},{... | collective-permute-start | bytes 196616 | tf_op jit(solution)/shard_map/ppermute | solution.py:41
  40.1 3.9 %collective-permute-start.17 = (bf16[16,512]{1,0:T(8,128)(2,1)S(1)}, bf16[16,512]{1,0:T(8,128)(2,1)S(1)}, u32[]{:S(2)}, u32[]{:S(2)}) collective-permute-start(bf16[16,512]{1,0:T(8,128)(2,1)S(1)} %get-tuple-element.80), channel_id=1, source_target_pairs={{0,6},{1,25},{2,0},{3,27},{4,2},{5,29},{6,4},{7,31},{8,14},{9,1},{... | collective-permute-start | bytes 49160 | tf_op jit(solution)/shard_map/ppermute | solution.py:41
  46.5 2.1 %collective-permute-start.13 = (bf16[256,512]{1,0:T(8,128)(2,1)S(1)}, bf16[256,512]{1,0:T(8,128)(2,1)S(1)}, u32[]{:S(2)}, u32[]{:S(2)}) collective-permute-start(bf16[256,512]{1,0:T(8,128)(2,1)S(1)} %bitcast.174), channel_id=1, source_target_pairs={{0,6},{1,25},{2,0},{3,27},{4,2},{5,29},{6,4},{7,31},{8,14},{9,1},{... | collective-permute-start | bytes 786440 | tf_op jit(solution)/shard_map/ppermute | solution.py:41
  48.6 1.7 collective-permute-start.14
  50.7 4.1 %collective-permute-done.13 = bf16[256,512]{1,0:T(8,128)(2,1)S(1)} collective-permute-done((bf16[256,512]{1,0:T(8,128)(2,1)S(1)}, bf16[256,512]{1,0:T(8,128)(2,1)S(1)}, u32[]{:S(2)}, u32[]{:S(2)}) %collective-permute-start.13) | collective-permute-done | bytes 262176 | tf_op jit(solution)/shard_map/ppermute | solution.py:41
  54.8 3.9 %collective-permute-done.14 = bf16[256,512]{1,0:T(8,128)(2,1)S(1)} collective-permute-done((bf16[256,512]{1,0:T(8,128)(2,1)S(1)}, bf16[256,512]{1,0:T(8,128)(2,1)S(1)}, u32[]{:S(2)}, u32[]{:S(2)}) %collective-permute-start.14) | collective-permute-done | bytes 262176 | tf_op jit(solution)/shard_map/ppermute | solution.py:41
  58.7 4.1 %collective-permute-done.15 = bf16[256,512]{1,0:T(8,128)(2,1)S(1)} collective-permute-done((bf16[256,512]{1,0:T(8,128)(2,1)S(1)}, bf16[256,512]{1,0:T(8,128)(2,1)S(1)}, u32[]{:S(2)}, u32[]{:S(2)}) %collective-permute-start.15) | collective-permute-done | bytes 262176 | tf_op jit(solution)/shard_map/ppermute | solution.py:41
  62.8 1.7 weave.3
  64.5 2.5 %copy-done = bf16[1,640,4096]{2,1,0:T(8,128)(2,1)S(1)} copy-done((bf16[1,640,4096]{2,1,0:T(8,128)(2,1)S(1)}, bf16[1,640,4096]{2,1,0:T(8,128)(2,1)}, u32[]{:S(2)}) %copy-start) | copy-done | bytes 5242904
  66.9 16.7 %normalize.1 = (f32[16,1280]{1,0:T(8,128)S(1)}, bf16[1280,4096]{1,0:T(8,128)(2,1)}, bf16[1280,1024]{1,0:T(8,128)(2,1)S(1)}, bf16[1280,1024]{1,0:T(8,128)(2,1)S(1...) custom-call(s32[9]{0:T(128)S(1)} %concatenate.69.places, ...), custom_call_target="tpu_custom_call" | custom-call | bytes 33554432 | tf_op jit(solution)/shard_map/normalize/pallas_call | solution.py:86
  83.7 1.5 copy-done.1
  85.2 1.5 copy-done.6
  86.7 1.5 copy-done.8
  88.2 1.5 copy-done.10
  89.7 1.5 copy-done.12
  91.2 1.5 copy-done.14
  92.7 1.5 copy-done.16
  96.5 4.3 %fusion.50 = f32[1280,512]{1,0:T(8,128)} fusion(bf16[1280,1024]{1,0:T(8,128)(2,1)S(1)} %get-tuple-element.84, bf16[1024,512]{1,0:T(8,128)(2,1)} %copy-done.17), kind=kOutput, calls=%fused_computation.155 | convolution fusion | flops 1342177280 | bytes 6291456 | tf_op jit(solution)/shard_map/dot_general | solution.py:251
  100.8 2.0 %collective-permute-start.31 = (bf16[1024,512]{1,0:T(8,128)(2,1)}, bf16[1024,512]{1,0:T(8,128)(2,1)}, u32[]{:S(2)}, u32[]{:S(2)}) collective-permute-start(bf16[1024,512]{1,0:T(8,128)(2,1)} %bitcast.26), channel_id=1, source_target_pairs={{0,32},{1,33},{2,34},{3,35},{4,36},{5,37},{6,38},{7,39},{8,40},{9,... | collective-permute-start | bytes 3145736 | tf_op jit(solution)/shard_map/ppermute | solution.py:41
  102.7 2.0 %collective-permute-start.21 = (bf16[1024,512]{1,0:T(8,128)(2,1)}, bf16[1024,512]{1,0:T(8,128)(2,1)}, u32[]{:S(2)}, u32[]{:S(2)}) collective-permute-start(bf16[1024,512]{1,0:T(8,128)(2,1)} %copy-done.17), channel_id=1, source_target_pairs={{0,4},{1,17},{2,6},{3,19},{4,0},{5,21},{6,2},{7,23},{8,12},{9,25},... | collective-permute-start | bytes 3145736 | tf_op jit(solution)/shard_map/ppermute | solution.py:41
  104.7 2.7 %collective-permute-start.20 = (bf16[1024,512]{1,0:T(8,128)(2,1)}, bf16[1024,512]{1,0:T(8,128)(2,1)}, u32[]{:S(2)}, u32[]{:S(2)}) collective-permute-start(bf16[1024,512]{1,0:T(8,128)(2,1)} %copy-done.17), channel_id=1, source_target_pairs={{0,6},{1,25},{2,0},{3,27},{4,2},{5,29},{6,4},{7,31},{8,14},{9,1},{... | collective-permute-start | bytes 3145736 | tf_op jit(solution)/shard_map/ppermute | solution.py:41
  107.4 15.9 %convolution_convert_fusion.left_ref.right_ref = bf16[1280,1024]{1,0:T(8,128)(2,1)S(1)} fusion(bf16[1280,4096]{1,0:T(8,128)(2,1)} %get-tuple-element.93, bf16[4096,1024]{1,0:T(8,128)(2,1)} %all-gather.2.cloned.1.call-done), kind=kOutput, calls=%fused_computation | convolution fusion | flops 10738728960 | bytes 21495808 | tf_op jit(solution)/shard_map/dot_general | solution.py:479
  123.6 1.3 collective-permute-start.30
  124.9 3.7 %fusion.51 = f32[1280,512]{1,0:T(8,128)S(1)} fusion(bf16[1280,1024]{1,0:T(8,128)(2,1)} %copy-done.16, bf16[1024,512]{1,0:T(8,128)(2,1)} %collective-permute-done.21), kind=kOutput, calls=%fused_computation.156 | convolution fusion | flops 1342177280 | bytes 6291456 | tf_op jit(solution)/shard_map/dot_general | solution.py:251
  129.7 2.9 %fusion.52 = f32[1280,512]{1,0:T(8,128)S(1)} fusion(bf16[1280,1024]{1,0:T(8,128)(2,1)S(1)} %copy-done.15, bf16[1024,512]{1,0:T(8,128)(2,1)} %collective-permute-done.22), kind=kOutput, calls=%fused_computation.157 | convolution fusion | flops 1342177280 | bytes 6291456 | tf_op jit(solution)/shard_map/dot_general | solution.py:251
  132.7 3.0 %fusion.4.key_ref = bf16[1280,512]{1,0:T(8,128)(2,1)S(1)} fusion(f32[1280,512]{1,0:T(8,128)S(1)} %fusion.52, f32[1280,512]{1,0:T(8,128)S(1)} %fusion.51, f32[1280,512]{1,0:T(8,128)S(1)} %copy-done.18, bf16[1280,1024]{1,0:T(8,128)(2,1)S(1)} %copy-done.2, bf16[1024,512]{1,0:T(8,128)(2,1)} %collective-permute-done.20), kind=kOutput, calls=%fused_computation.8 | convolution fusion | flops 1344798720 | bytes 12845056 | tf_op jit(solution)/shard_map/dot_general | solution.py:251
  135.7 2.2 %states.1 = bf16[2,2,256,512]{3,2,1,0:T(8,128)(2,1)S(1)} custom-call(f32[2,640,8]{2,1,0:T(8,128)S(1)} %copy.86.cols_ref, bf16[1280,512]{1,0:T(8,128)(2,1)S(1)} %fusion.4.key_ref, bf16[1280,1024]{1,0:T(8,128)(2,1)S(1)} %convolution_convert_fusion.left_ref.right_ref, bf16[1280,1024]{1,0:T(8,128)(2,1)S(1)} %convolution_convert_fusion.left_ref.right_ref), custom_call_target="tpu_custom_call" | custom-call | bytes 1024 | tf_op jit(solution)/shard_map/states/pallas_call | solution.py:268
  139.4 2.0 %collective-permute-start.24 = (bf16[2,72,512]{2,1,0:T(8,128)(2,1)S(1)}, bf16[2,72,512]{2,1,0:T(8,128)(2,1)S(1)}, u32[]{:S(2)}, u32[]{:S(2)}) collective-permute-start(bf16[2,72,512]{2,1,0:T(8,128)(2,1)S(1)} %get-tuple-element.156), channel_id=1, source_target_pairs={{0,4},{2,6},{4,0},{6,2},{1,5},{3,7},{5,1},{7,3},{8,12},{10,14},{12... | collective-permute-start | bytes 442376 | tf_op jit(solution)/shard_map/ppermute | solution.py:30
  142.0 2.9 %fusion.53 = f32[1280,512]{1,0:T(8,128)S(1)} fusion(bf16[1280,1024]{1,0:T(8,128)(2,1)S(1)} %copy-done.13, bf16[1024,512]{1,0:T(8,128)(2,1)} %collective-permute-done.26), kind=kOutput, calls=%fused_computation.158 | convolution fusion | flops 1342177280 | bytes 6291456 | tf_op jit(solution)/shard_map/dot_general | solution.py:251
  144.9 2.9 %convolution_add_fusion.1 = f32[1280,512]{1,0:T(8,128)S(1)} fusion(f32[1280,512]{1,0:T(8,128)S(1)} %fusion.53, bf16[1280,1024]{1,0:T(8,128)(2,1)S(1)} %copy-done.11, bf16[1024,512]{1,0:T(8,128)(2,1)} %bitcast.26), kind=kOutput, calls=%fused_computation.2 | convolution fusion | flops 1342832640 | bytes 8912896 | tf_op jit(solution)/shard_map/dot_general | solution.py:251
  147.8 2.8 %fusion.54 = f32[1280,512]{1,0:T(8,128)S(1)} fusion(bf16[1280,1024]{1,0:T(8,128)(2,1)S(1)} %copy-done.9, bf16[1024,512]{1,0:T(8,128)(2,1)} %collective-permute-done.31), kind=kOutput, calls=%fused_computation.159 | convolution fusion | flops 1342177280 | bytes 6291456 | tf_op jit(solution)/shard_map/dot_general | solution.py:251
  151.4 1.5 collective-permute-start.28
  152.9 1.6 collective-permute-start.29
  154.4 1.6 fusion.3.query_ref
  156.1 2.1 %collective-permute-done.27 = bf16[2,72,512]{2,1,0:T(8,128)(2,1)S(1)} collective-permute-done((bf16[2,72,512]{2,1,0:T(8,128)(2,1)S(1)}, bf16[2,72,512]{2,1,0:T(8,128)(2,1)S(1)}, u32[]{:S(2)}, u32[]{:S(2)}) %collective-permute-start.27) | collective-permute-done | bytes 147488 | tf_op jit(solution)/shard_map/ppermute | solution.py:30
  160.9 1.2 collective-permute-start.33
  162.1 1.6 collective-permute-start.34
  163.6 3.6 %intra.1.intra_ref = f32[1280,1024]{1,0:T(8,128)S(1)} custom-call(f32[2,640,8]{2,1,0:T(8,128)S(1)} %copy.86.cols_ref, f32[2,8,640]{2,1,0:T(8,128)S(1)} %bitcast.180, bf16[1280,512]{1,0:T(8,128)(2,1)S(1)} %fusion.3.query_ref, bf16[1280,512]{1,0:T(8,128)(2,1)S(1)} %fusion.4.key_ref, bf16[1280,1024]{1,0:T(8,128)(2,1)S(1)} %convolution_convert_fusion.left_ref.right_ref, ...), custom_call_target="tpu_custom_call" | custom-call | bytes 1024 | tf_op jit(solution)/shard_map/intra/pallas_call | solution.py:308
  167.9 1.4 readout.3
  169.3 15.0 %collective-permute-start.35 = (bf16[640,1024]{1,0:T(8,128)(2,1)S(1)}, bf16[640,1024]{1,0:T(8,128)(2,1)S(1)}, u32[]{:S(2)}, u32[]{:S(2)}) collective-permute-start(bf16[640,1024]{1,0:T(8,128)(2,1)S(1)} %readout.3), channel_id=1, source_target_pairs={{0,1},{1,0},{2,3},{3,2},{4,5},{5,4},{6,7},{7,6},{8,9},{9,8},{10,11... | collective-permute-start | bytes 3932168 | tf_op jit(solution)/shard_map/ppermute | solution.py:26
  184.3 1.4 readout.2
  185.7 1.3 collective-permute-done.35
  187.0 2.0 %maximum_select_fusion = bf16[1,640,2048]{2,1,0:T(8,128)(2,1)} fusion(bf16[1,640,1024]{2,1,0:T(8,128)(2,1)S(1)} %bitcast.184, bf16[1,640,1024]{2,1,0:T(8,128)(2,1)S(1)} %bitcast.171, pred[]{:T(512)S(6)} %eq.94), kind=kLoop, calls=%fused_computation.9 | loop fusion | flops 11796480 | bytes 5242881 | tf_op jit(solution)/shard_map/jit(_where)/select_n | solution.py:502
  (170 shorter events, 29.6 us)
Async XLA Ops:
  6.5 38.9 %copy-start.19 = (f32[4]{0:T(128)S(1)}, f32[4]{0:T(128)}, u32[]{:S(2)}) copy-start(f32[4]{0:T(128)} %param.12) | copy-start | bytes 52
  6.5 94.2 %all-gather.2.cloned.1.call-start = ((), (), s32[]{:S(2)}) async-start(), calls=%async_computation | async-start | bytes 8519680 | tf_op jit(solution)/shard_map/all_gather | solution.py:432
  7.2 1.5 collective-permute-start.3
  7.9 2.0 %collective-permute-start.2 = (bf16[32,2048]{1,0:T(8,128)(2,1)}, bf16[32,2048]{1,0:T(8,128)(2,1)S(1)}, u32[]{:S(2)}, u32[]{:S(2)}) collective-permute-start(bf16[32,2048]{1,0:T(8,128)(2,1)} %value.1), channel_id=1, source_target_pairs={{0,1},{1,0},{2,3},{3,2},{4,5},{5,4},{6,7},{7,6},{8,9},{9,8},{10,11... | collective-permute-start | bytes 393224 | tf_op jit(solution)/shard_map/ppermute | solution.py:26
  7.9 1.6 collective-permute-start
  8.4 1.5 collective-permute-start.1
  13.2 51.3 %collective-permute-start.16 = (bf16[640,4096]{1,0:T(8,128)(2,1)}, bf16[640,4096]{1,0:T(8,128)(2,1)}, u32[]{:S(2)}, u32[]{:S(2)}) collective-permute-start(bf16[640,4096]{1,0:T(8,128)(2,1)} %bitcast.172), channel_id=1, source_target_pairs={{0,1},{1,0},{2,3},{3,2},{4,5},{5,4},{6,7},{7,6},{8,9},{9,8},{10,11... | collective-permute-start | bytes 15728648 | tf_op jit(solution)/shard_map/ppermute | solution.py:26
  16.3 5.8 %collective-permute-start.4 = (bf16[80,512]{1,0:T(8,128)(2,1)S(1)}, bf16[80,512]{1,0:T(8,128)(2,1)S(1)}, u32[]{:S(2)}, u32[]{:S(2)}) collective-permute-start(bf16[80,512]{1,0:T(8,128)(2,1)S(1)} %get-tuple-element.57.refs_0_), channel_id=1, source_target_pairs={{0,96},{1,97},{2,98},{3,99},{4,100},{5,101},{6,102},{7,103},{8,104... | collective-permute-start | bytes 245768 | tf_op jit(solution)/shard_map/ppermute | solution.py:41
  16.8 5.3 %collective-permute-start.5 = (bf16[80,512]{1,0:T(8,128)(2,1)S(1)}, bf16[80,512]{1,0:T(8,128)(2,1)S(1)}, u32[]{:S(2)}, u32[]{:S(2)}) collective-permute-start(bf16[80,512]{1,0:T(8,128)(2,1)S(1)} %get-tuple-element.57.refs_0_), channel_id=1, source_target_pairs={{0,64},{1,65},{2,66},{3,67},{4,68},{5,69},{6,70},{7,71},{8,72},{9,... | collective-permute-start | bytes 245768 | tf_op jit(solution)/shard_map/ppermute | solution.py:41
  17.4 5.9 %collective-permute-start.6 = (bf16[80,512]{1,0:T(8,128)(2,1)S(1)}, bf16[80,512]{1,0:T(8,128)(2,1)S(1)}, u32[]{:S(2)}, u32[]{:S(2)}) collective-permute-start(bf16[80,512]{1,0:T(8,128)(2,1)S(1)} %get-tuple-element.57.refs_0_), channel_id=1, source_target_pairs={{0,32},{1,33},{2,34},{3,35},{4,36},{5,37},{6,38},{7,39},{8,40},{9,... | collective-permute-start | bytes 245768 | tf_op jit(solution)/shard_map/ppermute | solution.py:41
  24.4 9.5 %collective-permute-start.7 = (bf16[272,512]{1,0:T(8,128)(2,1)S(1)}, bf16[272,512]{1,0:T(8,128)(2,1)S(1)}, u32[]{:S(2)}, u32[]{:S(2)}) collective-permute-start(bf16[272,512]{1,0:T(8,128)(2,1)S(1)} %assemble.2.refs_0_), channel_id=1, source_target_pairs={{0,24},{1,7},{2,26},{3,1},{4,28},{5,3},{6,30},{7,5},{8,0},{9,15},{... | collective-permute-start | bytes 835592 | tf_op jit(solution)/shard_map/ppermute | solution.py:41
  27.1 7.3 %collective-permute-start.8 = (bf16[272,512]{1,0:T(8,128)(2,1)S(1)}, bf16[272,512]{1,0:T(8,128)(2,1)S(1)}, u32[]{:S(2)}, u32[]{:S(2)}) collective-permute-start(bf16[272,512]{1,0:T(8,128)(2,1)S(1)} %assemble.2.refs_0_), channel_id=1, source_target_pairs={{0,16},{1,5},{2,18},{3,7},{4,20},{5,1},{6,22},{7,3},{8,24},{9,13},... | collective-permute-start | bytes 835592 | tf_op jit(solution)/shard_map/ppermute | solution.py:41
  27.7 10.5 %collective-permute-start.9 = (bf16[272,512]{1,0:T(8,128)(2,1)S(1)}, bf16[272,512]{1,0:T(8,128)(2,1)S(1)}, u32[]{:S(2)}, u32[]{:S(2)}) collective-permute-start(bf16[272,512]{1,0:T(8,128)(2,1)S(1)} %assemble.2.refs_0_), channel_id=1, source_target_pairs={{0,8},{1,3},{2,10},{3,5},{4,12},{5,7},{6,14},{7,1},{8,16},{9,11},{... | collective-permute-start | bytes 835592 | tf_op jit(solution)/shard_map/ppermute | solution.py:41
  28.4 15.6 %collective-permute-start.10 = (bf16[64,512]{1,0:T(8,128)(2,1)S(1)}, bf16[64,512]{1,0:T(8,128)(2,1)S(1)}, u32[]{:S(2)}, u32[]{:S(2)}) collective-permute-start(bf16[64,512]{1,0:T(8,128)(2,1)S(1)} %get-tuple-element.69.refs_0_), channel_id=1, source_target_pairs={{0,24},{1,7},{2,26},{3,1},{4,28},{5,3},{6,30},{7,5},{8,0},{9,15},{... | collective-permute-start | bytes 196616 | tf_op jit(solution)/shard_map/ppermute | solution.py:41
  33.9 10.2 %collective-permute-start.11 = (bf16[64,512]{1,0:T(8,128)(2,1)S(1)}, bf16[64,512]{1,0:T(8,128)(2,1)S(1)}, u32[]{:S(2)}, u32[]{:S(2)}) collective-permute-start(bf16[64,512]{1,0:T(8,128)(2,1)S(1)} %get-tuple-element.69.refs_0_), channel_id=1, source_target_pairs={{0,16},{1,5},{2,18},{3,7},{4,20},{5,1},{6,22},{7,3},{8,24},{9,13},... | collective-permute-start | bytes 196616 | tf_op jit(solution)/shard_map/ppermute | solution.py:41
  34.5 11.1 %collective-permute-start.12 = (bf16[64,512]{1,0:T(8,128)(2,1)S(1)}, bf16[64,512]{1,0:T(8,128)(2,1)S(1)}, u32[]{:S(2)}, u32[]{:S(2)}) collective-permute-start(bf16[64,512]{1,0:T(8,128)(2,1)S(1)} %get-tuple-element.69.refs_0_), channel_id=1, source_target_pairs={{0,8},{1,3},{2,10},{3,5},{4,12},{5,7},{6,14},{7,1},{8,16},{9,11},{... | collective-permute-start | bytes 196616 | tf_op jit(solution)/shard_map/ppermute | solution.py:41
  40.1 8.5 %collective-permute-start.17 = (bf16[16,512]{1,0:T(8,128)(2,1)S(1)}, bf16[16,512]{1,0:T(8,128)(2,1)S(1)}, u32[]{:S(2)}, u32[]{:S(2)}) collective-permute-start(bf16[16,512]{1,0:T(8,128)(2,1)S(1)} %get-tuple-element.80), channel_id=1, source_target_pairs={{0,6},{1,25},{2,0},{3,27},{4,2},{5,29},{6,4},{7,31},{8,14},{9,1},{... | collective-permute-start | bytes 49160 | tf_op jit(solution)/shard_map/ppermute | solution.py:41
  44.0 6.3 %collective-permute-start.18 = (bf16[16,512]{1,0:T(8,128)(2,1)S(1)}, bf16[16,512]{1,0:T(8,128)(2,1)S(1)}, u32[]{:S(2)}, u32[]{:S(2)}) collective-permute-start(bf16[16,512]{1,0:T(8,128)(2,1)S(1)} %get-tuple-element.80), channel_id=1, source_target_pairs={{0,4},{1,17},{2,6},{3,19},{4,0},{5,21},{6,2},{7,23},{8,12},{9,25},... | collective-permute-start | bytes 49160 | tf_op jit(solution)/shard_map/ppermute | solution.py:41
  44.1 6.3 %collective-permute-start.19 = (bf16[16,512]{1,0:T(8,128)(2,1)S(1)}, bf16[16,512]{1,0:T(8,128)(2,1)S(1)}, u32[]{:S(2)}, u32[]{:S(2)}) collective-permute-start(bf16[16,512]{1,0:T(8,128)(2,1)S(1)} %get-tuple-element.80), channel_id=1, source_target_pairs={{0,2},{1,9},{2,4},{3,11},{4,6},{5,13},{6,0},{7,15},{8,10},{9,17},{... | collective-permute-start | bytes 49160 | tf_op jit(solution)/shard_map/ppermute | solution.py:41
  46.5 8.3 %collective-permute-start.13 = (bf16[256,512]{1,0:T(8,128)(2,1)S(1)}, bf16[256,512]{1,0:T(8,128)(2,1)S(1)}, u32[]{:S(2)}, u32[]{:S(2)}) collective-permute-start(bf16[256,512]{1,0:T(8,128)(2,1)S(1)} %bitcast.174), channel_id=1, source_target_pairs={{0,6},{1,25},{2,0},{3,27},{4,2},{5,29},{6,4},{7,31},{8,14},{9,1},{... | collective-permute-start | bytes 786440 | tf_op jit(solution)/shard_map/ppermute | solution.py:41
  48.6 10.1 %collective-permute-start.14 = (bf16[256,512]{1,0:T(8,128)(2,1)S(1)}, bf16[256,512]{1,0:T(8,128)(2,1)S(1)}, u32[]{:S(2)}, u32[]{:S(2)}) collective-permute-start(bf16[256,512]{1,0:T(8,128)(2,1)S(1)} %bitcast.175), channel_id=1, source_target_pairs={{0,4},{1,17},{2,6},{3,19},{4,0},{5,21},{6,2},{7,23},{8,12},{9,25},... | collective-permute-start | bytes 786440 | tf_op jit(solution)/shard_map/ppermute | solution.py:41
  50.3 12.5 %collective-permute-start.15 = (bf16[256,512]{1,0:T(8,128)(2,1)S(1)}, bf16[256,512]{1,0:T(8,128)(2,1)S(1)}, u32[]{:S(2)}, u32[]{:S(2)}) collective-permute-start(bf16[256,512]{1,0:T(8,128)(2,1)S(1)} %bitcast.176), channel_id=1, source_target_pairs={{0,2},{1,9},{2,4},{3,11},{4,6},{5,13},{6,0},{7,15},{8,10},{9,17},{... | collective-permute-start | bytes 786440 | tf_op jit(solution)/shard_map/ppermute | solution.py:41
  64.4 2.5 %copy-start = (bf16[1,640,4096]{2,1,0:T(8,128)(2,1)S(1)}, bf16[1,640,4096]{2,1,0:T(8,128)(2,1)}, u32[]{:S(2)}) copy-start(bf16[1,640,4096]{2,1,0:T(8,128)(2,1)} %param.7) | copy-start | bytes 15728644
  89.7 1.5 copy-start.12
  92.7 1.5 copy-start.16
  100.8 47.1 %collective-permute-start.31 = (bf16[1024,512]{1,0:T(8,128)(2,1)}, bf16[1024,512]{1,0:T(8,128)(2,1)}, u32[]{:S(2)}, u32[]{:S(2)}) collective-permute-start(bf16[1024,512]{1,0:T(8,128)(2,1)} %bitcast.26), channel_id=1, source_target_pairs={{0,32},{1,33},{2,34},{3,35},{4,36},{5,37},{6,38},{7,39},{8,40},{9,... | collective-permute-start | bytes 3145736 | tf_op jit(solution)/shard_map/ppermute | solution.py:41
  102.7 38.7 %collective-permute-start.26 = (bf16[1024,512]{1,0:T(8,128)(2,1)}, bf16[1024,512]{1,0:T(8,128)(2,1)}, u32[]{:S(2)}, u32[]{:S(2)}) collective-permute-start(bf16[1024,512]{1,0:T(8,128)(2,1)} %bitcast.26), channel_id=1, source_target_pairs={{0,96},{1,97},{2,98},{3,99},{4,100},{5,101},{6,102},{7,103},{8,104... | collective-permute-start | bytes 3145736 | tf_op jit(solution)/shard_map/ppermute | solution.py:41
  102.7 20.9 %collective-permute-start.21 = (bf16[1024,512]{1,0:T(8,128)(2,1)}, bf16[1024,512]{1,0:T(8,128)(2,1)}, u32[]{:S(2)}, u32[]{:S(2)}) collective-permute-start(bf16[1024,512]{1,0:T(8,128)(2,1)} %copy-done.17), channel_id=1, source_target_pairs={{0,4},{1,17},{2,6},{3,19},{4,0},{5,21},{6,2},{7,23},{8,12},{9,25},... | collective-permute-start | bytes 3145736 | tf_op jit(solution)/shard_map/ppermute | solution.py:41
  104.7 25.0 %collective-permute-start.22 = (bf16[1024,512]{1,0:T(8,128)(2,1)}, bf16[1024,512]{1,0:T(8,128)(2,1)}, u32[]{:S(2)}, u32[]{:S(2)}) collective-permute-start(bf16[1024,512]{1,0:T(8,128)(2,1)} %copy-done.17), channel_id=1, source_target_pairs={{0,2},{1,9},{2,4},{3,11},{4,6},{5,13},{6,0},{7,15},{8,10},{9,17},{... | collective-permute-start | bytes 3145736 | tf_op jit(solution)/shard_map/ppermute | solution.py:41
  104.7 27.9 %collective-permute-start.20 = (bf16[1024,512]{1,0:T(8,128)(2,1)}, bf16[1024,512]{1,0:T(8,128)(2,1)}, u32[]{:S(2)}, u32[]{:S(2)}) collective-permute-start(bf16[1024,512]{1,0:T(8,128)(2,1)} %copy-done.17), channel_id=1, source_target_pairs={{0,6},{1,25},{2,0},{3,27},{4,2},{5,29},{6,4},{7,31},{8,14},{9,1},{... | collective-permute-start | bytes 3145736 | tf_op jit(solution)/shard_map/ppermute | solution.py:41
  123.6 30.8 %collective-permute-start.30 = (bf16[1024,512]{1,0:T(8,128)(2,1)}, bf16[1024,512]{1,0:T(8,128)(2,1)S(1)}, u32[]{:S(2)}, u32[]{:S(2)}) collective-permute-start(bf16[1024,512]{1,0:T(8,128)(2,1)} %bitcast.26), channel_id=1, source_target_pairs={{0,64},{1,65},{2,66},{3,67},{4,68},{5,69},{6,70},{7,71},{8,72},{9,... | collective-permute-start | bytes 3145736 | tf_op jit(solution)/shard_map/ppermute | solution.py:41
  124.9 4.9 %copy-start.15 = (bf16[1280,1024]{1,0:T(8,128)(2,1)S(1)}, bf16[1280,1024]{1,0:T(8,128)(2,1)}, u32[]{:S(2)}) copy-start(bf16[1280,1024]{1,0:T(8,128)(2,1)} %copy-done.14) | copy-start | bytes 7864324
  129.7 2.9 %copy-start.2 = (bf16[1280,1024]{1,0:T(8,128)(2,1)S(1)}, bf16[1280,1024]{1,0:T(8,128)(2,1)}, u32[]{:S(2)}) copy-start(bf16[1280,1024]{1,0:T(8,128)(2,1)} %copy-done.1) | copy-start | bytes 7864324
  129.7 2.9 %copy-start.18 = (f32[1280,512]{1,0:T(8,128)S(1)}, f32[1280,512]{1,0:T(8,128)}, u32[]{:S(2)}) copy-start(f32[1280,512]{1,0:T(8,128)} %fusion.50) | copy-start | bytes 7864324
  138.0 3.9 %copy-start.13 = (bf16[1280,1024]{1,0:T(8,128)(2,1)S(1)}, bf16[1280,1024]{1,0:T(8,128)(2,1)}, u32[]{:S(2)}) copy-start(bf16[1280,1024]{1,0:T(8,128)(2,1)} %copy-done.12) | copy-start | bytes 7864324
  138.5 12.1 %collective-permute-start.23 = (bf16[2,72,512]{2,1,0:T(8,128)(2,1)S(1)}, bf16[2,72,512]{2,1,0:T(8,128)(2,1)S(1)}, u32[]{:S(2)}, u32[]{:S(2)}) collective-permute-start(bf16[2,72,512]{2,1,0:T(8,128)(2,1)S(1)} %get-tuple-element.155), channel_id=1, source_target_pairs={{0,2},{2,4},{4,6},{6,0},{1,3},{3,5},{5,7},{7,1},{8,10},{10,12},{12... | collective-permute-start | bytes 442376 | tf_op jit(solution)/shard_map/ppermute | solution.py:30
  139.4 11.3 %collective-permute-start.24 = (bf16[2,72,512]{2,1,0:T(8,128)(2,1)S(1)}, bf16[2,72,512]{2,1,0:T(8,128)(2,1)S(1)}, u32[]{:S(2)}, u32[]{:S(2)}) collective-permute-start(bf16[2,72,512]{2,1,0:T(8,128)(2,1)S(1)} %get-tuple-element.156), channel_id=1, source_target_pairs={{0,4},{2,6},{4,0},{6,2},{1,5},{3,7},{5,1},{7,3},{8,12},{10,14},{12... | collective-permute-start | bytes 442376 | tf_op jit(solution)/shard_map/ppermute | solution.py:30
  141.4 9.2 %collective-permute-start.25 = (bf16[2,72,512]{2,1,0:T(8,128)(2,1)S(1)}, bf16[2,72,512]{2,1,0:T(8,128)(2,1)S(1)}, u32[]{:S(2)}, u32[]{:S(2)}) collective-permute-start(bf16[2,72,512]{2,1,0:T(8,128)(2,1)S(1)} %get-tuple-element.157), channel_id=1, source_target_pairs={{0,6},{2,0},{4,2},{6,4},{1,7},{3,1},{5,3},{7,5},{8,14},{10,8},{12,... | collective-permute-start | bytes 442376 | tf_op jit(solution)/shard_map/ppermute | solution.py:30
  142.0 2.9 %copy-start.11 = (bf16[1280,1024]{1,0:T(8,128)(2,1)S(1)}, bf16[1280,1024]{1,0:T(8,128)(2,1)}, u32[]{:S(2)}) copy-start(bf16[1280,1024]{1,0:T(8,128)(2,1)} %copy-done.10) | copy-start | bytes 7864324
  144.9 2.9 %copy-start.9 = (bf16[1280,1024]{1,0:T(8,128)(2,1)S(1)}, bf16[1280,1024]{1,0:T(8,128)(2,1)}, u32[]{:S(2)}) copy-start(bf16[1280,1024]{1,0:T(8,128)(2,1)} %copy-done.8) | copy-start | bytes 7864324
  150.6 3.8 %copy-start.7 = (bf16[1280,1024]{1,0:T(8,128)(2,1)S(1)}, bf16[1280,1024]{1,0:T(8,128)(2,1)}, u32[]{:S(2)}) copy-start(bf16[1280,1024]{1,0:T(8,128)(2,1)} %copy-done.6) | copy-start | bytes 7864324
  151.3 6.9 %collective-permute-start.27 = (bf16[2,72,512]{2,1,0:T(8,128)(2,1)S(1)}, bf16[2,72,512]{2,1,0:T(8,128)(2,1)S(1)}, u32[]{:S(2)}, u32[]{:S(2)}) collective-permute-start(bf16[2,72,512]{2,1,0:T(8,128)(2,1)S(1)} %pad_maximum_fusion.9), channel_id=1, source_target_pairs={{0,8},{8,16},{16,24},{24,0},{1,9},{9,17},{17,25},{25,1},{2,10},{10... | collective-permute-start | bytes 442376 | tf_op jit(solution)/shard_map/ppermute | solution.py:30
  151.4 6.8 %collective-permute-start.28 = (bf16[2,72,512]{2,1,0:T(8,128)(2,1)S(1)}, bf16[2,72,512]{2,1,0:T(8,128)(2,1)S(1)}, u32[]{:S(2)}, u32[]{:S(2)}) collective-permute-start(bf16[2,72,512]{2,1,0:T(8,128)(2,1)S(1)} %pad_maximum_fusion.9), channel_id=1, source_target_pairs={{0,16},{8,24},{16,0},{24,8},{1,17},{9,25},{17,1},{25,9},{2,18},{10... | collective-permute-start | bytes 442376 | tf_op jit(solution)/shard_map/ppermute | solution.py:30
  152.9 5.9 %collective-permute-start.29 = (bf16[2,72,512]{2,1,0:T(8,128)(2,1)S(1)}, bf16[2,72,512]{2,1,0:T(8,128)(2,1)S(1)}, u32[]{:S(2)}, u32[]{:S(2)}) collective-permute-start(bf16[2,72,512]{2,1,0:T(8,128)(2,1)S(1)} %pad_maximum_fusion.9), channel_id=1, source_target_pairs={{0,24},{8,0},{16,8},{24,16},{1,25},{9,1},{17,9},{25,17},{2,26},{10... | collective-permute-start | bytes 442376 | tf_op jit(solution)/shard_map/ppermute | solution.py:30
  159.9 7.4 %collective-permute-start.32 = (bf16[2,64,512]{2,1,0:T(8,128)(2,1)S(1)}, bf16[2,64,512]{2,1,0:T(8,128)(2,1)S(1)}, u32[]{:S(2)}, u32[]{:S(2)}) collective-permute-start(bf16[2,64,512]{2,1,0:T(8,128)(2,1)S(1)} %get-tuple-element.139), channel_id=1, source_target_pairs={{0,2},{2,4},{4,6},{6,0},{1,3},{3,5},{5,7},{7,1},{8,10},{10,12},{12... | collective-permute-start | bytes 393224 | tf_op jit(solution)/shard_map/ppermute | solution.py:30
  160.9 6.4 %collective-permute-start.33 = (bf16[2,64,512]{2,1,0:T(8,128)(2,1)S(1)}, bf16[2,64,512]{2,1,0:T(8,128)(2,1)S(1)}, u32[]{:S(2)}, u32[]{:S(2)}) collective-permute-start(bf16[2,64,512]{2,1,0:T(8,128)(2,1)S(1)} %get-tuple-element.138), channel_id=1, source_target_pairs={{0,4},{2,6},{4,0},{6,2},{1,5},{3,7},{5,1},{7,3},{8,12},{10,14},{12... | collective-permute-start | bytes 393224 | tf_op jit(solution)/shard_map/ppermute | solution.py:30
  162.1 5.2 %collective-permute-start.34 = (bf16[2,64,512]{2,1,0:T(8,128)(2,1)S(1)}, bf16[2,64,512]{2,1,0:T(8,128)(2,1)S(1)}, u32[]{:S(2)}, u32[]{:S(2)}) collective-permute-start(bf16[2,64,512]{2,1,0:T(8,128)(2,1)S(1)} %get-tuple-element.137), channel_id=1, source_target_pairs={{0,6},{2,0},{4,2},{6,4},{1,7},{3,1},{5,3},{7,5},{8,14},{10,8},{12,... | collective-permute-start | bytes 393224 | tf_op jit(solution)/shard_map/ppermute | solution.py:30
  169.3 17.7 %collective-permute-start.35 = (bf16[640,1024]{1,0:T(8,128)(2,1)S(1)}, bf16[640,1024]{1,0:T(8,128)(2,1)S(1)}, u32[]{:S(2)}, u32[]{:S(2)}) collective-permute-start(bf16[640,1024]{1,0:T(8,128)(2,1)S(1)} %readout.3), channel_id=1, source_target_pairs={{0,1},{1,0},{2,3},{3,2},{4,5},{5,4},{6,7},{7,6},{8,9},{9,8},{10,11... | collective-permute-start | bytes 3932168 | tf_op jit(solution)/shard_map/ppermute | solution.py:26
  (9 other events, 11.0 us)
Sparse Core Ops, SparseCore 0:
  13.3 86.3 all-gather.1
where the time goes:
time: 197 us; the launch traced here: 196 us
  starting transfers between devices  55.6 us (28%)
  matrix products  40 us (20%)
  Pallas kernels  30.6 us (16%)
  waiting for transfers between devices  26.3 us (13%)
  local copies, waits for them, and re-layouts  20.2 us (10%)
  between operations  14.3 us (7%)
  other arithmetic  8.88 us (5%)
    ppermute x21, starting transfers between devices, hop(): return lax.ppermute(value, names, pairs)  28.8 us
    dot_general x8, matrix products, project(): term = jnp.dot(chunk, weight, preferred_element_type=F32)  24 us
    ppermute x21, waiting for transfers between devices, hop(): return lax.ppermute(value, names, pairs)  21.2 us
    pallas_call x1, Pallas kernels, normalize(): pl.pallas_call(normalize_kernel, grid_spec=pltpu.PrefetchScalarGridSpec(n...  16.7 us
    unnamed x40, local copies, waits for them, and re-layouts  16.6 us
    ppermute x6, starting transfers between devices, swap(): return lax.ppermute(value, 'core', [(0, 1), (1, 0)])  16.5 us
    dot_general x1, matrix products, per_device(): value = jnp.dot(normed, rest, preferred_element_type=F32).astype(BF)  15.9 us
    ppermute x9, starting transfers between devices, shift(): return lax.ppermute(value, axis, [(i, (i + by) % 4) for i in range(4)])  10.4 us
  transfers between devices with their start and end apart: 37, of which 15 were waited for; matrix products, arithmetic and copies ran while one was open for 25% of the time, Pallas kernels for 15%

commit v1 on v0

--- a/solution.py
+++ b/solution.py
@@ -19,6 +19,7 @@
 F32 = jnp.float32
 COST = pl.CostEstimate(flops=0, bytes_accessed=1 << 10, transcendentals=0)
 SMALL = pltpu.CompilerParams(vmem_limit_bytes=20 * 1024 * 1024)
+LARGE = pltpu.CompilerParams(vmem_limit_bytes=60 * 1024 * 1024)
 PARAMS = pltpu.CompilerParams(vmem_limit_bytes=20 * 1024 * 1024)
 
 
@@ -103,7 +104,7 @@
             jax.ShapeDtypeStruct((2 * ROWS, 4096), BF),
         ]
         + [jax.ShapeDtypeStruct((2 * ROWS, 1024), BF)] * 8,
-        compiler_params=PARAMS,
+        compiler_params=LARGE,
         cost_estimate=pl.CostEstimate(flops=0, bytes_accessed=32 << 20, transcendentals=0),
         name="normalize",
     )(places, own, mate, w_gates)
@@ -471,8 +472,9 @@
     rows = rows.transpose(0, 2, 1)
 
     key = project(chunks[:1], [held])
-    held, columns, rest, key, cols, rows, decay = together(
-        held, columns, rest, key, cols, rows, decay
+    query = project(by_y[:1], [columns])
+    held, columns, rest, key, query, cols, rows, decay = together(
+        held, columns, rest, key, query, cols, rows, decay
     )
     blocks = around(held, "xz")
     columns = around(columns, "yy")
@@ -488,8 +490,8 @@
         times(fade_first, fade_second),
         chip_state,
         (
-            lambda: project(by_y[:2], columns[:2]),
-            lambda total: project(by_y[2:], columns[2:], total).astype(BF),
+            lambda: (project(by_y[1:2], columns[1:2], query), by_y[2], by_y[3]),
+            lambda done: project(done[1:], columns[2:], done[0]).astype(BF),
             lambda query: intra(cols, rows, query, key, value),
         ),
     )

time: 197 us -> 194 us (0.985)
  local copies, waits for them, and re-layouts: 20.2 us -> 8.24 us
  Pallas kernels: 30.6 us -> 35.4 us
  matrix products: 40 us -> 42.2 us
    unnamed x40 -> x24, local copies, waits for them, and re-layouts: 16.6 us -> 2.62 us
    pallas_call x1, Pallas kernels: 16.7 us -> 20.4 us  [normalize(): pl.pallas_call(normalize_kernel, grid_spec=pltpu.PrefetchScalarGridSpec(n...]
    dot_general x8, matrix products: 24 us -> 26.2 us  [project(): term = jnp.dot(chunk, weight, preferred_element_type=F32)]
  transfers between devices with their start and end apart: 37 -> 37, of which waited for: 15 -> 17; matrix products, arithmetic and copies ran while one was open for 25% -> 27% of each run, Pallas kernels for 15% -> 17%
where the time goes in v1:
time: 194 us; the launch traced here: 193 us
  starting transfers between devices  56.9 us (29%)
  matrix products  42.2 us (22%)
  Pallas kernels  35.4 us (18%)
  waiting for transfers between devices  27.1 us (14%)
  between operations  14.3 us (7%)
  other arithmetic  8.86 us (5%)
  local copies, waits for them, and re-layouts  8.24 us (4%)
    ppermute x21, starting transfers between devices, hop(): return lax.ppermute(value, names, pairs)  29.7 us
    dot_general x8, matrix products, project(): term = jnp.dot(chunk, weight, preferred_element_type=F32)  26.2 us
    ppermute x21, waiting for transfers between devices, hop(): return lax.ppermute(value, names, pairs)  21.5 us
    pallas_call x1, Pallas kernels, normalize(): pl.pallas_call(normalize_kernel, grid_spec=pltpu.PrefetchScalarGridSpec(n...  20.4 us
    dot_general x1, matrix products, per_device(): value = jnp.dot(normed, rest, preferred_element_type=F32).astype(BF)  15.9 us
    ppermute x6, starting transfers between devices, swap(): return lax.ppermute(value, 'core', [(0, 1), (1, 0)])  15.6 us
    ppermute x9, starting transfers between devices, shift(): return lax.ppermute(value, axis, [(i, (i + by) % 4) for i in range(4)])  11.6 us
  transfers between devices with their start and end apart: 37, of which 17 were waited for; matrix products, arithmetic and copies ran while one was open for 27% of the time, Pallas kernels for 17%

profile of v1, /device:TPU:25, one launch (start us, length us, event | category | flops | bytes accessed | tf_op | source)
XLA Modules:
  0.0 193.0 jit_solution(6889972024229572462)
XLA Ops:
  17.4 2.0 %collective-permute-start.6 = (bf16[80,512]{1,0:T(8,128)(2,1)S(1)}, bf16[80,512]{1,0:T(8,128)(2,1)S(1)}, u32[]{:S(2)}, u32[]{:S(2)}) collective-permute-start(bf16[80,512]{1,0:T(8,128)(2,1)S(1)} %get-tuple-element.60.refs_0_), channel_id=1, source_target_pairs={{0,32},{1,33},{2,34},{3,35},{4,36},{5,37},{6,38},{7,39},{8,40},{9,... | collective-permute-start | bytes 245768 | tf_op jit(solution)/shard_map/ppermute | solution.py:42
  19.5 2.7 %collective-permute-done.4.refs_1_ = bf16[80,512]{1,0:T(8,128)(2,1)S(1)} collective-permute-done((bf16[80,512]{1,0:T(8,128)(2,1)S(1)}, bf16[80,512]{1,0:T(8,128)(2,1)S(1)}, u32[]{:S(2)}, u32[]{:S(2)}) %collective-permute-start.4) | collective-permute-done | bytes 81952 | tf_op jit(solution)/shard_map/ppermute | solution.py:42
  22.2 1.1 collective-permute-done.6.refs_3_
  23.3 1.1 assemble.2.refs_0_
  24.4 2.5 %collective-permute-start.7 = (bf16[272,512]{1,0:T(8,128)(2,1)S(1)}, bf16[272,512]{1,0:T(8,128)(2,1)S(1)}, u32[]{:S(2)}, u32[]{:S(2)}) collective-permute-start(bf16[272,512]{1,0:T(8,128)(2,1)S(1)} %assemble.2.refs_0_), channel_id=1, source_target_pairs={{0,24},{1,7},{2,26},{3,1},{4,28},{5,3},{6,30},{7,5},{8,0},{9,15},{... | collective-permute-start | bytes 835592 | tf_op jit(solution)/shard_map/ppermute | solution.py:42
  28.4 2.1 %collective-permute-start.10 = (bf16[64,512]{1,0:T(8,128)(2,1)S(1)}, bf16[64,512]{1,0:T(8,128)(2,1)S(1)}, u32[]{:S(2)}, u32[]{:S(2)}) collective-permute-start(bf16[64,512]{1,0:T(8,128)(2,1)S(1)} %get-tuple-element.72.refs_0_), channel_id=1, source_target_pairs={{0,24},{1,7},{2,26},{3,1},{4,28},{5,3},{6,30},{7,5},{8,0},{9,15},{... | collective-permute-start | bytes 196616 | tf_op jit(solution)/shard_map/ppermute | solution.py:42
  30.5 3.4 %collective-permute-done.7.refs_1_ = bf16[272,512]{1,0:T(8,128)(2,1)S(1)} collective-permute-done((bf16[272,512]{1,0:T(8,128)(2,1)S(1)}, bf16[272,512]{1,0:T(8,128)(2,1)S(1)}, u32[]{:S(2)}, u32[]{:S(2)}) %collective-permute-start.7) | collective-permute-done | bytes 278560 | tf_op jit(solution)/shard_map/ppermute | solution.py:42
  34.5 3.5 %collective-permute-start.12 = (bf16[64,512]{1,0:T(8,128)(2,1)S(1)}, bf16[64,512]{1,0:T(8,128)(2,1)S(1)}, u32[]{:S(2)}, u32[]{:S(2)}) collective-permute-start(bf16[64,512]{1,0:T(8,128)(2,1)S(1)} %get-tuple-element.72.refs_0_), channel_id=1, source_target_pairs={{0,8},{1,3},{2,10},{3,5},{4,12},{5,7},{6,14},{7,1},{8,16},{9,11},{... | collective-permute-start | bytes 196616 | tf_op jit(solution)/shard_map/ppermute | solution.py:42
  38.2 1.9 assemble.3
  40.1 4.0 %collective-permute-start.17 = (bf16[16,512]{1,0:T(8,128)(2,1)S(1)}, bf16[16,512]{1,0:T(8,128)(2,1)S(1)}, u32[]{:S(2)}, u32[]{:S(2)}) collective-permute-start(bf16[16,512]{1,0:T(8,128)(2,1)S(1)} %get-tuple-element.83), channel_id=1, source_target_pairs={{0,6},{1,25},{2,0},{3,27},{4,2},{5,29},{6,4},{7,31},{8,14},{9,1},{... | collective-permute-start | bytes 49160 | tf_op jit(solution)/shard_map/ppermute | solution.py:42
  46.1 1.0 weave.2
  47.1 2.1 %collective-permute-start.13 = (bf16[256,512]{1,0:T(8,128)(2,1)S(1)}, bf16[256,512]{1,0:T(8,128)(2,1)S(1)}, u32[]{:S(2)}, u32[]{:S(2)}) collective-permute-start(bf16[256,512]{1,0:T(8,128)(2,1)S(1)} %bitcast.172), channel_id=1, source_target_pairs={{0,6},{1,25},{2,0},{3,27},{4,2},{5,29},{6,4},{7,31},{8,14},{9,1},{... | collective-permute-start | bytes 786440 | tf_op jit(solution)/shard_map/ppermute | solution.py:42
  49.2 1.7 collective-permute-start.14
  51.9 3.4 %collective-permute-done.13 = bf16[256,512]{1,0:T(8,128)(2,1)S(1)} collective-permute-done((bf16[256,512]{1,0:T(8,128)(2,1)S(1)}, bf16[256,512]{1,0:T(8,128)(2,1)S(1)}, u32[]{:S(2)}, u32[]{:S(2)}) %collective-permute-start.13) | collective-permute-done | bytes 262176 | tf_op jit(solution)/shard_map/ppermute | solution.py:42
  55.4 3.8 %collective-permute-done.14 = bf16[256,512]{1,0:T(8,128)(2,1)S(1)} collective-permute-done((bf16[256,512]{1,0:T(8,128)(2,1)S(1)}, bf16[256,512]{1,0:T(8,128)(2,1)S(1)}, u32[]{:S(2)}, u32[]{:S(2)}) %collective-permute-start.14) | collective-permute-done | bytes 262176 | tf_op jit(solution)/shard_map/ppermute | solution.py:42
  59.2 4.1 %collective-permute-done.15 = bf16[256,512]{1,0:T(8,128)(2,1)S(1)} collective-permute-done((bf16[256,512]{1,0:T(8,128)(2,1)S(1)}, bf16[256,512]{1,0:T(8,128)(2,1)S(1)}, u32[]{:S(2)}, u32[]{:S(2)}) %collective-permute-start.15) | collective-permute-done | bytes 262176 | tf_op jit(solution)/shard_map/ppermute | solution.py:42
  63.3 1.8 weave.3
  65.2 20.4 %normalize.1 = (f32[16,1280]{1,0:T(8,128)}, bf16[1280,4096]{1,0:T(8,128)(2,1)}, bf16[1280,1024]{1,0:T(8,128)(2,1)}, bf16[1280,1024]{1,0:T(8,128)(2,1)}, bf16[128...) custom-call(s32[9]{0:T(128)} %concatenate.69.places, ...), custom_call_target="tpu_custom_call" | custom-call | bytes 33554432 | tf_op jit(solution)/shard_map/normalize/pallas_call | solution.py:87
  86.5 1.2 reduce-window.21
  88.7 5.2 %fusion.49 = f32[1280,512]{1,0:T(8,128)} fusion(bf16[1280,1024]{1,0:T(8,128)(2,1)} %get-tuple-element.88, bf16[1024,512]{1,0:T(8,128)(2,1)} %bitcast.26), kind=kOutput, calls=%fused_computation.154 | convolution fusion | flops 1342177280 | bytes 6291456 | tf_op jit(solution)/shard_map/dot_general | solution.py:252
  93.9 4.2 %fusion.48 = f32[1280,512]{1,0:T(8,128)} fusion(bf16[1280,1024]{1,0:T(8,128)(2,1)S(1)} %copy-done.9, bf16[1024,512]{1,0:T(8,128)(2,1)} %get-tuple-element.94), kind=kOutput, calls=%fused_computation.153 | convolution fusion | flops 1342177280 | bytes 6291456 | tf_op jit(solution)/shard_map/dot_general | solution.py:252
  98.2 1.6 all-gather.2.cloned.1.call-done
  99.7 2.6 %collective-permute-start.21 = (bf16[1024,512]{1,0:T(8,128)(2,1)}, bf16[1024,512]{1,0:T(8,128)(2,1)}, u32[]{:S(2)}, u32[]{:S(2)}) collective-permute-start(bf16[1024,512]{1,0:T(8,128)(2,1)} %get-tuple-element.94), channel_id=1, source_target_pairs={{0,4},{1,17},{2,6},{3,19},{4,0},{5,21},{6,2},{7,23},{8,12},{9,25},... | collective-permute-start | bytes 3145736 | tf_op jit(solution)/shard_map/ppermute | solution.py:42
  102.7 2.3 %collective-permute-start.20 = (bf16[1024,512]{1,0:T(8,128)(2,1)}, bf16[1024,512]{1,0:T(8,128)(2,1)}, u32[]{:S(2)}, u32[]{:S(2)}) collective-permute-start(bf16[1024,512]{1,0:T(8,128)(2,1)} %get-tuple-element.94), channel_id=1, source_target_pairs={{0,6},{1,25},{2,0},{3,27},{4,2},{5,29},{6,4},{7,31},{8,14},{9,1},{... | collective-permute-start | bytes 3145736 | tf_op jit(solution)/shard_map/ppermute | solution.py:42
  106.4 15.9 %convolution_convert_fusion.left_ref.right_ref = bf16[1280,1024]{1,0:T(8,128)(2,1)S(1)} fusion(bf16[1280,4096]{1,0:T(8,128)(2,1)} %get-tuple-element.97, bf16[4096,1024]{1,0:T(8,128)(2,1)} %all-gather.2.cloned.1.call-done), kind=kOutput, calls=%fused_computation | convolution fusion | flops 10738728960 | bytes 21495808 | tf_op jit(solution)/shard_map/dot_general | solution.py:481
  122.6 2.1 %collective-permute-start.31 = (bf16[1024,512]{1,0:T(8,128)(2,1)}, bf16[1024,512]{1,0:T(8,128)(2,1)S(1)}, u32[]{:S(2)}, u32[]{:S(2)}) collective-permute-start(bf16[1024,512]{1,0:T(8,128)(2,1)} %bitcast.26), channel_id=1, source_target_pairs={{0,32},{1,33},{2,34},{3,35},{4,36},{5,37},{6,38},{7,39},{8,40},{9,... | collective-permute-start | bytes 3145736 | tf_op jit(solution)/shard_map/ppermute | solution.py:42
  124.7 3.7 %fusion.50 = f32[1280,512]{1,0:T(8,128)S(1)} fusion(bf16[1280,1024]{1,0:T(8,128)(2,1)} %get-tuple-element.95, bf16[1024,512]{1,0:T(8,128)(2,1)} %collective-permute-done.21), kind=kOutput, calls=%fused_computation.155 | convolution fusion | flops 1342177280 | bytes 6291456 | tf_op jit(solution)/shard_map/dot_general | solution.py:252
  128.4 2.9 %fusion.51 = f32[1280,512]{1,0:T(8,128)S(1)} fusion(bf16[1280,1024]{1,0:T(8,128)(2,1)S(1)} %copy-done.8, bf16[1024,512]{1,0:T(8,128)(2,1)} %collective-permute-done.22), kind=kOutput, calls=%fused_computation.156 | convolution fusion | flops 1342177280 | bytes 6291456 | tf_op jit(solution)/shard_map/dot_general | solution.py:252
  131.3 3.0 %fusion.2.key_ref = bf16[1280,512]{1,0:T(8,128)(2,1)S(1)} fusion(f32[1280,512]{1,0:T(8,128)S(1)} %fusion.51, f32[1280,512]{1,0:T(8,128)S(1)} %fusion.50, f32[1280,512]{1,0:T(8,128)S(1)} %copy-done.4, bf16[1280,1024]{1,0:T(8,128)(2,1)S(1)} %copy-done.3, bf16[1024,512]{1,0:T(8,128)(2,1)} %collective-permute-done.20), kind=kOutput, calls=%fused_computation.5 | convolution fusion | flops 1344798720 | bytes 12845056 | tf_op jit(solution)/shard_map/dot_general | solution.py:252
  134.3 2.2 %states.1 = bf16[2,2,256,512]{3,2,1,0:T(8,128)(2,1)S(1)} custom-call(f32[2,640,8]{2,1,0:T(8,128)S(1)} %copy.86.cols_ref, bf16[1280,512]{1,0:T(8,128)(2,1)S(1)} %fusion.2.key_ref, bf16[1280,1024]{1,0:T(8,128)(2,1)S(1)} %convolution_convert_fusion.left_ref.right_ref, bf16[1280,1024]{1,0:T(8,128)(2,1)S(1)} %convolution_convert_fusion.left_ref.right_ref), custom_call_target="tpu_custom_call" | custom-call | bytes 1024 | tf_op jit(solution)/shard_map/states/pallas_call | solution.py:269
  137.2 2.2 %collective-permute-start.24 = (bf16[2,72,512]{2,1,0:T(8,128)(2,1)S(1)}, bf16[2,72,512]{2,1,0:T(8,128)(2,1)S(1)}, u32[]{:S(2)}, u32[]{:S(2)}) collective-permute-start(bf16[2,72,512]{2,1,0:T(8,128)(2,1)S(1)} %get-tuple-element.162), channel_id=1, source_target_pairs={{0,4},{2,6},{4,0},{6,2},{1,5},{3,7},{5,1},{7,3},{8,12},{10,14},{12... | collective-permute-start | bytes 442376 | tf_op jit(solution)/shard_map/ppermute | solution.py:31
  139.4 1.2 collective-permute-start.25
  140.7 2.8 %convolution_add_fusion = f32[1280,512]{1,0:T(8,128)S(1)} fusion(f32[1280,512]{1,0:T(8,128)S(1)} %copy-done.11, bf16[1280,1024]{1,0:T(8,128)(2,1)S(1)} %copy-done.7, bf16[1024,512]{1,0:T(8,128)(2,1)} %collective-permute-done.26), kind=kOutput, calls=%fused_computation.1 | convolution fusion | flops 1342832640 | bytes 8912896 | tf_op jit(solution)/shard_map/dot_general | solution.py:252
  143.7 1.3 collective-permute-done.24
  145.8 1.1 collective-permute-start.28
  146.9 1.7 collective-permute-start.29
  148.6 1.2 collective-permute-done.30
  149.8 2.8 %fusion.52 = f32[1280,512]{1,0:T(8,128)S(1)} fusion(bf16[1280,1024]{1,0:T(8,128)(2,1)S(1)} %copy-done.6, bf16[1024,512]{1,0:T(8,128)(2,1)} %collective-permute-done.30), kind=kOutput, calls=%fused_computation.157 | convolution fusion | flops 1342177280 | bytes 6291456 | tf_op jit(solution)/shard_map/dot_general | solution.py:252
  152.6 1.0 collective-permute-done.31
  153.6 1.6 add_convert_fusion.query_ref
  156.4 2.1 %collective-permute-start.32 = (bf16[2,64,512]{2,1,0:T(8,128)(2,1)S(1)}, bf16[2,64,512]{2,1,0:T(8,128)(2,1)S(1)}, u32[]{:S(2)}, u32[]{:S(2)}) collective-permute-start(bf16[2,64,512]{2,1,0:T(8,128)(2,1)S(1)} %get-tuple-element.145), channel_id=1, source_target_pairs={{0,2},{2,4},{4,6},{6,0},{1,3},{3,5},{5,7},{7,1},{8,10},{10,12},{12... | collective-permute-start | bytes 393224 | tf_op jit(solution)/shard_map/ppermute | solution.py:31
  158.5 2.4 %collective-permute-start.33 = (bf16[2,64,512]{2,1,0:T(8,128)(2,1)S(1)}, bf16[2,64,512]{2,1,0:T(8,128)(2,1)S(1)}, u32[]{:S(2)}, u32[]{:S(2)}) collective-permute-start(bf16[2,64,512]{2,1,0:T(8,128)(2,1)S(1)} %get-tuple-element.144), channel_id=1, source_target_pairs={{0,4},{2,6},{4,0},{6,2},{1,5},{3,7},{5,1},{7,3},{8,12},{10,14},{12... | collective-permute-start | bytes 393224 | tf_op jit(solution)/shard_map/ppermute | solution.py:31
  161.6 3.7 %intra.1.intra_ref = f32[1280,1024]{1,0:T(8,128)S(1)} custom-call(f32[2,640,8]{2,1,0:T(8,128)S(1)} %copy.86.cols_ref, f32[2,8,640]{2,1,0:T(8,128)S(1)} %bitcast.178, bf16[1280,512]{1,0:T(8,128)(2,1)S(1)} %add_convert_fusion.query_ref, bf16[1280,512]{1,0:T(8,128)(2,1)S(1)} %fusion.2.key_ref, ...), custom_call_target="tpu_custom_call" | custom-call | bytes 1024 | tf_op jit(solution)/shard_map/intra/pallas_call | solution.py:309
  165.8 1.4 readout.3
  167.2 14.2 %collective-permute-start.35 = (bf16[640,1024]{1,0:T(8,128)(2,1)S(1)}, bf16[640,1024]{1,0:T(8,128)(2,1)S(1)}, u32[]{:S(2)}, u32[]{:S(2)}) collective-permute-start(bf16[640,1024]{1,0:T(8,128)(2,1)S(1)} %readout.3), channel_id=1, source_target_pairs={{0,1},{1,0},{2,3},{3,2},{4,5},{5,4},{6,7},{7,6},{8,9},{9,8},{10,11... | collective-permute-start | bytes 3932168 | tf_op jit(solution)/shard_map/ppermute | solution.py:27
  181.4 1.4 readout.2
  182.8 1.3 collective-permute-done.35
  184.1 2.0 %maximum_select_fusion = bf16[1,640,2048]{2,1,0:T(8,128)(2,1)} fusion(bf16[1,640,1024]{2,1,0:T(8,128)(2,1)S(1)} %bitcast.184, bf16[1,640,1024]{2,1,0:T(8,128)(2,1)S(1)} %bitcast.171, pred[]{:T(512)S(6)} %eq.94), kind=kLoop, calls=%fused_computation.6 | loop fusion | flops 11796480 | bytes 5242881 | tf_op jit(solution)/shard_map/jit(_where)/select_n | solution.py:504
  (154 shorter events, 23.9 us)
Async XLA Ops:
  6.5 39.5 %copy-start.10 = (f32[4]{0:T(128)S(1)}, f32[4]{0:T(128)}, u32[]{:S(2)}) copy-start(f32[4]{0:T(128)} %param.12) | copy-start | bytes 52
  6.5 93.2 %all-gather.2.cloned.1.call-start = ((), (), s32[]{:S(2)}) async-start(), calls=%async_computation | async-start | bytes 8519680 | tf_op jit(solution)/shard_map/all_gather | solution.py:433
  7.2 1.5 collective-permute-start.3
  7.9 2.0 %collective-permute-start.2 = (bf16[32,2048]{1,0:T(8,128)(2,1)}, bf16[32,2048]{1,0:T(8,128)(2,1)S(1)}, u32[]{:S(2)}, u32[]{:S(2)}) collective-permute-start(bf16[32,2048]{1,0:T(8,128)(2,1)} %value.1), channel_id=1, source_target_pairs={{0,1},{1,0},{2,3},{3,2},{4,5},{5,4},{6,7},{7,6},{8,9},{9,8},{10,11... | collective-permute-start | bytes 393224 | tf_op jit(solution)/shard_map/ppermute | solution.py:27
  7.9 1.6 collective-permute-start
  8.4 1.5 collective-permute-start.1
  9.9 0.9 copy-start
  10.8 0.8 copy-start.1
  13.2 52.0 %collective-permute-start.16 = (bf16[640,4096]{1,0:T(8,128)(2,1)}, bf16[640,4096]{1,0:T(8,128)(2,1)}, u32[]{:S(2)}, u32[]{:S(2)}) collective-permute-start(bf16[640,4096]{1,0:T(8,128)(2,1)} %bitcast.180), channel_id=1, source_target_pairs={{0,1},{1,0},{2,3},{3,2},{4,5},{5,4},{6,7},{7,6},{8,9},{9,8},{10,11... | collective-permute-start | bytes 15728648 | tf_op jit(solution)/shard_map/ppermute | solution.py:27
  16.3 5.8 %collective-permute-start.4 = (bf16[80,512]{1,0:T(8,128)(2,1)S(1)}, bf16[80,512]{1,0:T(8,128)(2,1)S(1)}, u32[]{:S(2)}, u32[]{:S(2)}) collective-permute-start(bf16[80,512]{1,0:T(8,128)(2,1)S(1)} %get-tuple-element.60.refs_0_), channel_id=1, source_target_pairs={{0,96},{1,97},{2,98},{3,99},{4,100},{5,101},{6,102},{7,103},{8,104... | collective-permute-start | bytes 245768 | tf_op jit(solution)/shard_map/ppermute | solution.py:42
  16.8 5.3 %collective-permute-start.5 = (bf16[80,512]{1,0:T(8,128)(2,1)S(1)}, bf16[80,512]{1,0:T(8,128)(2,1)S(1)}, u32[]{:S(2)}, u32[]{:S(2)}) collective-permute-start(bf16[80,512]{1,0:T(8,128)(2,1)S(1)} %get-tuple-element.60.refs_0_), channel_id=1, source_target_pairs={{0,64},{1,65},{2,66},{3,67},{4,68},{5,69},{6,70},{7,71},{8,72},{9,... | collective-permute-start | bytes 245768 | tf_op jit(solution)/shard_map/ppermute | solution.py:42
  17.4 5.9 %collective-permute-start.6 = (bf16[80,512]{1,0:T(8,128)(2,1)S(1)}, bf16[80,512]{1,0:T(8,128)(2,1)S(1)}, u32[]{:S(2)}, u32[]{:S(2)}) collective-permute-start(bf16[80,512]{1,0:T(8,128)(2,1)S(1)} %get-tuple-element.60.refs_0_), channel_id=1, source_target_pairs={{0,32},{1,33},{2,34},{3,35},{4,36},{5,37},{6,38},{7,39},{8,40},{9,... | collective-permute-start | bytes 245768 | tf_op jit(solution)/shard_map/ppermute | solution.py:42
  24.4 9.5 %collective-permute-start.7 = (bf16[272,512]{1,0:T(8,128)(2,1)S(1)}, bf16[272,512]{1,0:T(8,128)(2,1)S(1)}, u32[]{:S(2)}, u32[]{:S(2)}) collective-permute-start(bf16[272,512]{1,0:T(8,128)(2,1)S(1)} %assemble.2.refs_0_), channel_id=1, source_target_pairs={{0,24},{1,7},{2,26},{3,1},{4,28},{5,3},{6,30},{7,5},{8,0},{9,15},{... | collective-permute-start | bytes 835592 | tf_op jit(solution)/shard_map/ppermute | solution.py:42
  27.1 7.3 %collective-permute-start.8 = (bf16[272,512]{1,0:T(8,128)(2,1)S(1)}, bf16[272,512]{1,0:T(8,128)(2,1)S(1)}, u32[]{:S(2)}, u32[]{:S(2)}) collective-permute-start(bf16[272,512]{1,0:T(8,128)(2,1)S(1)} %assemble.2.refs_0_), channel_id=1, source_target_pairs={{0,16},{1,5},{2,18},{3,7},{4,20},{5,1},{6,22},{7,3},{8,24},{9,13},... | collective-permute-start | bytes 835592 | tf_op jit(solution)/shard_map/ppermute | solution.py:42
  27.8 10.5 %collective-permute-start.9 = (bf16[272,512]{1,0:T(8,128)(2,1)S(1)}, bf16[272,512]{1,0:T(8,128)(2,1)S(1)}, u32[]{:S(2)}, u32[]{:S(2)}) collective-permute-start(bf16[272,512]{1,0:T(8,128)(2,1)S(1)} %assemble.2.refs_0_), channel_id=1, source_target_pairs={{0,8},{1,3},{2,10},{3,5},{4,12},{5,7},{6,14},{7,1},{8,16},{9,11},{... | collective-permute-start | bytes 835592 | tf_op jit(solution)/shard_map/ppermute | solution.py:42
  28.4 15.6 %collective-permute-start.10 = (bf16[64,512]{1,0:T(8,128)(2,1)S(1)}, bf16[64,512]{1,0:T(8,128)(2,1)S(1)}, u32[]{:S(2)}, u32[]{:S(2)}) collective-permute-start(bf16[64,512]{1,0:T(8,128)(2,1)S(1)} %get-tuple-element.72.refs_0_), channel_id=1, source_target_pairs={{0,24},{1,7},{2,26},{3,1},{4,28},{5,3},{6,30},{7,5},{8,0},{9,15},{... | collective-permute-start | bytes 196616 | tf_op jit(solution)/shard_map/ppermute | solution.py:42
  33.9 10.2 %collective-permute-start.11 = (bf16[64,512]{1,0:T(8,128)(2,1)S(1)}, bf16[64,512]{1,0:T(8,128)(2,1)S(1)}, u32[]{:S(2)}, u32[]{:S(2)}) collective-permute-start(bf16[64,512]{1,0:T(8,128)(2,1)S(1)} %get-tuple-element.72.refs_0_), channel_id=1, source_target_pairs={{0,16},{1,5},{2,18},{3,7},{4,20},{5,1},{6,22},{7,3},{8,24},{9,13},... | collective-permute-start | bytes 196616 | tf_op jit(solution)/shard_map/ppermute | solution.py:42
  34.5 11.6 %collective-permute-start.12 = (bf16[64,512]{1,0:T(8,128)(2,1)S(1)}, bf16[64,512]{1,0:T(8,128)(2,1)S(1)}, u32[]{:S(2)}, u32[]{:S(2)}) collective-permute-start(bf16[64,512]{1,0:T(8,128)(2,1)S(1)} %get-tuple-element.72.refs_0_), channel_id=1, source_target_pairs={{0,8},{1,3},{2,10},{3,5},{4,12},{5,7},{6,14},{7,1},{8,16},{9,11},{... | collective-permute-start | bytes 196616 | tf_op jit(solution)/shard_map/ppermute | solution.py:42
  40.1 9.1 %collective-permute-start.17 = (bf16[16,512]{1,0:T(8,128)(2,1)S(1)}, bf16[16,512]{1,0:T(8,128)(2,1)S(1)}, u32[]{:S(2)}, u32[]{:S(2)}) collective-permute-start(bf16[16,512]{1,0:T(8,128)(2,1)S(1)} %get-tuple-element.83), channel_id=1, source_target_pairs={{0,6},{1,25},{2,0},{3,27},{4,2},{5,29},{6,4},{7,31},{8,14},{9,1},{... | collective-permute-start | bytes 49160 | tf_op jit(solution)/shard_map/ppermute | solution.py:42
  44.1 6.8 %collective-permute-start.18 = (bf16[16,512]{1,0:T(8,128)(2,1)S(1)}, bf16[16,512]{1,0:T(8,128)(2,1)S(1)}, u32[]{:S(2)}, u32[]{:S(2)}) collective-permute-start(bf16[16,512]{1,0:T(8,128)(2,1)S(1)} %get-tuple-element.83), channel_id=1, source_target_pairs={{0,4},{1,17},{2,6},{3,19},{4,0},{5,21},{6,2},{7,23},{8,12},{9,25},... | collective-permute-start | bytes 49160 | tf_op jit(solution)/shard_map/ppermute | solution.py:42
  44.1 6.8 %collective-permute-start.19 = (bf16[16,512]{1,0:T(8,128)(2,1)S(1)}, bf16[16,512]{1,0:T(8,128)(2,1)S(1)}, u32[]{:S(2)}, u32[]{:S(2)}) collective-permute-start(bf16[16,512]{1,0:T(8,128)(2,1)S(1)} %get-tuple-element.83), channel_id=1, source_target_pairs={{0,2},{1,9},{2,4},{3,11},{4,6},{5,13},{6,0},{7,15},{8,10},{9,17},{... | collective-permute-start | bytes 49160 | tf_op jit(solution)/shard_map/ppermute | solution.py:42
  47.1 8.3 %collective-permute-start.13 = (bf16[256,512]{1,0:T(8,128)(2,1)S(1)}, bf16[256,512]{1,0:T(8,128)(2,1)S(1)}, u32[]{:S(2)}, u32[]{:S(2)}) collective-permute-start(bf16[256,512]{1,0:T(8,128)(2,1)S(1)} %bitcast.172), channel_id=1, source_target_pairs={{0,6},{1,25},{2,0},{3,27},{4,2},{5,29},{6,4},{7,31},{8,14},{9,1},{... | collective-permute-start | bytes 786440 | tf_op jit(solution)/shard_map/ppermute | solution.py:42
  49.2 10.0 %collective-permute-start.14 = (bf16[256,512]{1,0:T(8,128)(2,1)S(1)}, bf16[256,512]{1,0:T(8,128)(2,1)S(1)}, u32[]{:S(2)}, u32[]{:S(2)}) collective-permute-start(bf16[256,512]{1,0:T(8,128)(2,1)S(1)} %bitcast.173), channel_id=1, source_target_pairs={{0,4},{1,17},{2,6},{3,19},{4,0},{5,21},{6,2},{7,23},{8,12},{9,25},... | collective-permute-start | bytes 786440 | tf_op jit(solution)/shard_map/ppermute | solution.py:42
  50.9 12.5 %collective-permute-start.15 = (bf16[256,512]{1,0:T(8,128)(2,1)S(1)}, bf16[256,512]{1,0:T(8,128)(2,1)S(1)}, u32[]{:S(2)}, u32[]{:S(2)}) collective-permute-start(bf16[256,512]{1,0:T(8,128)(2,1)S(1)} %bitcast.174), channel_id=1, source_target_pairs={{0,2},{1,9},{2,4},{3,11},{4,6},{5,13},{6,0},{7,15},{8,10},{9,17},{... | collective-permute-start | bytes 786440 | tf_op jit(solution)/shard_map/ppermute | solution.py:42
  88.7 5.3 %copy-start.9 = (bf16[1280,1024]{1,0:T(8,128)(2,1)S(1)}, bf16[1280,1024]{1,0:T(8,128)(2,1)}, u32[]{:S(2)}) copy-start(bf16[1280,1024]{1,0:T(8,128)(2,1)} %get-tuple-element.87) | copy-start | bytes 7864324
  99.7 22.8 %collective-permute-start.21 = (bf16[1024,512]{1,0:T(8,128)(2,1)}, bf16[1024,512]{1,0:T(8,128)(2,1)}, u32[]{:S(2)}, u32[]{:S(2)}) collective-permute-start(bf16[1024,512]{1,0:T(8,128)(2,1)} %get-tuple-element.94), channel_id=1, source_target_pairs={{0,4},{1,17},{2,6},{3,19},{4,0},{5,21},{6,2},{7,23},{8,12},{9,25},... | collective-permute-start | bytes 3145736 | tf_op jit(solution)/shard_map/ppermute | solution.py:42
  102.3 26.1 %collective-permute-start.22 = (bf16[1024,512]{1,0:T(8,128)(2,1)}, bf16[1024,512]{1,0:T(8,128)(2,1)}, u32[]{:S(2)}, u32[]{:S(2)}) collective-permute-start(bf16[1024,512]{1,0:T(8,128)(2,1)} %get-tuple-element.94), channel_id=1, source_target_pairs={{0,2},{1,9},{2,4},{3,11},{4,6},{5,13},{6,0},{7,15},{8,10},{9,17},{... | collective-permute-start | bytes 3145736 | tf_op jit(solution)/shard_map/ppermute | solution.py:42
  102.7 28.6 %collective-permute-start.20 = (bf16[1024,512]{1,0:T(8,128)(2,1)}, bf16[1024,512]{1,0:T(8,128)(2,1)}, u32[]{:S(2)}, u32[]{:S(2)}) collective-permute-start(bf16[1024,512]{1,0:T(8,128)(2,1)} %get-tuple-element.94), channel_id=1, source_target_pairs={{0,6},{1,25},{2,0},{3,27},{4,2},{5,29},{6,4},{7,31},{8,14},{9,1},{... | collective-permute-start | bytes 3145736 | tf_op jit(solution)/shard_map/ppermute | solution.py:42
  105.0 34.5 %collective-permute-start.26 = (bf16[1024,512]{1,0:T(8,128)(2,1)}, bf16[1024,512]{1,0:T(8,128)(2,1)}, u32[]{:S(2)}, u32[]{:S(2)}) collective-permute-start(bf16[1024,512]{1,0:T(8,128)(2,1)} %bitcast.26), channel_id=1, source_target_pairs={{0,96},{1,97},{2,98},{3,99},{4,100},{5,101},{6,102},{7,103},{8,104... | collective-permute-start | bytes 3145736 | tf_op jit(solution)/shard_map/ppermute | solution.py:42
  105.5 44.3 %collective-permute-start.30 = (bf16[1024,512]{1,0:T(8,128)(2,1)}, bf16[1024,512]{1,0:T(8,128)(2,1)}, u32[]{:S(2)}, u32[]{:S(2)}) collective-permute-start(bf16[1024,512]{1,0:T(8,128)(2,1)} %bitcast.26), channel_id=1, source_target_pairs={{0,64},{1,65},{2,66},{3,67},{4,68},{5,69},{6,70},{7,71},{8,72},{9,... | collective-permute-start | bytes 3145736 | tf_op jit(solution)/shard_map/ppermute | solution.py:42
  122.6 31.0 %collective-permute-start.31 = (bf16[1024,512]{1,0:T(8,128)(2,1)}, bf16[1024,512]{1,0:T(8,128)(2,1)S(1)}, u32[]{:S(2)}, u32[]{:S(2)}) collective-permute-start(bf16[1024,512]{1,0:T(8,128)(2,1)} %bitcast.26), channel_id=1, source_target_pairs={{0,32},{1,33},{2,34},{3,35},{4,36},{5,37},{6,38},{7,39},{8,40},{9,... | collective-permute-start | bytes 3145736 | tf_op jit(solution)/shard_map/ppermute | solution.py:42
  124.7 3.7 %copy-start.8 = (bf16[1280,1024]{1,0:T(8,128)(2,1)S(1)}, bf16[1280,1024]{1,0:T(8,128)(2,1)}, u32[]{:S(2)}) copy-start(bf16[1280,1024]{1,0:T(8,128)(2,1)} %get-tuple-element.96) | copy-start | bytes 7864324
  128.4 2.9 %copy-start.3 = (bf16[1280,1024]{1,0:T(8,128)(2,1)S(1)}, bf16[1280,1024]{1,0:T(8,128)(2,1)}, u32[]{:S(2)}) copy-start(bf16[1280,1024]{1,0:T(8,128)(2,1)} %get-tuple-element.93) | copy-start | bytes 7864324
  128.4 2.9 %copy-start.4 = (f32[1280,512]{1,0:T(8,128)S(1)}, f32[1280,512]{1,0:T(8,128)}, u32[]{:S(2)}) copy-start(f32[1280,512]{1,0:T(8,128)} %fusion.48) | copy-start | bytes 7864324
  136.5 4.1 %copy-start.11 = (f32[1280,512]{1,0:T(8,128)S(1)}, f32[1280,512]{1,0:T(8,128)}, u32[]{:S(2)}) copy-start(f32[1280,512]{1,0:T(8,128)} %fusion.49) | copy-start | bytes 7864324
  136.7 3.9 %copy-start.7 = (bf16[1280,1024]{1,0:T(8,128)(2,1)S(1)}, bf16[1280,1024]{1,0:T(8,128)(2,1)}, u32[]{:S(2)}) copy-start(bf16[1280,1024]{1,0:T(8,128)(2,1)} %get-tuple-element.100) | copy-start | bytes 7864324
  137.1 6.6 %collective-permute-start.23 = (bf16[2,72,512]{2,1,0:T(8,128)(2,1)S(1)}, bf16[2,72,512]{2,1,0:T(8,128)(2,1)S(1)}, u32[]{:S(2)}, u32[]{:S(2)}) collective-permute-start(bf16[2,72,512]{2,1,0:T(8,128)(2,1)S(1)} %get-tuple-element.161), channel_id=1, source_target_pairs={{0,2},{2,4},{4,6},{6,0},{1,3},{3,5},{5,7},{7,1},{8,10},{10,12},{12... | collective-permute-start | bytes 442376 | tf_op jit(solution)/shard_map/ppermute | solution.py:31
  137.2 7.8 %collective-permute-start.24 = (bf16[2,72,512]{2,1,0:T(8,128)(2,1)S(1)}, bf16[2,72,512]{2,1,0:T(8,128)(2,1)S(1)}, u32[]{:S(2)}, u32[]{:S(2)}) collective-permute-start(bf16[2,72,512]{2,1,0:T(8,128)(2,1)S(1)} %get-tuple-element.162), channel_id=1, source_target_pairs={{0,4},{2,6},{4,0},{6,2},{1,5},{3,7},{5,1},{7,3},{8,12},{10,14},{12... | collective-permute-start | bytes 442376 | tf_op jit(solution)/shard_map/ppermute | solution.py:31
  139.4 5.6 %collective-permute-start.25 = (bf16[2,72,512]{2,1,0:T(8,128)(2,1)S(1)}, bf16[2,72,512]{2,1,0:T(8,128)(2,1)S(1)}, u32[]{:S(2)}, u32[]{:S(2)}) collective-permute-start(bf16[2,72,512]{2,1,0:T(8,128)(2,1)S(1)} %get-tuple-element.163), channel_id=1, source_target_pairs={{0,6},{2,0},{4,2},{6,4},{1,7},{3,1},{5,3},{7,5},{8,14},{10,8},{12,... | collective-permute-start | bytes 442376 | tf_op jit(solution)/shard_map/ppermute | solution.py:31
  143.4 6.4 %copy-start.6 = (bf16[1280,1024]{1,0:T(8,128)(2,1)S(1)}, bf16[1280,1024]{1,0:T(8,128)(2,1)}, u32[]{:S(2)}) copy-start(bf16[1280,1024]{1,0:T(8,128)(2,1)} %get-tuple-element.106) | copy-start | bytes 7864324
  145.7 7.9 %copy-start.5 = (bf16[1280,1024]{1,0:T(8,128)(2,1)S(1)}, bf16[1280,1024]{1,0:T(8,128)(2,1)}, u32[]{:S(2)}) copy-start(bf16[1280,1024]{1,0:T(8,128)(2,1)} %get-tuple-element.107) | copy-start | bytes 7864324
  145.7 9.5 %collective-permute-start.27 = (bf16[2,72,512]{2,1,0:T(8,128)(2,1)S(1)}, bf16[2,72,512]{2,1,0:T(8,128)(2,1)S(1)}, u32[]{:S(2)}, u32[]{:S(2)}) collective-permute-start(bf16[2,72,512]{2,1,0:T(8,128)(2,1)S(1)} %pad_maximum_fusion.9), channel_id=1, source_target_pairs={{0,8},{8,16},{16,24},{24,0},{1,9},{9,17},{17,25},{25,1},{2,10},{10... | collective-permute-start | bytes 442376 | tf_op jit(solution)/shard_map/ppermute | solution.py:31
  145.8 9.4 %collective-permute-start.28 = (bf16[2,72,512]{2,1,0:T(8,128)(2,1)S(1)}, bf16[2,72,512]{2,1,0:T(8,128)(2,1)S(1)}, u32[]{:S(2)}, u32[]{:S(2)}) collective-permute-start(bf16[2,72,512]{2,1,0:T(8,128)(2,1)S(1)} %pad_maximum_fusion.9), channel_id=1, source_target_pairs={{0,16},{8,24},{16,0},{24,8},{1,17},{9,25},{17,1},{25,9},{2,18},{10... | collective-permute-start | bytes 442376 | tf_op jit(solution)/shard_map/ppermute | solution.py:31
  146.9 8.4 %collective-permute-start.29 = (bf16[2,72,512]{2,1,0:T(8,128)(2,1)S(1)}, bf16[2,72,512]{2,1,0:T(8,128)(2,1)S(1)}, u32[]{:S(2)}, u32[]{:S(2)}) collective-permute-start(bf16[2,72,512]{2,1,0:T(8,128)(2,1)S(1)} %pad_maximum_fusion.9), channel_id=1, source_target_pairs={{0,24},{8,0},{16,8},{24,16},{1,25},{9,1},{17,9},{25,17},{2,26},{10... | collective-permute-start | bytes 442376 | tf_op jit(solution)/shard_map/ppermute | solution.py:31
  156.4 8.8 %collective-permute-start.32 = (bf16[2,64,512]{2,1,0:T(8,128)(2,1)S(1)}, bf16[2,64,512]{2,1,0:T(8,128)(2,1)S(1)}, u32[]{:S(2)}, u32[]{:S(2)}) collective-permute-start(bf16[2,64,512]{2,1,0:T(8,128)(2,1)S(1)} %get-tuple-element.145), channel_id=1, source_target_pairs={{0,2},{2,4},{4,6},{6,0},{1,3},{3,5},{5,7},{7,1},{8,10},{10,12},{12... | collective-permute-start | bytes 393224 | tf_op jit(solution)/shard_map/ppermute | solution.py:31
  158.5 6.8 %collective-permute-start.33 = (bf16[2,64,512]{2,1,0:T(8,128)(2,1)S(1)}, bf16[2,64,512]{2,1,0:T(8,128)(2,1)S(1)}, u32[]{:S(2)}, u32[]{:S(2)}) collective-permute-start(bf16[2,64,512]{2,1,0:T(8,128)(2,1)S(1)} %get-tuple-element.144), channel_id=1, source_target_pairs={{0,4},{2,6},{4,0},{6,2},{1,5},{3,7},{5,1},{7,3},{8,12},{10,14},{12... | collective-permute-start | bytes 393224 | tf_op jit(solution)/shard_map/ppermute | solution.py:31
  160.9 4.4 %collective-permute-start.34 = (bf16[2,64,512]{2,1,0:T(8,128)(2,1)S(1)}, bf16[2,64,512]{2,1,0:T(8,128)(2,1)S(1)}, u32[]{:S(2)}, u32[]{:S(2)}) collective-permute-start(bf16[2,64,512]{2,1,0:T(8,128)(2,1)S(1)} %get-tuple-element.143), channel_id=1, source_target_pairs={{0,6},{2,0},{4,2},{6,4},{1,7},{3,1},{5,3},{7,5},{8,14},{10,8},{12,... | collective-permute-start | bytes 393224 | tf_op jit(solution)/shard_map/ppermute | solution.py:31
  167.2 16.9 %collective-permute-start.35 = (bf16[640,1024]{1,0:T(8,128)(2,1)S(1)}, bf16[640,1024]{1,0:T(8,128)(2,1)S(1)}, u32[]{:S(2)}, u32[]{:S(2)}) collective-permute-start(bf16[640,1024]{1,0:T(8,128)(2,1)S(1)} %readout.3), channel_id=1, source_target_pairs={{0,1},{1,0},{2,3},{3,2},{4,5},{5,4},{6,7},{7,6},{8,9},{9,8},{10,11... | collective-permute-start | bytes 3932168 | tf_op jit(solution)/shard_map/ppermute | solution.py:27
  (1 other events, 0.8 us)
Sparse Core Ops, SparseCore 0:
  13.3 86.3 all-gather.1

commit v2 on v1

--- a/solution.py
+++ b/solution.py
@@ -110,17 +110,33 @@
     )(places, own, mate, w_gates)
 
 
-def prepare_kernel(
-    core_ref, query, key, value, mate_query, mate_key, mate_value, region, held_ref, q_ref, rest_ref
-):
+def prepare_values_kernel(core_ref, value, mate_value, rest_ref):
+    core = core_ref[0]
+    wide = pl.ds(pl.multiple_of(core * 2 * WIDE, WIDE), 2 * WIDE)
+    for source, rows in ((value, core), (mate_value, 1 - core)):
+        rest_ref[pl.ds(pl.multiple_of(rows * OWN, OWN), OWN), :] = source[:, wide]
+
+
+def prepare_values(core, own, mate):
+    vmem = pl.BlockSpec(memory_space=pltpu.VMEM)
+    return pl.pallas_call(
+        prepare_values_kernel,
+        in_specs=[pl.BlockSpec(memory_space=pltpu.SMEM)] + [vmem] * 2,
+        out_specs=vmem,
+        out_shape=jax.ShapeDtypeStruct((PIECE, 2 * WIDE), BF),
+        compiler_params=LARGE,
+        cost_estimate=COST,
+        name="prepare_values",
+    )(core, own, mate)
+
+
+def prepare_kernel(core_ref, query, key, mate_query, mate_key, region, held_ref, q_ref):
     core = core_ref[0]
     narrow = pl.ds(pl.multiple_of(core * WIDE, WIDE), WIDE)
-    wide = pl.ds(pl.multiple_of(core * 2 * WIDE, WIDE), 2 * WIDE)
-    for source, rows in (((query, key, value), core), ((mate_query, mate_key, mate_value), 1 - core)):
+    for queries, keys, rows in ((query, key, core), (mate_query, mate_key, 1 - core)):
         rows = pl.ds(pl.multiple_of(rows * OWN, OWN), OWN)
-        q_ref[rows, :] = source[0][:, narrow]
-        held_ref[rows, :] = source[1][:, narrow]
-        rest_ref[rows, :] = source[2][:, wide]
+        q_ref[rows, :] = queries[:, narrow]
+        held_ref[rows, :] = keys[:, narrow]
     held_ref[PIECE:, :] = region[...]
 
 
@@ -128,14 +144,13 @@
     vmem = pl.BlockSpec(memory_space=pltpu.VMEM)
     return pl.pallas_call(
         prepare_kernel,
-        in_specs=[pl.BlockSpec(memory_space=pltpu.SMEM)] + [vmem] * 7,
-        out_specs=[vmem] * 3,
+        in_specs=[pl.BlockSpec(memory_space=pltpu.SMEM)] + [vmem] * 5,
+        out_specs=[vmem] * 2,
         out_shape=[
             jax.ShapeDtypeStruct((PIECE + EXTRA, WIDE), BF),
             jax.ShapeDtypeStruct((PIECE, WIDE), BF),
-            jax.ShapeDtypeStruct((PIECE, 2 * WIDE), BF),
         ],
-        compiler_params=PARAMS,
+        compiler_params=LARGE,
         cost_estimate=COST,
         name="prepare",
     )(core, *own, *mate, region)
@@ -427,9 +442,11 @@
     restore_places = jnp.concatenate([places(last), core_scalar])
     q_places = jnp.concatenate([places(middle), core_scalar])
 
-    own = (w_query, w_key, w_value)
+    rest = prepare_values(core_scalar, w_value, swap(w_value))
+    w_query, w_key, w_gates, rest = together(w_query, w_key, w_gates, rest)
+    own = (w_query, w_key)
     mate = tuple(swap(weight) for weight in own)
-    held, columns, rest = prepare(core_scalar, own, mate, gate_rows(w_gates, core, middle * 4 + y))
+    held, columns = prepare(core_scalar, own, mate, gate_rows(w_gates, core, middle * 4 + y))
     rest = lax.all_gather(rest, ("y", "z", "x"), axis=0, tiled=True)
     tokens = together(tokens[0], held)[0]
     mate_tokens = swap(tokens)

time: 194 us -> 191 us (0.985)
  waiting for transfers between devices: 27.1 us -> 21.8 us
  Pallas kernels: 35.4 us -> 38 us
    ppermute x21, waiting for transfers between devices: 21.5 us -> 16.8 us  [hop(): return lax.ppermute(value, names, pairs)]
  transfers between devices with their start and end apart: 37 -> 37, of which waited for: 17 -> 13; matrix products, arithmetic and copies ran while one was open for 27% -> 28% of each run, Pallas kernels for 17% -> 18%
where the time goes in v2:
time: 191 us
  starting transfers between devices  56.5 us (30%)
  matrix products  42.1 us (22%)
  Pallas kernels  38 us (20%)
  waiting for transfers between devices  21.8 us (11%)
  between operations  14.3 us (7%)
  other arithmetic  9.46 us (5%)
  local copies, waits for them, and re-layouts  8.43 us (4%)
    ppermute x21, starting transfers between devices, hop(): return lax.ppermute(value, names, pairs)  29.5 us
    dot_general x8, matrix products, project(): term = jnp.dot(chunk, weight, preferred_element_type=F32)  26.1 us
    pallas_call x1, Pallas kernels, normalize(): pl.pallas_call(normalize_kernel, grid_spec=pltpu.PrefetchScalarGridSpec(n...  20.4 us
    ppermute x6, starting transfers between devices, swap(): return lax.ppermute(value, 'core', [(0, 1), (1, 0)])  17.3 us
    ppermute x21, waiting for transfers between devices, hop(): return lax.ppermute(value, names, pairs)  16.8 us
    dot_general x1, matrix products, per_device(): value = jnp.dot(normed, rest, preferred_element_type=F32).astype(BF)  15.9 us
    ppermute x9, starting transfers between devices, shift(): return lax.ppermute(value, axis, [(i, (i + by) % 4) for i in range(4)])  9.74 us
  transfers between devices with their start and end apart: 37, of which 13 were waited for; matrix products, arithmetic and copies ran while one was open for 28% of the time, Pallas kernels for 18%

profile of v2, /device:TPU:25, one launch (start us, length us, event | category | flops | bytes accessed | tf_op | source)
XLA Modules:
  0.0 190.5 jit_solution(3627271612798263532)
XLA Ops:
  7.2 1.2 collective-permute-done.mate_value
  9.1 1.6 prepare_values.1
  14.7 1.6 prepare.1
  20.7 2.0 %collective-permute-start.6 = (bf16[80,512]{1,0:T(8,128)(2,1)}, bf16[80,512]{1,0:T(8,128)(2,1)S(1)}, u32[]{:S(2)}, u32[]{:S(2)}) collective-permute-start(bf16[80,512]{1,0:T(8,128)(2,1)} %get-tuple-element.66.refs_0_), channel_id=1, source_target_pairs={{0,32},{1,33},{2,34},{3,35},{4,36},{5,37},{6,38},{7,39},{8,40},{9,... | collective-permute-start | bytes 245768 | tf_op jit(solution)/shard_map/ppermute | solution.py:42
  22.8 4.4 %collective-permute-done.4.refs_1_ = bf16[80,512]{1,0:T(8,128)(2,1)S(1)} collective-permute-done((bf16[80,512]{1,0:T(8,128)(2,1)}, bf16[80,512]{1,0:T(8,128)(2,1)S(1)}, u32[]{:S(2)}, u32[]{:S(2)}) %collective-permute-start.4) | collective-permute-done | bytes 81952 | tf_op jit(solution)/shard_map/ppermute | solution.py:42
  28.4 1.1 assemble.2.refs_0_
  29.6 2.5 %collective-permute-start.7 = (bf16[272,512]{1,0:T(8,128)(2,1)S(1)}, bf16[272,512]{1,0:T(8,128)(2,1)S(1)}, u32[]{:S(2)}, u32[]{:S(2)}) collective-permute-start(bf16[272,512]{1,0:T(8,128)(2,1)S(1)} %assemble.2.refs_0_), channel_id=1, source_target_pairs={{0,24},{1,7},{2,26},{3,1},{4,28},{5,3},{6,30},{7,5},{8,0},{9,15},{... | collective-permute-start | bytes 835592 | tf_op jit(solution)/shard_map/ppermute | solution.py:42
  33.5 2.1 %collective-permute-start.10 = (bf16[64,512]{1,0:T(8,128)(2,1)}, bf16[64,512]{1,0:T(8,128)(2,1)S(1)}, u32[]{:S(2)}, u32[]{:S(2)}) collective-permute-start(bf16[64,512]{1,0:T(8,128)(2,1)} %get-tuple-element.78.refs_0_), channel_id=1, source_target_pairs={{0,24},{1,7},{2,26},{3,1},{4,28},{5,3},{6,30},{7,5},{8,0},{9,15},{... | collective-permute-start | bytes 196616 | tf_op jit(solution)/shard_map/ppermute | solution.py:42
  35.6 3.2 %collective-permute-done.7.refs_1_ = bf16[272,512]{1,0:T(8,128)(2,1)S(1)} collective-permute-done((bf16[272,512]{1,0:T(8,128)(2,1)S(1)}, bf16[272,512]{1,0:T(8,128)(2,1)S(1)}, u32[]{:S(2)}, u32[]{:S(2)}) %collective-permute-start.7) | collective-permute-done | bytes 278560 | tf_op jit(solution)/shard_map/ppermute | solution.py:42
  39.4 3.2 %collective-permute-start.12 = (bf16[64,512]{1,0:T(8,128)(2,1)}, bf16[64,512]{1,0:T(8,128)(2,1)S(1)}, u32[]{:S(2)}, u32[]{:S(2)}) collective-permute-start(bf16[64,512]{1,0:T(8,128)(2,1)} %get-tuple-element.78.refs_0_), channel_id=1, source_target_pairs={{0,8},{1,3},{2,10},{3,5},{4,12},{5,7},{6,14},{7,1},{8,16},{9,11},{... | collective-permute-start | bytes 196616 | tf_op jit(solution)/shard_map/ppermute | solution.py:42
  42.5 1.9 assemble.3
  44.4 4.7 %collective-permute-start.17 = (bf16[16,512]{1,0:T(8,128)(2,1)S(1)}, bf16[16,512]{1,0:T(8,128)(2,1)S(1)}, u32[]{:S(2)}, u32[]{:S(2)}) collective-permute-start(bf16[16,512]{1,0:T(8,128)(2,1)S(1)} %get-tuple-element.89), channel_id=1, source_target_pairs={{0,6},{1,25},{2,0},{3,27},{4,2},{5,29},{6,4},{7,31},{8,14},{9,1},{... | collective-permute-start | bytes 49160 | tf_op jit(solution)/shard_map/ppermute | solution.py:42
  52.2 2.1 %collective-permute-start.13 = (bf16[256,512]{1,0:T(8,128)(2,1)S(1)}, bf16[256,512]{1,0:T(8,128)(2,1)S(1)}, u32[]{:S(2)}, u32[]{:S(2)}) collective-permute-start(bf16[256,512]{1,0:T(8,128)(2,1)S(1)} %bitcast.172), channel_id=1, source_target_pairs={{0,6},{1,25},{2,0},{3,27},{4,2},{5,29},{6,4},{7,31},{8,14},{9,1},{... | collective-permute-start | bytes 786440 | tf_op jit(solution)/shard_map/ppermute | solution.py:42
  54.3 1.7 collective-permute-start.14
  57.0 2.8 %collective-permute-done.13 = bf16[256,512]{1,0:T(8,128)(2,1)S(1)} collective-permute-done((bf16[256,512]{1,0:T(8,128)(2,1)S(1)}, bf16[256,512]{1,0:T(8,128)(2,1)S(1)}, u32[]{:S(2)}, u32[]{:S(2)}) %collective-permute-start.13) | collective-permute-done | bytes 262176 | tf_op jit(solution)/shard_map/ppermute | solution.py:42
  59.8 1.5 collective-permute-done.14
  61.3 3.0 %collective-permute-done.15 = bf16[256,512]{1,0:T(8,128)(2,1)S(1)} collective-permute-done((bf16[256,512]{1,0:T(8,128)(2,1)S(1)}, bf16[256,512]{1,0:T(8,128)(2,1)S(1)}, u32[]{:S(2)}, u32[]{:S(2)}) %collective-permute-start.15) | collective-permute-done | bytes 262176 | tf_op jit(solution)/shard_map/ppermute | solution.py:42
  64.3 1.8 weave.3
  66.2 20.4 %normalize.1 = (f32[16,1280]{1,0:T(8,128)}, bf16[1280,4096]{1,0:T(8,128)(2,1)}, bf16[1280,1024]{1,0:T(8,128)(2,1)}, bf16[1280,1024]{1,0:T(8,128)(2,1)}, bf16[128...) custom-call(s32[9]{0:T(128)} %concatenate.69.places, ...), custom_call_target="tpu_custom_call" | custom-call | bytes 33554432 | tf_op jit(solution)/shard_map/normalize/pallas_call | solution.py:87
  87.5 1.2 reduce-window.21
  89.7 5.2 %fusion.49 = f32[1280,512]{1,0:T(8,128)} fusion(bf16[1280,1024]{1,0:T(8,128)(2,1)} %get-tuple-element.94, bf16[1024,512]{1,0:T(8,128)(2,1)} %bitcast.26), kind=kOutput, calls=%fused_computation.154 | convolution fusion | flops 1342177280 | bytes 6291456 | tf_op jit(solution)/shard_map/dot_general | solution.py:267
  94.8 4.2 %fusion.48 = f32[1280,512]{1,0:T(8,128)} fusion(bf16[1280,1024]{1,0:T(8,128)(2,1)S(1)} %copy-done.11, bf16[1024,512]{1,0:T(8,128)(2,1)} %get-tuple-element.100), kind=kOutput, calls=%fused_computation.153 | convolution fusion | flops 1342177280 | bytes 6291456 | tf_op jit(solution)/shard_map/dot_general | solution.py:267
  99.1 1.4 collective-permute-start.21
  100.5 2.7 %collective-permute-start.20 = (bf16[1024,512]{1,0:T(8,128)(2,1)}, bf16[1024,512]{1,0:T(8,128)(2,1)}, u32[]{:S(2)}, u32[]{:S(2)}) collective-permute-start(bf16[1024,512]{1,0:T(8,128)(2,1)} %get-tuple-element.100), channel_id=1, source_target_pairs={{0,6},{1,25},{2,0},{3,27},{4,2},{5,29},{6,4},{7,31},{8,14},{9,1},{... | collective-permute-start | bytes 3145736 | tf_op jit(solution)/shard_map/ppermute | solution.py:42
  103.6 3.4 %collective-permute-start.30 = (bf16[1024,512]{1,0:T(8,128)(2,1)}, bf16[1024,512]{1,0:T(8,128)(2,1)}, u32[]{:S(2)}, u32[]{:S(2)}) collective-permute-start(bf16[1024,512]{1,0:T(8,128)(2,1)} %bitcast.26), channel_id=1, source_target_pairs={{0,64},{1,65},{2,66},{3,67},{4,68},{5,69},{6,70},{7,71},{8,72},{9,... | collective-permute-start | bytes 3145736 | tf_op jit(solution)/shard_map/ppermute | solution.py:42
  107.0 15.9 %convolution_convert_fusion.left_ref.right_ref = bf16[1280,1024]{1,0:T(8,128)(2,1)S(1)} fusion(bf16[1280,4096]{1,0:T(8,128)(2,1)} %get-tuple-element.103, bf16[4096,1024]{1,0:T(8,128)(2,1)} %all-gather.2.cloned.1.call-done), kind=kOutput, calls=%fused_computation | convolution fusion | flops 10738728960 | bytes 21495808 | tf_op jit(solution)/shard_map/dot_general | solution.py:498
  123.5 3.7 %fusion.50 = f32[1280,512]{1,0:T(8,128)S(1)} fusion(bf16[1280,1024]{1,0:T(8,128)(2,1)} %get-tuple-element.101, bf16[1024,512]{1,0:T(8,128)(2,1)} %collective-permute-done.21), kind=kOutput, calls=%fused_computation.155 | convolution fusion | flops 1342177280 | bytes 6291456 | tf_op jit(solution)/shard_map/dot_general | solution.py:267
  127.3 2.9 %fusion.51 = f32[1280,512]{1,0:T(8,128)S(1)} fusion(bf16[1280,1024]{1,0:T(8,128)(2,1)S(1)} %copy-done.10, bf16[1024,512]{1,0:T(8,128)(2,1)} %collective-permute-done.22), kind=kOutput, calls=%fused_computation.156 | convolution fusion | flops 1342177280 | bytes 6291456 | tf_op jit(solution)/shard_map/dot_general | solution.py:267
  130.2 3.0 %fusion.2.key_ref = bf16[1280,512]{1,0:T(8,128)(2,1)S(1)} fusion(f32[1280,512]{1,0:T(8,128)S(1)} %fusion.51, f32[1280,512]{1,0:T(8,128)S(1)} %fusion.50, f32[1280,512]{1,0:T(8,128)S(1)} %copy-done.3, bf16[1280,1024]{1,0:T(8,128)(2,1)S(1)} %copy-done.2, bf16[1024,512]{1,0:T(8,128)(2,1)} %collective-permute-done.20), kind=kOutput, calls=%fused_computation.5 | convolution fusion | flops 1344798720 | bytes 12845056 | tf_op jit(solution)/shard_map/dot_general | solution.py:267
  133.2 2.2 %states.1 = bf16[2,2,256,512]{3,2,1,0:T(8,128)(2,1)S(1)} custom-call(f32[2,640,8]{2,1,0:T(8,128)S(1)} %copy.86.cols_ref, bf16[1280,512]{1,0:T(8,128)(2,1)S(1)} %fusion.2.key_ref, bf16[1280,1024]{1,0:T(8,128)(2,1)S(1)} %convolution_convert_fusion.left_ref.right_ref, bf16[1280,1024]{1,0:T(8,128)(2,1)S(1)} %convolution_convert_fusion.left_ref.right_ref), custom_call_target="tpu_custom_call" | custom-call | bytes 1024 | tf_op jit(solution)/shard_map/states/pallas_call | solution.py:284
  136.1 1.5 collective-permute-start.24
  137.6 1.3 collective-permute-start.25
  138.9 2.8 %convolution_add_fusion = f32[1280,512]{1,0:T(8,128)S(1)} fusion(f32[1280,512]{1,0:T(8,128)S(1)} %copy-done.13, bf16[1280,1024]{1,0:T(8,128)(2,1)S(1)} %copy-done.9, bf16[1024,512]{1,0:T(8,128)(2,1)} %collective-permute-done.26), kind=kOutput, calls=%fused_computation.1 | convolution fusion | flops 1342832640 | bytes 8912896 | tf_op jit(solution)/shard_map/dot_general | solution.py:267
  141.7 1.6 collective-permute-done.23
  144.6 1.4 collective-permute-start.28
  146.0 1.3 collective-permute-start.29
  147.3 1.0 collective-permute-done.30
  148.3 2.8 %fusion.52 = f32[1280,512]{1,0:T(8,128)S(1)} fusion(bf16[1280,1024]{1,0:T(8,128)(2,1)S(1)} %copy-done.8, bf16[1024,512]{1,0:T(8,128)(2,1)} %collective-permute-done.30), kind=kOutput, calls=%fused_computation.157 | convolution fusion | flops 1342177280 | bytes 6291456 | tf_op jit(solution)/shard_map/dot_general | solution.py:267
  151.1 1.6 add_convert_fusion.query_ref
  153.9 1.6 collective-permute-start.32
  155.5 1.1 collective-permute-start.33
  156.6 1.3 collective-permute-start.34
  158.0 3.6 %intra.1.intra_ref = f32[1280,1024]{1,0:T(8,128)S(1)} custom-call(f32[2,640,8]{2,1,0:T(8,128)S(1)} %copy.86.cols_ref, f32[2,8,640]{2,1,0:T(8,128)S(1)} %bitcast.178, bf16[1280,512]{1,0:T(8,128)(2,1)S(1)} %add_convert_fusion.query_ref, bf16[1280,512]{1,0:T(8,128)(2,1)S(1)} %fusion.2.key_ref, ...), custom_call_target="tpu_custom_call" | custom-call | bytes 1024 | tf_op jit(solution)/shard_map/intra/pallas_call | solution.py:324
  162.3 1.4 readout.3
  163.6 15.4 %collective-permute-start.35 = (bf16[640,1024]{1,0:T(8,128)(2,1)S(1)}, bf16[640,1024]{1,0:T(8,128)(2,1)S(1)}, u32[]{:S(2)}, u32[]{:S(2)}) collective-permute-start(bf16[640,1024]{1,0:T(8,128)(2,1)S(1)} %readout.3), channel_id=1, source_target_pairs={{0,1},{1,0},{2,3},{3,2},{4,5},{5,4},{6,7},{7,6},{8,9},{9,8},{10,11... | collective-permute-start | bytes 3932168 | tf_op jit(solution)/shard_map/ppermute | solution.py:27
  179.0 1.4 readout.2
  180.4 1.3 collective-permute-done.35
  181.7 2.0 %maximum_select_fusion = bf16[1,640,2048]{2,1,0:T(8,128)(2,1)} fusion(bf16[1,640,1024]{2,1,0:T(8,128)(2,1)S(1)} %bitcast.184, bf16[1,640,1024]{2,1,0:T(8,128)(2,1)S(1)} %bitcast.171, pred[]{:T(512)S(6)} %eq.94), kind=kLoop, calls=%fused_computation.6 | loop fusion | flops 11796480 | bytes 5242881 | tf_op jit(solution)/shard_map/jit(_where)/select_n | solution.py:521
  (159 shorter events, 23.4 us)
Async XLA Ops:
  6.5 44.5 %copy-start.12 = (f32[4]{0:T(128)S(1)}, f32[4]{0:T(128)}, u32[]{:S(2)}) copy-start(f32[4]{0:T(128)} %param.12) | copy-start | bytes 52
  6.5 92.6 %all-gather.2.cloned.1.call-start = ((), (), s32[]{:S(2)}) async-start(), calls=%async_computation | async-start | bytes 8519680 | tf_op jit(solution)/shard_map/all_gather | solution.py:450
  6.5 1.9 collective-permute-start
  11.4 1.2 collective-permute-start.3
  11.8 1.7 collective-permute-start.1
  12.0 1.6 collective-permute-start.2
  16.3 34.8 %copy-start.1 = (bf16[64,512]{1,0:T(8,128)(2,1)S(1)}, bf16[64,512]{1,0:T(8,128)(2,1)}, u32[]{:S(2)}) copy-start(bf16[64,512]{1,0:T(8,128)(2,1)} %get-tuple-element.78.refs_0_) | copy-start | bytes 196612
  16.3 49.8 %collective-permute-start.16 = (bf16[640,4096]{1,0:T(8,128)(2,1)}, bf16[640,4096]{1,0:T(8,128)(2,1)}, u32[]{:S(2)}, u32[]{:S(2)}) collective-permute-start(bf16[640,4096]{1,0:T(8,128)(2,1)} %bitcast.180), channel_id=1, source_target_pairs={{0,1},{1,0},{2,3},{3,2},{4,5},{5,4},{6,7},{7,6},{8,9},{9,8},{10,11... | collective-permute-start | bytes 15728648 | tf_op jit(solution)/shard_map/ppermute | solution.py:27
  19.6 7.5 %collective-permute-start.4 = (bf16[80,512]{1,0:T(8,128)(2,1)}, bf16[80,512]{1,0:T(8,128)(2,1)S(1)}, u32[]{:S(2)}, u32[]{:S(2)}) collective-permute-start(bf16[80,512]{1,0:T(8,128)(2,1)} %get-tuple-element.66.refs_0_), channel_id=1, source_target_pairs={{0,96},{1,97},{2,98},{3,99},{4,100},{5,101},{6,102},{7,103},{8,104... | collective-permute-start | bytes 245768 | tf_op jit(solution)/shard_map/ppermute | solution.py:42
  20.1 7.0 %collective-permute-start.5 = (bf16[80,512]{1,0:T(8,128)(2,1)}, bf16[80,512]{1,0:T(8,128)(2,1)S(1)}, u32[]{:S(2)}, u32[]{:S(2)}) collective-permute-start(bf16[80,512]{1,0:T(8,128)(2,1)} %get-tuple-element.66.refs_0_), channel_id=1, source_target_pairs={{0,64},{1,65},{2,66},{3,67},{4,68},{5,69},{6,70},{7,71},{8,72},{9,... | collective-permute-start | bytes 245768 | tf_op jit(solution)/shard_map/ppermute | solution.py:42
  20.7 6.8 %collective-permute-start.6 = (bf16[80,512]{1,0:T(8,128)(2,1)}, bf16[80,512]{1,0:T(8,128)(2,1)S(1)}, u32[]{:S(2)}, u32[]{:S(2)}) collective-permute-start(bf16[80,512]{1,0:T(8,128)(2,1)} %get-tuple-element.66.refs_0_), channel_id=1, source_target_pairs={{0,32},{1,33},{2,34},{3,35},{4,36},{5,37},{6,38},{7,39},{8,40},{9,... | collective-permute-start | bytes 245768 | tf_op jit(solution)/shard_map/ppermute | solution.py:42
  27.5 0.9 copy-start
  29.6 9.2 %collective-permute-start.7 = (bf16[272,512]{1,0:T(8,128)(2,1)S(1)}, bf16[272,512]{1,0:T(8,128)(2,1)S(1)}, u32[]{:S(2)}, u32[]{:S(2)}) collective-permute-start(bf16[272,512]{1,0:T(8,128)(2,1)S(1)} %assemble.2.refs_0_), channel_id=1, source_target_pairs={{0,24},{1,7},{2,26},{3,1},{4,28},{5,3},{6,30},{7,5},{8,0},{9,15},{... | collective-permute-start | bytes 835592 | tf_op jit(solution)/shard_map/ppermute | solution.py:42
  32.2 7.1 %collective-permute-start.8 = (bf16[272,512]{1,0:T(8,128)(2,1)S(1)}, bf16[272,512]{1,0:T(8,128)(2,1)S(1)}, u32[]{:S(2)}, u32[]{:S(2)}) collective-permute-start(bf16[272,512]{1,0:T(8,128)(2,1)S(1)} %assemble.2.refs_0_), channel_id=1, source_target_pairs={{0,16},{1,5},{2,18},{3,7},{4,20},{5,1},{6,22},{7,3},{8,24},{9,13},... | collective-permute-start | bytes 835592 | tf_op jit(solution)/shard_map/ppermute | solution.py:42
  32.8 9.7 %collective-permute-start.9 = (bf16[272,512]{1,0:T(8,128)(2,1)S(1)}, bf16[272,512]{1,0:T(8,128)(2,1)S(1)}, u32[]{:S(2)}, u32[]{:S(2)}) collective-permute-start(bf16[272,512]{1,0:T(8,128)(2,1)S(1)} %assemble.2.refs_0_), channel_id=1, source_target_pairs={{0,8},{1,3},{2,10},{3,5},{4,12},{5,7},{6,14},{7,1},{8,16},{9,11},{... | collective-permute-start | bytes 835592 | tf_op jit(solution)/shard_map/ppermute | solution.py:42
  33.5 15.7 %collective-permute-start.10 = (bf16[64,512]{1,0:T(8,128)(2,1)}, bf16[64,512]{1,0:T(8,128)(2,1)S(1)}, u32[]{:S(2)}, u32[]{:S(2)}) collective-permute-start(bf16[64,512]{1,0:T(8,128)(2,1)} %get-tuple-element.78.refs_0_), channel_id=1, source_target_pairs={{0,24},{1,7},{2,26},{3,1},{4,28},{5,3},{6,30},{7,5},{8,0},{9,15},{... | collective-permute-start | bytes 196616 | tf_op jit(solution)/shard_map/ppermute | solution.py:42
  38.8 10.4 %collective-permute-start.11 = (bf16[64,512]{1,0:T(8,128)(2,1)}, bf16[64,512]{1,0:T(8,128)(2,1)S(1)}, u32[]{:S(2)}, u32[]{:S(2)}) collective-permute-start(bf16[64,512]{1,0:T(8,128)(2,1)} %get-tuple-element.78.refs_0_), channel_id=1, source_target_pairs={{0,16},{1,5},{2,18},{3,7},{4,20},{5,1},{6,22},{7,3},{8,24},{9,13},... | collective-permute-start | bytes 196616 | tf_op jit(solution)/shard_map/ppermute | solution.py:42
  39.4 11.8 %collective-permute-start.12 = (bf16[64,512]{1,0:T(8,128)(2,1)}, bf16[64,512]{1,0:T(8,128)(2,1)S(1)}, u32[]{:S(2)}, u32[]{:S(2)}) collective-permute-start(bf16[64,512]{1,0:T(8,128)(2,1)} %get-tuple-element.78.refs_0_), channel_id=1, source_target_pairs={{0,8},{1,3},{2,10},{3,5},{4,12},{5,7},{6,14},{7,1},{8,16},{9,11},{... | collective-permute-start | bytes 196616 | tf_op jit(solution)/shard_map/ppermute | solution.py:42
  44.4 9.9 %collective-permute-start.17 = (bf16[16,512]{1,0:T(8,128)(2,1)S(1)}, bf16[16,512]{1,0:T(8,128)(2,1)S(1)}, u32[]{:S(2)}, u32[]{:S(2)}) collective-permute-start(bf16[16,512]{1,0:T(8,128)(2,1)S(1)} %get-tuple-element.89), channel_id=1, source_target_pairs={{0,6},{1,25},{2,0},{3,27},{4,2},{5,29},{6,4},{7,31},{8,14},{9,1},{... | collective-permute-start | bytes 49160 | tf_op jit(solution)/shard_map/ppermute | solution.py:42
  49.2 6.8 %collective-permute-start.18 = (bf16[16,512]{1,0:T(8,128)(2,1)S(1)}, bf16[16,512]{1,0:T(8,128)(2,1)S(1)}, u32[]{:S(2)}, u32[]{:S(2)}) collective-permute-start(bf16[16,512]{1,0:T(8,128)(2,1)S(1)} %get-tuple-element.89), channel_id=1, source_target_pairs={{0,4},{1,17},{2,6},{3,19},{4,0},{5,21},{6,2},{7,23},{8,12},{9,25},... | collective-permute-start | bytes 49160 | tf_op jit(solution)/shard_map/ppermute | solution.py:42
  49.2 6.8 %collective-permute-start.19 = (bf16[16,512]{1,0:T(8,128)(2,1)S(1)}, bf16[16,512]{1,0:T(8,128)(2,1)S(1)}, u32[]{:S(2)}, u32[]{:S(2)}) collective-permute-start(bf16[16,512]{1,0:T(8,128)(2,1)S(1)} %get-tuple-element.89), channel_id=1, source_target_pairs={{0,2},{1,9},{2,4},{3,11},{4,6},{5,13},{6,0},{7,15},{8,10},{9,17},{... | collective-permute-start | bytes 49160 | tf_op jit(solution)/shard_map/ppermute | solution.py:42
  52.2 7.6 %collective-permute-start.13 = (bf16[256,512]{1,0:T(8,128)(2,1)S(1)}, bf16[256,512]{1,0:T(8,128)(2,1)S(1)}, u32[]{:S(2)}, u32[]{:S(2)}) collective-permute-start(bf16[256,512]{1,0:T(8,128)(2,1)S(1)} %bitcast.172), channel_id=1, source_target_pairs={{0,6},{1,25},{2,0},{3,27},{4,2},{5,29},{6,4},{7,31},{8,14},{9,1},{... | collective-permute-start | bytes 786440 | tf_op jit(solution)/shard_map/ppermute | solution.py:42
  54.3 7.0 %collective-permute-start.14 = (bf16[256,512]{1,0:T(8,128)(2,1)S(1)}, bf16[256,512]{1,0:T(8,128)(2,1)S(1)}, u32[]{:S(2)}, u32[]{:S(2)}) collective-permute-start(bf16[256,512]{1,0:T(8,128)(2,1)S(1)} %bitcast.173), channel_id=1, source_target_pairs={{0,4},{1,17},{2,6},{3,19},{4,0},{5,21},{6,2},{7,23},{8,12},{9,25},... | collective-permute-start | bytes 786440 | tf_op jit(solution)/shard_map/ppermute | solution.py:42
  56.0 8.3 %collective-permute-start.15 = (bf16[256,512]{1,0:T(8,128)(2,1)S(1)}, bf16[256,512]{1,0:T(8,128)(2,1)S(1)}, u32[]{:S(2)}, u32[]{:S(2)}) collective-permute-start(bf16[256,512]{1,0:T(8,128)(2,1)S(1)} %bitcast.174), channel_id=1, source_target_pairs={{0,2},{1,9},{2,4},{3,11},{4,6},{5,13},{6,0},{7,15},{8,10},{9,17},{... | collective-permute-start | bytes 786440 | tf_op jit(solution)/shard_map/ppermute | solution.py:42
  89.7 5.2 %copy-start.11 = (bf16[1280,1024]{1,0:T(8,128)(2,1)S(1)}, bf16[1280,1024]{1,0:T(8,128)(2,1)}, u32[]{:S(2)}) copy-start(bf16[1280,1024]{1,0:T(8,128)(2,1)} %get-tuple-element.93) | copy-start | bytes 7864324
  99.1 24.1 %collective-permute-start.21 = (bf16[1024,512]{1,0:T(8,128)(2,1)}, bf16[1024,512]{1,0:T(8,128)(2,1)}, u32[]{:S(2)}, u32[]{:S(2)}) collective-permute-start(bf16[1024,512]{1,0:T(8,128)(2,1)} %get-tuple-element.100), channel_id=1, source_target_pairs={{0,4},{1,17},{2,6},{3,19},{4,0},{5,21},{6,2},{7,23},{8,12},{9,25},... | collective-permute-start | bytes 3145736 | tf_op jit(solution)/shard_map/ppermute | solution.py:42
  100.5 26.8 %collective-permute-start.22 = (bf16[1024,512]{1,0:T(8,128)(2,1)}, bf16[1024,512]{1,0:T(8,128)(2,1)}, u32[]{:S(2)}, u32[]{:S(2)}) collective-permute-start(bf16[1024,512]{1,0:T(8,128)(2,1)} %get-tuple-element.100), channel_id=1, source_target_pairs={{0,2},{1,9},{2,4},{3,11},{4,6},{5,13},{6,0},{7,15},{8,10},{9,17},{... | collective-permute-start | bytes 3145736 | tf_op jit(solution)/shard_map/ppermute | solution.py:42
  100.5 29.7 %collective-permute-start.20 = (bf16[1024,512]{1,0:T(8,128)(2,1)}, bf16[1024,512]{1,0:T(8,128)(2,1)}, u32[]{:S(2)}, u32[]{:S(2)}) collective-permute-start(bf16[1024,512]{1,0:T(8,128)(2,1)} %get-tuple-element.100), channel_id=1, source_target_pairs={{0,6},{1,25},{2,0},{3,27},{4,2},{5,29},{6,4},{7,31},{8,14},{9,1},{... | collective-permute-start | bytes 3145736 | tf_op jit(solution)/shard_map/ppermute | solution.py:42
  103.2 34.4 %collective-permute-start.26 = (bf16[1024,512]{1,0:T(8,128)(2,1)}, bf16[1024,512]{1,0:T(8,128)(2,1)}, u32[]{:S(2)}, u32[]{:S(2)}) collective-permute-start(bf16[1024,512]{1,0:T(8,128)(2,1)} %bitcast.26), channel_id=1, source_target_pairs={{0,96},{1,97},{2,98},{3,99},{4,100},{5,101},{6,102},{7,103},{8,104... | collective-permute-start | bytes 3145736 | tf_op jit(solution)/shard_map/ppermute | solution.py:42
  103.6 44.7 %collective-permute-start.30 = (bf16[1024,512]{1,0:T(8,128)(2,1)}, bf16[1024,512]{1,0:T(8,128)(2,1)}, u32[]{:S(2)}, u32[]{:S(2)}) collective-permute-start(bf16[1024,512]{1,0:T(8,128)(2,1)} %bitcast.26), channel_id=1, source_target_pairs={{0,64},{1,65},{2,66},{3,67},{4,68},{5,69},{6,70},{7,71},{8,72},{9,... | collective-permute-start | bytes 3145736 | tf_op jit(solution)/shard_map/ppermute | solution.py:42
  123.2 27.8 %collective-permute-start.31 = (bf16[1024,512]{1,0:T(8,128)(2,1)}, bf16[1024,512]{1,0:T(8,128)(2,1)S(1)}, u32[]{:S(2)}, u32[]{:S(2)}) collective-permute-start(bf16[1024,512]{1,0:T(8,128)(2,1)} %bitcast.26), channel_id=1, source_target_pairs={{0,32},{1,33},{2,34},{3,35},{4,36},{5,37},{6,38},{7,39},{8,40},{9,... | collective-permute-start | bytes 3145736 | tf_op jit(solution)/shard_map/ppermute | solution.py:42
  123.5 3.7 %copy-start.10 = (bf16[1280,1024]{1,0:T(8,128)(2,1)S(1)}, bf16[1280,1024]{1,0:T(8,128)(2,1)}, u32[]{:S(2)}) copy-start(bf16[1280,1024]{1,0:T(8,128)(2,1)} %get-tuple-element.102) | copy-start | bytes 7864324
  127.3 2.9 %copy-start.2 = (bf16[1280,1024]{1,0:T(8,128)(2,1)S(1)}, bf16[1280,1024]{1,0:T(8,128)(2,1)}, u32[]{:S(2)}) copy-start(bf16[1280,1024]{1,0:T(8,128)(2,1)} %get-tuple-element.99) | copy-start | bytes 7864324
  127.3 2.9 %copy-start.3 = (f32[1280,512]{1,0:T(8,128)S(1)}, f32[1280,512]{1,0:T(8,128)}, u32[]{:S(2)}) copy-start(f32[1280,512]{1,0:T(8,128)} %fusion.48) | copy-start | bytes 7864324
  135.4 3.5 %copy-start.13 = (f32[1280,512]{1,0:T(8,128)S(1)}, f32[1280,512]{1,0:T(8,128)}, u32[]{:S(2)}) copy-start(f32[1280,512]{1,0:T(8,128)} %fusion.49) | copy-start | bytes 7864324
  135.6 3.3 %copy-start.9 = (bf16[1280,1024]{1,0:T(8,128)(2,1)S(1)}, bf16[1280,1024]{1,0:T(8,128)(2,1)}, u32[]{:S(2)}) copy-start(bf16[1280,1024]{1,0:T(8,128)(2,1)} %get-tuple-element.106) | copy-start | bytes 7864324
  136.0 7.3 %collective-permute-start.23 = (bf16[2,72,512]{2,1,0:T(8,128)(2,1)S(1)}, bf16[2,72,512]{2,1,0:T(8,128)(2,1)S(1)}, u32[]{:S(2)}, u32[]{:S(2)}) collective-permute-start(bf16[2,72,512]{2,1,0:T(8,128)(2,1)S(1)} %get-tuple-element.167), channel_id=1, source_target_pairs={{0,2},{2,4},{4,6},{6,0},{1,3},{3,5},{5,7},{7,1},{8,10},{10,12},{12... | collective-permute-start | bytes 442376 | tf_op jit(solution)/shard_map/ppermute | solution.py:31
  136.1 7.2 %collective-permute-start.24 = (bf16[2,72,512]{2,1,0:T(8,128)(2,1)S(1)}, bf16[2,72,512]{2,1,0:T(8,128)(2,1)S(1)}, u32[]{:S(2)}, u32[]{:S(2)}) collective-permute-start(bf16[2,72,512]{2,1,0:T(8,128)(2,1)S(1)} %get-tuple-element.168), channel_id=1, source_target_pairs={{0,4},{2,6},{4,0},{6,2},{1,5},{3,7},{5,1},{7,3},{8,12},{10,14},{12... | collective-permute-start | bytes 442376 | tf_op jit(solution)/shard_map/ppermute | solution.py:31
  137.6 6.3 %collective-permute-start.25 = (bf16[2,72,512]{2,1,0:T(8,128)(2,1)S(1)}, bf16[2,72,512]{2,1,0:T(8,128)(2,1)S(1)}, u32[]{:S(2)}, u32[]{:S(2)}) collective-permute-start(bf16[2,72,512]{2,1,0:T(8,128)(2,1)S(1)} %get-tuple-element.169), channel_id=1, source_target_pairs={{0,6},{2,0},{4,2},{6,4},{1,7},{3,1},{5,3},{7,5},{8,14},{10,8},{12,... | collective-permute-start | bytes 442376 | tf_op jit(solution)/shard_map/ppermute | solution.py:31
  141.7 6.6 %copy-start.8 = (bf16[1280,1024]{1,0:T(8,128)(2,1)S(1)}, bf16[1280,1024]{1,0:T(8,128)(2,1)}, u32[]{:S(2)}) copy-start(bf16[1280,1024]{1,0:T(8,128)(2,1)} %get-tuple-element.112) | copy-start | bytes 7864324
  144.5 6.5 %copy-start.7 = (bf16[1280,1024]{1,0:T(8,128)(2,1)S(1)}, bf16[1280,1024]{1,0:T(8,128)(2,1)}, u32[]{:S(2)}) copy-start(bf16[1280,1024]{1,0:T(8,128)(2,1)} %get-tuple-element.113) | copy-start | bytes 7864324
  144.6 8.1 %collective-permute-start.27 = (bf16[2,72,512]{2,1,0:T(8,128)(2,1)S(1)}, bf16[2,72,512]{2,1,0:T(8,128)(2,1)S(1)}, u32[]{:S(2)}, u32[]{:S(2)}) collective-permute-start(bf16[2,72,512]{2,1,0:T(8,128)(2,1)S(1)} %pad_maximum_fusion.9), channel_id=1, source_target_pairs={{0,8},{8,16},{16,24},{24,0},{1,9},{9,17},{17,25},{25,1},{2,10},{10... | collective-permute-start | bytes 442376 | tf_op jit(solution)/shard_map/ppermute | solution.py:31
  144.6 8.1 %collective-permute-start.28 = (bf16[2,72,512]{2,1,0:T(8,128)(2,1)S(1)}, bf16[2,72,512]{2,1,0:T(8,128)(2,1)S(1)}, u32[]{:S(2)}, u32[]{:S(2)}) collective-permute-start(bf16[2,72,512]{2,1,0:T(8,128)(2,1)S(1)} %pad_maximum_fusion.9), channel_id=1, source_target_pairs={{0,16},{8,24},{16,0},{24,8},{1,17},{9,25},{17,1},{25,9},{2,18},{10... | collective-permute-start | bytes 442376 | tf_op jit(solution)/shard_map/ppermute | solution.py:31
  146.0 6.7 %collective-permute-start.29 = (bf16[2,72,512]{2,1,0:T(8,128)(2,1)S(1)}, bf16[2,72,512]{2,1,0:T(8,128)(2,1)S(1)}, u32[]{:S(2)}, u32[]{:S(2)}) collective-permute-start(bf16[2,72,512]{2,1,0:T(8,128)(2,1)S(1)} %pad_maximum_fusion.9), channel_id=1, source_target_pairs={{0,24},{8,0},{16,8},{24,16},{1,25},{9,1},{17,9},{25,17},{2,26},{10... | collective-permute-start | bytes 442376 | tf_op jit(solution)/shard_map/ppermute | solution.py:31
  153.9 7.8 %collective-permute-start.32 = (bf16[2,64,512]{2,1,0:T(8,128)(2,1)S(1)}, bf16[2,64,512]{2,1,0:T(8,128)(2,1)S(1)}, u32[]{:S(2)}, u32[]{:S(2)}) collective-permute-start(bf16[2,64,512]{2,1,0:T(8,128)(2,1)S(1)} %get-tuple-element.151), channel_id=1, source_target_pairs={{0,2},{2,4},{4,6},{6,0},{1,3},{3,5},{5,7},{7,1},{8,10},{10,12},{12... | collective-permute-start | bytes 393224 | tf_op jit(solution)/shard_map/ppermute | solution.py:31
  155.5 6.2 %collective-permute-start.33 = (bf16[2,64,512]{2,1,0:T(8,128)(2,1)S(1)}, bf16[2,64,512]{2,1,0:T(8,128)(2,1)S(1)}, u32[]{:S(2)}, u32[]{:S(2)}) collective-permute-start(bf16[2,64,512]{2,1,0:T(8,128)(2,1)S(1)} %get-tuple-element.150), channel_id=1, source_target_pairs={{0,4},{2,6},{4,0},{6,2},{1,5},{3,7},{5,1},{7,3},{8,12},{10,14},{12... | collective-permute-start | bytes 393224 | tf_op jit(solution)/shard_map/ppermute | solution.py:31
  156.6 5.0 %collective-permute-start.34 = (bf16[2,64,512]{2,1,0:T(8,128)(2,1)S(1)}, bf16[2,64,512]{2,1,0:T(8,128)(2,1)S(1)}, u32[]{:S(2)}, u32[]{:S(2)}) collective-permute-start(bf16[2,64,512]{2,1,0:T(8,128)(2,1)S(1)} %get-tuple-element.149), channel_id=1, source_target_pairs={{0,6},{2,0},{4,2},{6,4},{1,7},{3,1},{5,3},{7,5},{8,14},{10,8},{12,... | collective-permute-start | bytes 393224 | tf_op jit(solution)/shard_map/ppermute | solution.py:31
  163.6 18.0 %collective-permute-start.35 = (bf16[640,1024]{1,0:T(8,128)(2,1)S(1)}, bf16[640,1024]{1,0:T(8,128)(2,1)S(1)}, u32[]{:S(2)}, u32[]{:S(2)}) collective-permute-start(bf16[640,1024]{1,0:T(8,128)(2,1)S(1)} %readout.3), channel_id=1, source_target_pairs={{0,1},{1,0},{2,3},{3,2},{4,5},{5,4},{6,7},{7,6},{8,9},{9,8},{10,11... | collective-permute-start | bytes 3932168 | tf_op jit(solution)/shard_map/ppermute | solution.py:27
  (3 other events, 1.9 us)
Sparse Core Ops, SparseCore 0:
  10.8 84.6 all-gather.1

commit v3 on v2

--- a/solution.py
+++ b/solution.py
@@ -489,9 +489,8 @@
     rows = rows.transpose(0, 2, 1)
 
     key = project(chunks[:1], [held])
-    query = project(by_y[:1], [columns])
-    held, columns, rest, key, query, cols, rows, decay = together(
-        held, columns, rest, key, query, cols, rows, decay
+    held, columns, rest, key, cols, rows, decay = together(
+        held, columns, rest, key, cols, rows, decay
     )
     blocks = around(held, "xz")
     columns = around(columns, "yy")
@@ -507,7 +506,7 @@
         times(fade_first, fade_second),
         chip_state,
         (
-            lambda: (project(by_y[1:2], columns[1:2], query), by_y[2], by_y[3]),
+            lambda: (project(by_y[:2], columns[:2]), by_y[2], by_y[3]),
             lambda done: project(done[1:], columns[2:], done[0]).astype(BF),
             lambda query: intra(cols, rows, query, key, value),
         ),

time: 191 us -> 191 us (level)
  starting transfers between devices: 56.5 us -> 59.8 us
  waiting for transfers between devices: 21.8 us -> 19.8 us
    ppermute x9, waiting for transfers between devices: 2.2 us -> 0.08 us  [shift(): return lax.ppermute(value, axis, [(i, (i + by) % 4) for i in range(4)])]
    ppermute x6, starting transfers between devices: 17.3 us -> 19.2 us  [swap(): return lax.ppermute(value, 'core', [(0, 1), (1, 0)])]
  transfers between devices with their start and end apart: 37 -> 37, of which waited for: 13 -> 12; matrix products, arithmetic and copies ran while one was open for 28% -> 27% of each run, Pallas kernels for 18% -> 18%
where the time goes in v3:
time: 191 us; the launch traced here: 190 us
  starting transfers between devices  59.8 us (31%)
  matrix products  40.6 us (21%)
  Pallas kernels  37.8 us (20%)
  waiting for transfers between devices  19.8 us (10%)
  between operations  14.3 us (7%)
  other arithmetic  9.47 us (5%)
  local copies, waits for them, and re-layouts  8.47 us (4%)
    ppermute x21, starting transfers between devices, hop(): return lax.ppermute(value, names, pairs)  29.8 us
    dot_general x8, matrix products, project(): term = jnp.dot(chunk, weight, preferred_element_type=F32)  24.7 us
    pallas_call x1, Pallas kernels, normalize(): pl.pallas_call(normalize_kernel, grid_spec=pltpu.PrefetchScalarGridSpec(n...  20.4 us
    ppermute x6, starting transfers between devices, swap(): return lax.ppermute(value, 'core', [(0, 1), (1, 0)])  19.2 us
    dot_general x1, matrix products, per_device(): value = jnp.dot(normed, rest, preferred_element_type=F32).astype(BF)  15.9 us
    ppermute x21, waiting for transfers between devices, hop(): return lax.ppermute(value, names, pairs)  15.8 us
    ppermute x9, starting transfers between devices, shift(): return lax.ppermute(value, axis, [(i, (i + by) % 4) for i in range(4)])  10.8 us
  transfers between devices with their start and end apart: 37, of which 12 were waited for; matrix products, arithmetic and copies ran while one was open for 27% of the time, Pallas kernels for 18%

profile of v3, /device:TPU:25, one launch (start us, length us, event | category | flops | bytes accessed | tf_op | source)
XLA Modules:
  0.0 190.3 jit_solution(7344152170199278996)
XLA Ops:
  7.2 1.2 collective-permute-done.mate_value
  9.1 1.6 prepare_values.1
  14.7 1.6 prepare.1
  20.7 2.0 %collective-permute-start.6 = (bf16[80,512]{1,0:T(8,128)(2,1)}, bf16[80,512]{1,0:T(8,128)(2,1)S(1)}, u32[]{:S(2)}, u32[]{:S(2)}) collective-permute-start(bf16[80,512]{1,0:T(8,128)(2,1)} %get-tuple-element.65.refs_0_), channel_id=1, source_target_pairs={{0,32},{1,33},{2,34},{3,35},{4,36},{5,37},{6,38},{7,39},{8,40},{9,... | collective-permute-start | bytes 245768 | tf_op jit(solution)/shard_map/ppermute | solution.py:42
  22.8 4.4 %collective-permute-done.4.refs_1_ = bf16[80,512]{1,0:T(8,128)(2,1)S(1)} collective-permute-done((bf16[80,512]{1,0:T(8,128)(2,1)}, bf16[80,512]{1,0:T(8,128)(2,1)S(1)}, u32[]{:S(2)}, u32[]{:S(2)}) %collective-permute-start.4) | collective-permute-done | bytes 81952 | tf_op jit(solution)/shard_map/ppermute | solution.py:42
  27.6 0.9 copy-done
  28.4 1.1 assemble.2.refs_0_
  29.6 2.5 %collective-permute-start.7 = (bf16[272,512]{1,0:T(8,128)(2,1)S(1)}, bf16[272,512]{1,0:T(8,128)(2,1)S(1)}, u32[]{:S(2)}, u32[]{:S(2)}) collective-permute-start(bf16[272,512]{1,0:T(8,128)(2,1)S(1)} %assemble.2.refs_0_), channel_id=1, source_target_pairs={{0,24},{1,7},{2,26},{3,1},{4,28},{5,3},{6,30},{7,5},{8,0},{9,15},{... | collective-permute-start | bytes 835592 | tf_op jit(solution)/shard_map/ppermute | solution.py:42
  33.5 2.1 %collective-permute-start.10 = (bf16[64,512]{1,0:T(8,128)(2,1)}, bf16[64,512]{1,0:T(8,128)(2,1)S(1)}, u32[]{:S(2)}, u32[]{:S(2)}) collective-permute-start(bf16[64,512]{1,0:T(8,128)(2,1)} %get-tuple-element.77.refs_0_), channel_id=1, source_target_pairs={{0,24},{1,7},{2,26},{3,1},{4,28},{5,3},{6,30},{7,5},{8,0},{9,15},{... | collective-permute-start | bytes 196616 | tf_op jit(solution)/shard_map/ppermute | solution.py:42
  35.6 3.2 %collective-permute-done.7.refs_1_ = bf16[272,512]{1,0:T(8,128)(2,1)S(1)} collective-permute-done((bf16[272,512]{1,0:T(8,128)(2,1)S(1)}, bf16[272,512]{1,0:T(8,128)(2,1)S(1)}, u32[]{:S(2)}, u32[]{:S(2)}) %collective-permute-start.7) | collective-permute-done | bytes 278560 | tf_op jit(solution)/shard_map/ppermute | solution.py:42
  39.3 3.3 %collective-permute-start.12 = (bf16[64,512]{1,0:T(8,128)(2,1)}, bf16[64,512]{1,0:T(8,128)(2,1)S(1)}, u32[]{:S(2)}, u32[]{:S(2)}) collective-permute-start(bf16[64,512]{1,0:T(8,128)(2,1)} %get-tuple-element.77.refs_0_), channel_id=1, source_target_pairs={{0,8},{1,3},{2,10},{3,5},{4,12},{5,7},{6,14},{7,1},{8,16},{9,11},{... | collective-permute-start | bytes 196616 | tf_op jit(solution)/shard_map/ppermute | solution.py:42
  42.6 1.8 assemble.3
  44.4 4.7 %collective-permute-start.17 = (bf16[16,512]{1,0:T(8,128)(2,1)S(1)}, bf16[16,512]{1,0:T(8,128)(2,1)S(1)}, u32[]{:S(2)}, u32[]{:S(2)}) collective-permute-start(bf16[16,512]{1,0:T(8,128)(2,1)S(1)} %get-tuple-element.88), channel_id=1, source_target_pairs={{0,6},{1,25},{2,0},{3,27},{4,2},{5,29},{6,4},{7,31},{8,14},{9,1},{... | collective-permute-start | bytes 49160 | tf_op jit(solution)/shard_map/ppermute | solution.py:42
  51.1 1.0 weave.2
  52.1 2.1 %collective-permute-start.13 = (bf16[256,512]{1,0:T(8,128)(2,1)S(1)}, bf16[256,512]{1,0:T(8,128)(2,1)S(1)}, u32[]{:S(2)}, u32[]{:S(2)}) collective-permute-start(bf16[256,512]{1,0:T(8,128)(2,1)S(1)} %bitcast.172), channel_id=1, source_target_pairs={{0,6},{1,25},{2,0},{3,27},{4,2},{5,29},{6,4},{7,31},{8,14},{9,1},{... | collective-permute-start | bytes 786440 | tf_op jit(solution)/shard_map/ppermute | solution.py:42
  54.2 1.7 collective-permute-start.14
  56.9 2.8 %collective-permute-done.13 = bf16[256,512]{1,0:T(8,128)(2,1)S(1)} collective-permute-done((bf16[256,512]{1,0:T(8,128)(2,1)S(1)}, bf16[256,512]{1,0:T(8,128)(2,1)S(1)}, u32[]{:S(2)}, u32[]{:S(2)}) %collective-permute-start.13) | collective-permute-done | bytes 262176 | tf_op jit(solution)/shard_map/ppermute | solution.py:42
  59.7 1.5 collective-permute-done.14
  61.2 3.0 %collective-permute-done.15 = bf16[256,512]{1,0:T(8,128)(2,1)S(1)} collective-permute-done((bf16[256,512]{1,0:T(8,128)(2,1)S(1)}, bf16[256,512]{1,0:T(8,128)(2,1)S(1)}, u32[]{:S(2)}, u32[]{:S(2)}) %collective-permute-start.15) | collective-permute-done | bytes 262176 | tf_op jit(solution)/shard_map/ppermute | solution.py:42
  64.3 1.7 weave.3
  66.0 20.4 %normalize.1 = (f32[16,1280]{1,0:T(8,128)}, bf16[1280,4096]{1,0:T(8,128)(2,1)}, bf16[1280,1024]{1,0:T(8,128)(2,1)}, bf16[1280,1024]{1,0:T(8,128)(2,1)}, bf16[128...) custom-call(s32[9]{0:T(128)} %concatenate.69.places, ...), custom_call_target="tpu_custom_call" | custom-call | bytes 33554432 | tf_op jit(solution)/shard_map/normalize/pallas_call | solution.py:87
  87.3 1.2 reduce-window.21
  89.5 5.0 %fusion.48 = f32[1280,512]{1,0:T(8,128)} fusion(bf16[1280,1024]{1,0:T(8,128)(2,1)} %get-tuple-element.92, bf16[1024,512]{1,0:T(8,128)(2,1)} %get-tuple-element.98), kind=kOutput, calls=%fused_computation.153 | convolution fusion | flops 1342177280 | bytes 6291456 | tf_op jit(solution)/shard_map/dot_general | solution.py:267
  94.5 1.1 all-gather.2.cloned.1.call-done
  95.6 2.6 %collective-permute-start.21 = (bf16[1024,512]{1,0:T(8,128)(2,1)}, bf16[1024,512]{1,0:T(8,128)(2,1)}, u32[]{:S(2)}, u32[]{:S(2)}) collective-permute-start(bf16[1024,512]{1,0:T(8,128)(2,1)} %get-tuple-element.98), channel_id=1, source_target_pairs={{0,4},{1,17},{2,6},{3,19},{4,0},{5,21},{6,2},{7,23},{8,12},{9,25},... | collective-permute-start | bytes 3145736 | tf_op jit(solution)/shard_map/ppermute | solution.py:42
  98.6 2.3 %collective-permute-start.20 = (bf16[1024,512]{1,0:T(8,128)(2,1)}, bf16[1024,512]{1,0:T(8,128)(2,1)}, u32[]{:S(2)}, u32[]{:S(2)}) collective-permute-start(bf16[1024,512]{1,0:T(8,128)(2,1)} %get-tuple-element.98), channel_id=1, source_target_pairs={{0,6},{1,25},{2,0},{3,27},{4,2},{5,29},{6,4},{7,31},{8,14},{9,1},{... | collective-permute-start | bytes 3145736 | tf_op jit(solution)/shard_map/ppermute | solution.py:42
  102.3 15.9 %convolution_convert_fusion.left_ref.right_ref = bf16[1280,1024]{1,0:T(8,128)(2,1)S(1)} fusion(bf16[1280,4096]{1,0:T(8,128)(2,1)} %get-tuple-element.101, bf16[4096,1024]{1,0:T(8,128)(2,1)} %all-gather.2.cloned.1.call-done), kind=kOutput, calls=%fused_computation | convolution fusion | flops 10738728960 | bytes 21495808 | tf_op jit(solution)/shard_map/dot_general | solution.py:497
  118.5 1.9 collective-permute-start.31
  120.4 3.7 %fusion.49 = f32[1280,512]{1,0:T(8,128)S(1)} fusion(bf16[1280,1024]{1,0:T(8,128)(2,1)} %get-tuple-element.99, bf16[1024,512]{1,0:T(8,128)(2,1)} %collective-permute-done.21), kind=kOutput, calls=%fused_computation.154 | convolution fusion | flops 1342177280 | bytes 6291456 | tf_op jit(solution)/shard_map/dot_general | solution.py:267
  124.1 2.9 %fusion.50 = f32[1280,512]{1,0:T(8,128)S(1)} fusion(bf16[1280,1024]{1,0:T(8,128)(2,1)S(1)} %copy-done.11, bf16[1024,512]{1,0:T(8,128)(2,1)} %collective-permute-done.22), kind=kOutput, calls=%fused_computation.155 | convolution fusion | flops 1342177280 | bytes 6291456 | tf_op jit(solution)/shard_map/dot_general | solution.py:267
  127.1 3.0 %fusion.2.key_ref = bf16[1280,512]{1,0:T(8,128)(2,1)S(1)} fusion(f32[1280,512]{1,0:T(8,128)S(1)} %fusion.50, f32[1280,512]{1,0:T(8,128)S(1)} %fusion.49, f32[1280,512]{1,0:T(8,128)S(1)} %copy-done.3, bf16[1280,1024]{1,0:T(8,128)(2,1)S(1)} %copy-done.2, bf16[1024,512]{1,0:T(8,128)(2,1)} %collective-permute-done.20), kind=kOutput, calls=%fused_computation.5 | convolution fusion | flops 1344798720 | bytes 12845056 | tf_op jit(solution)/shard_map/dot_general | solution.py:267
  130.1 2.2 %states.1 = bf16[2,2,256,512]{3,2,1,0:T(8,128)(2,1)S(1)} custom-call(f32[2,640,8]{2,1,0:T(8,128)S(1)} %copy.86.cols_ref, bf16[1280,512]{1,0:T(8,128)(2,1)S(1)} %fusion.2.key_ref, bf16[1280,1024]{1,0:T(8,128)(2,1)S(1)} %convolution_convert_fusion.left_ref.right_ref, bf16[1280,1024]{1,0:T(8,128)(2,1)S(1)} %convolution_convert_fusion.left_ref.right_ref), custom_call_target="tpu_custom_call" | custom-call | bytes 1024 | tf_op jit(solution)/shard_map/states/pallas_call | solution.py:284
  133.0 2.1 %collective-permute-start.24 = (bf16[2,72,512]{2,1,0:T(8,128)(2,1)S(1)}, bf16[2,72,512]{2,1,0:T(8,128)(2,1)S(1)}, u32[]{:S(2)}, u32[]{:S(2)}) collective-permute-start(bf16[2,72,512]{2,1,0:T(8,128)(2,1)S(1)} %get-tuple-element.166), channel_id=1, source_target_pairs={{0,4},{2,6},{4,0},{6,2},{1,5},{3,7},{5,1},{7,3},{8,12},{10,14},{12... | collective-permute-start | bytes 442376 | tf_op jit(solution)/shard_map/ppermute | solution.py:31
  135.1 1.2 collective-permute-start.25
  136.3 2.9 %fusion.51 = f32[1280,512]{1,0:T(8,128)S(1)} fusion(bf16[1280,1024]{1,0:T(8,128)(2,1)S(1)} %copy-done.10, bf16[1024,512]{1,0:T(8,128)(2,1)} %collective-permute-done.26), kind=kOutput, calls=%fused_computation.156 | convolution fusion | flops 1342177280 | bytes 6291456 | tf_op jit(solution)/shard_map/dot_general | solution.py:267
  139.3 2.8 %convolution_add_fusion = f32[1280,512]{1,0:T(8,128)S(1)} fusion(f32[1280,512]{1,0:T(8,128)S(1)} %fusion.51, bf16[1280,1024]{1,0:T(8,128)(2,1)S(1)} %copy-done.9, bf16[1024,512]{1,0:T(8,128)(2,1)} %bitcast.26), kind=kOutput, calls=%fused_computation.1 | convolution fusion | flops 1342832640 | bytes 8912896 | tf_op jit(solution)/shard_map/dot_general | solution.py:267
  142.8 1.4 collective-permute-start.28
  144.2 1.7 collective-permute-start.29
  146.0 2.8 %fusion.52 = f32[1280,512]{1,0:T(8,128)S(1)} fusion(bf16[1280,1024]{1,0:T(8,128)(2,1)S(1)} %copy-done.8, bf16[1024,512]{1,0:T(8,128)(2,1)} %collective-permute-done.30), kind=kOutput, calls=%fused_computation.157 | convolution fusion | flops 1342177280 | bytes 6291456 | tf_op jit(solution)/shard_map/dot_general | solution.py:267
  148.8 1.6 add_convert_fusion.query_ref
  152.4 2.2 %collective-permute-start.33 = (bf16[2,64,512]{2,1,0:T(8,128)(2,1)S(1)}, bf16[2,64,512]{2,1,0:T(8,128)(2,1)S(1)}, u32[]{:S(2)}, u32[]{:S(2)}) collective-permute-start(bf16[2,64,512]{2,1,0:T(8,128)(2,1)S(1)} %get-tuple-element.148), channel_id=1, source_target_pairs={{0,4},{2,6},{4,0},{6,2},{1,5},{3,7},{5,1},{7,3},{8,12},{10,14},{12... | collective-permute-start | bytes 393224 | tf_op jit(solution)/shard_map/ppermute | solution.py:31
  154.6 1.2 collective-permute-start.34
  155.8 3.6 %intra.1.intra_ref = f32[1280,1024]{1,0:T(8,128)S(1)} custom-call(f32[2,640,8]{2,1,0:T(8,128)S(1)} %copy.86.cols_ref, f32[2,8,640]{2,1,0:T(8,128)S(1)} %bitcast.178, bf16[1280,512]{1,0:T(8,128)(2,1)S(1)} %add_convert_fusion.query_ref, bf16[1280,512]{1,0:T(8,128)(2,1)S(1)} %fusion.2.key_ref, ...), custom_call_target="tpu_custom_call" | custom-call | bytes 1024 | tf_op jit(solution)/shard_map/intra/pallas_call | solution.py:324
  160.1 1.4 readout.3
  161.4 17.3 %collective-permute-start.35 = (bf16[640,1024]{1,0:T(8,128)(2,1)S(1)}, bf16[640,1024]{1,0:T(8,128)(2,1)S(1)}, u32[]{:S(2)}, u32[]{:S(2)}) collective-permute-start(bf16[640,1024]{1,0:T(8,128)(2,1)S(1)} %readout.3), channel_id=1, source_target_pairs={{0,1},{1,0},{2,3},{3,2},{4,5},{5,4},{6,7},{7,6},{8,9},{9,8},{10,11... | collective-permute-start | bytes 3932168 | tf_op jit(solution)/shard_map/ppermute | solution.py:27
  178.7 1.4 readout.2
  180.1 1.3 collective-permute-done.35
  181.4 2.0 %maximum_select_fusion = bf16[1,640,2048]{2,1,0:T(8,128)(2,1)} fusion(bf16[1,640,1024]{2,1,0:T(8,128)(2,1)S(1)} %bitcast.184, bf16[1,640,1024]{2,1,0:T(8,128)(2,1)S(1)} %bitcast.171, pred[]{:T(512)S(6)} %eq.94), kind=kLoop, calls=%fused_computation.6 | loop fusion | flops 11796480 | bytes 5242881 | tf_op jit(solution)/shard_map/jit(_where)/select_n | solution.py:520
  (157 shorter events, 22.8 us)
Async XLA Ops:
  6.5 44.4 %copy-start.12 = (f32[4]{0:T(128)S(1)}, f32[4]{0:T(128)}, u32[]{:S(2)}) copy-start(f32[4]{0:T(128)} %param.12) | copy-start | bytes 52
  6.5 89.1 %all-gather.2.cloned.1.call-start = ((), (), s32[]{:S(2)}) async-start(), calls=%async_computation | async-start | bytes 8519680 | tf_op jit(solution)/shard_map/all_gather | solution.py:450
  6.5 1.9 collective-permute-start
  8.4 0.7 copy-start.4
  11.4 1.2 collective-permute-start.3
  11.8 1.7 collective-permute-start.1
  12.0 1.5 collective-permute-start.2
  16.4 34.7 %copy-start.1 = (bf16[64,512]{1,0:T(8,128)(2,1)S(1)}, bf16[64,512]{1,0:T(8,128)(2,1)}, u32[]{:S(2)}) copy-start(bf16[64,512]{1,0:T(8,128)(2,1)} %get-tuple-element.77.refs_0_) | copy-start | bytes 196612
  16.4 49.6 %collective-permute-start.16 = (bf16[640,4096]{1,0:T(8,128)(2,1)}, bf16[640,4096]{1,0:T(8,128)(2,1)}, u32[]{:S(2)}, u32[]{:S(2)}) collective-permute-start(bf16[640,4096]{1,0:T(8,128)(2,1)} %bitcast.180), channel_id=1, source_target_pairs={{0,1},{1,0},{2,3},{3,2},{4,5},{5,4},{6,7},{7,6},{8,9},{9,8},{10,11... | collective-permute-start | bytes 15728648 | tf_op jit(solution)/shard_map/ppermute | solution.py:27
  19.6 7.5 %collective-permute-start.4 = (bf16[80,512]{1,0:T(8,128)(2,1)}, bf16[80,512]{1,0:T(8,128)(2,1)S(1)}, u32[]{:S(2)}, u32[]{:S(2)}) collective-permute-start(bf16[80,512]{1,0:T(8,128)(2,1)} %get-tuple-element.65.refs_0_), channel_id=1, source_target_pairs={{0,96},{1,97},{2,98},{3,99},{4,100},{5,101},{6,102},{7,103},{8,104... | collective-permute-start | bytes 245768 | tf_op jit(solution)/shard_map/ppermute | solution.py:42
  20.1 7.0 %collective-permute-start.5 = (bf16[80,512]{1,0:T(8,128)(2,1)}, bf16[80,512]{1,0:T(8,128)(2,1)S(1)}, u32[]{:S(2)}, u32[]{:S(2)}) collective-permute-start(bf16[80,512]{1,0:T(8,128)(2,1)} %get-tuple-element.65.refs_0_), channel_id=1, source_target_pairs={{0,64},{1,65},{2,66},{3,67},{4,68},{5,69},{6,70},{7,71},{8,72},{9,... | collective-permute-start | bytes 245768 | tf_op jit(solution)/shard_map/ppermute | solution.py:42
  20.7 6.8 %collective-permute-start.6 = (bf16[80,512]{1,0:T(8,128)(2,1)}, bf16[80,512]{1,0:T(8,128)(2,1)S(1)}, u32[]{:S(2)}, u32[]{:S(2)}) collective-permute-start(bf16[80,512]{1,0:T(8,128)(2,1)} %get-tuple-element.65.refs_0_), channel_id=1, source_target_pairs={{0,32},{1,33},{2,34},{3,35},{4,36},{5,37},{6,38},{7,39},{8,40},{9,... | collective-permute-start | bytes 245768 | tf_op jit(solution)/shard_map/ppermute | solution.py:42
  27.6 0.9 copy-start
  29.6 9.2 %collective-permute-start.7 = (bf16[272,512]{1,0:T(8,128)(2,1)S(1)}, bf16[272,512]{1,0:T(8,128)(2,1)S(1)}, u32[]{:S(2)}, u32[]{:S(2)}) collective-permute-start(bf16[272,512]{1,0:T(8,128)(2,1)S(1)} %assemble.2.refs_0_), channel_id=1, source_target_pairs={{0,24},{1,7},{2,26},{3,1},{4,28},{5,3},{6,30},{7,5},{8,0},{9,15},{... | collective-permute-start | bytes 835592 | tf_op jit(solution)/shard_map/ppermute | solution.py:42
  32.2 7.1 %collective-permute-start.8 = (bf16[272,512]{1,0:T(8,128)(2,1)S(1)}, bf16[272,512]{1,0:T(8,128)(2,1)S(1)}, u32[]{:S(2)}, u32[]{:S(2)}) collective-permute-start(bf16[272,512]{1,0:T(8,128)(2,1)S(1)} %assemble.2.refs_0_), channel_id=1, source_target_pairs={{0,16},{1,5},{2,18},{3,7},{4,20},{5,1},{6,22},{7,3},{8,24},{9,13},... | collective-permute-start | bytes 835592 | tf_op jit(solution)/shard_map/ppermute | solution.py:42
  32.8 9.8 %collective-permute-start.9 = (bf16[272,512]{1,0:T(8,128)(2,1)S(1)}, bf16[272,512]{1,0:T(8,128)(2,1)S(1)}, u32[]{:S(2)}, u32[]{:S(2)}) collective-permute-start(bf16[272,512]{1,0:T(8,128)(2,1)S(1)} %assemble.2.refs_0_), channel_id=1, source_target_pairs={{0,8},{1,3},{2,10},{3,5},{4,12},{5,7},{6,14},{7,1},{8,16},{9,11},{... | collective-permute-start | bytes 835592 | tf_op jit(solution)/shard_map/ppermute | solution.py:42
  33.5 15.6 %collective-permute-start.10 = (bf16[64,512]{1,0:T(8,128)(2,1)}, bf16[64,512]{1,0:T(8,128)(2,1)S(1)}, u32[]{:S(2)}, u32[]{:S(2)}) collective-permute-start(bf16[64,512]{1,0:T(8,128)(2,1)} %get-tuple-element.77.refs_0_), channel_id=1, source_target_pairs={{0,24},{1,7},{2,26},{3,1},{4,28},{5,3},{6,30},{7,5},{8,0},{9,15},{... | collective-permute-start | bytes 196616 | tf_op jit(solution)/shard_map/ppermute | solution.py:42
  38.8 10.3 %collective-permute-start.11 = (bf16[64,512]{1,0:T(8,128)(2,1)}, bf16[64,512]{1,0:T(8,128)(2,1)S(1)}, u32[]{:S(2)}, u32[]{:S(2)}) collective-permute-start(bf16[64,512]{1,0:T(8,128)(2,1)} %get-tuple-element.77.refs_0_), channel_id=1, source_target_pairs={{0,16},{1,5},{2,18},{3,7},{4,20},{5,1},{6,22},{7,3},{8,24},{9,13},... | collective-permute-start | bytes 196616 | tf_op jit(solution)/shard_map/ppermute | solution.py:42
  39.3 11.8 %collective-permute-start.12 = (bf16[64,512]{1,0:T(8,128)(2,1)}, bf16[64,512]{1,0:T(8,128)(2,1)S(1)}, u32[]{:S(2)}, u32[]{:S(2)}) collective-permute-start(bf16[64,512]{1,0:T(8,128)(2,1)} %get-tuple-element.77.refs_0_), channel_id=1, source_target_pairs={{0,8},{1,3},{2,10},{3,5},{4,12},{5,7},{6,14},{7,1},{8,16},{9,11},{... | collective-permute-start | bytes 196616 | tf_op jit(solution)/shard_map/ppermute | solution.py:42
  44.4 9.8 %collective-permute-start.17 = (bf16[16,512]{1,0:T(8,128)(2,1)S(1)}, bf16[16,512]{1,0:T(8,128)(2,1)S(1)}, u32[]{:S(2)}, u32[]{:S(2)}) collective-permute-start(bf16[16,512]{1,0:T(8,128)(2,1)S(1)} %get-tuple-element.88), channel_id=1, source_target_pairs={{0,6},{1,25},{2,0},{3,27},{4,2},{5,29},{6,4},{7,31},{8,14},{9,1},{... | collective-permute-start | bytes 49160 | tf_op jit(solution)/shard_map/ppermute | solution.py:42
  49.1 6.8 %collective-permute-start.18 = (bf16[16,512]{1,0:T(8,128)(2,1)S(1)}, bf16[16,512]{1,0:T(8,128)(2,1)S(1)}, u32[]{:S(2)}, u32[]{:S(2)}) collective-permute-start(bf16[16,512]{1,0:T(8,128)(2,1)S(1)} %get-tuple-element.88), channel_id=1, source_target_pairs={{0,4},{1,17},{2,6},{3,19},{4,0},{5,21},{6,2},{7,23},{8,12},{9,25},... | collective-permute-start | bytes 49160 | tf_op jit(solution)/shard_map/ppermute | solution.py:42
  49.1 6.8 %collective-permute-start.19 = (bf16[16,512]{1,0:T(8,128)(2,1)S(1)}, bf16[16,512]{1,0:T(8,128)(2,1)S(1)}, u32[]{:S(2)}, u32[]{:S(2)}) collective-permute-start(bf16[16,512]{1,0:T(8,128)(2,1)S(1)} %get-tuple-element.88), channel_id=1, source_target_pairs={{0,2},{1,9},{2,4},{3,11},{4,6},{5,13},{6,0},{7,15},{8,10},{9,17},{... | collective-permute-start | bytes 49160 | tf_op jit(solution)/shard_map/ppermute | solution.py:42
  52.1 7.7 %collective-permute-start.13 = (bf16[256,512]{1,0:T(8,128)(2,1)S(1)}, bf16[256,512]{1,0:T(8,128)(2,1)S(1)}, u32[]{:S(2)}, u32[]{:S(2)}) collective-permute-start(bf16[256,512]{1,0:T(8,128)(2,1)S(1)} %bitcast.172), channel_id=1, source_target_pairs={{0,6},{1,25},{2,0},{3,27},{4,2},{5,29},{6,4},{7,31},{8,14},{9,1},{... | collective-permute-start | bytes 786440 | tf_op jit(solution)/shard_map/ppermute | solution.py:42
  54.2 7.0 %collective-permute-start.14 = (bf16[256,512]{1,0:T(8,128)(2,1)S(1)}, bf16[256,512]{1,0:T(8,128)(2,1)S(1)}, u32[]{:S(2)}, u32[]{:S(2)}) collective-permute-start(bf16[256,512]{1,0:T(8,128)(2,1)S(1)} %bitcast.173), channel_id=1, source_target_pairs={{0,4},{1,17},{2,6},{3,19},{4,0},{5,21},{6,2},{7,23},{8,12},{9,25},... | collective-permute-start | bytes 786440 | tf_op jit(solution)/shard_map/ppermute | solution.py:42
  55.9 8.4 %collective-permute-start.15 = (bf16[256,512]{1,0:T(8,128)(2,1)S(1)}, bf16[256,512]{1,0:T(8,128)(2,1)S(1)}, u32[]{:S(2)}, u32[]{:S(2)}) collective-permute-start(bf16[256,512]{1,0:T(8,128)(2,1)S(1)} %bitcast.174), channel_id=1, source_target_pairs={{0,2},{1,9},{2,4},{3,11},{4,6},{5,13},{6,0},{7,15},{8,10},{9,17},{... | collective-permute-start | bytes 786440 | tf_op jit(solution)/shard_map/ppermute | solution.py:42
  95.6 22.9 %collective-permute-start.21 = (bf16[1024,512]{1,0:T(8,128)(2,1)}, bf16[1024,512]{1,0:T(8,128)(2,1)}, u32[]{:S(2)}, u32[]{:S(2)}) collective-permute-start(bf16[1024,512]{1,0:T(8,128)(2,1)} %get-tuple-element.98), channel_id=1, source_target_pairs={{0,4},{1,17},{2,6},{3,19},{4,0},{5,21},{6,2},{7,23},{8,12},{9,25},... | collective-permute-start | bytes 3145736 | tf_op jit(solution)/shard_map/ppermute | solution.py:42
  98.2 25.9 %collective-permute-start.22 = (bf16[1024,512]{1,0:T(8,128)(2,1)}, bf16[1024,512]{1,0:T(8,128)(2,1)}, u32[]{:S(2)}, u32[]{:S(2)}) collective-permute-start(bf16[1024,512]{1,0:T(8,128)(2,1)} %get-tuple-element.98), channel_id=1, source_target_pairs={{0,2},{1,9},{2,4},{3,11},{4,6},{5,13},{6,0},{7,15},{8,10},{9,17},{... | collective-permute-start | bytes 3145736 | tf_op jit(solution)/shard_map/ppermute | solution.py:42
  98.6 28.4 %collective-permute-start.20 = (bf16[1024,512]{1,0:T(8,128)(2,1)}, bf16[1024,512]{1,0:T(8,128)(2,1)}, u32[]{:S(2)}, u32[]{:S(2)}) collective-permute-start(bf16[1024,512]{1,0:T(8,128)(2,1)} %get-tuple-element.98), channel_id=1, source_target_pairs={{0,6},{1,25},{2,0},{3,27},{4,2},{5,29},{6,4},{7,31},{8,14},{9,1},{... | collective-permute-start | bytes 3145736 | tf_op jit(solution)/shard_map/ppermute | solution.py:42
  100.9 34.2 %collective-permute-start.26 = (bf16[1024,512]{1,0:T(8,128)(2,1)}, bf16[1024,512]{1,0:T(8,128)(2,1)}, u32[]{:S(2)}, u32[]{:S(2)}) collective-permute-start(bf16[1024,512]{1,0:T(8,128)(2,1)} %bitcast.26), channel_id=1, source_target_pairs={{0,96},{1,97},{2,98},{3,99},{4,100},{5,101},{6,102},{7,103},{8,104... | collective-permute-start | bytes 3145736 | tf_op jit(solution)/shard_map/ppermute | solution.py:42
  101.5 44.5 %collective-permute-start.30 = (bf16[1024,512]{1,0:T(8,128)(2,1)}, bf16[1024,512]{1,0:T(8,128)(2,1)}, u32[]{:S(2)}, u32[]{:S(2)}) collective-permute-start(bf16[1024,512]{1,0:T(8,128)(2,1)} %bitcast.26), channel_id=1, source_target_pairs={{0,64},{1,65},{2,66},{3,67},{4,68},{5,69},{6,70},{7,71},{8,72},{9,... | collective-permute-start | bytes 3145736 | tf_op jit(solution)/shard_map/ppermute | solution.py:42
  118.5 30.2 %collective-permute-start.31 = (bf16[1024,512]{1,0:T(8,128)(2,1)}, bf16[1024,512]{1,0:T(8,128)(2,1)S(1)}, u32[]{:S(2)}, u32[]{:S(2)}) collective-permute-start(bf16[1024,512]{1,0:T(8,128)(2,1)} %bitcast.26), channel_id=1, source_target_pairs={{0,32},{1,33},{2,34},{3,35},{4,36},{5,37},{6,38},{7,39},{8,40},{9,... | collective-permute-start | bytes 3145736 | tf_op jit(solution)/shard_map/ppermute | solution.py:42
  120.4 3.7 %copy-start.11 = (bf16[1280,1024]{1,0:T(8,128)(2,1)S(1)}, bf16[1280,1024]{1,0:T(8,128)(2,1)}, u32[]{:S(2)}) copy-start(bf16[1280,1024]{1,0:T(8,128)(2,1)} %get-tuple-element.100) | copy-start | bytes 7864324
  124.1 2.9 %copy-start.2 = (bf16[1280,1024]{1,0:T(8,128)(2,1)S(1)}, bf16[1280,1024]{1,0:T(8,128)(2,1)}, u32[]{:S(2)}) copy-start(bf16[1280,1024]{1,0:T(8,128)(2,1)} %get-tuple-element.97) | copy-start | bytes 7864324
  124.1 2.9 %copy-start.3 = (f32[1280,512]{1,0:T(8,128)S(1)}, f32[1280,512]{1,0:T(8,128)}, u32[]{:S(2)}) copy-start(f32[1280,512]{1,0:T(8,128)} %fusion.48) | copy-start | bytes 7864324
  132.5 3.9 %copy-start.10 = (bf16[1280,1024]{1,0:T(8,128)(2,1)S(1)}, bf16[1280,1024]{1,0:T(8,128)(2,1)}, u32[]{:S(2)}) copy-start(bf16[1280,1024]{1,0:T(8,128)(2,1)} %get-tuple-element.105) | copy-start | bytes 7864324
  132.9 9.2 %collective-permute-start.23 = (bf16[2,72,512]{2,1,0:T(8,128)(2,1)S(1)}, bf16[2,72,512]{2,1,0:T(8,128)(2,1)S(1)}, u32[]{:S(2)}, u32[]{:S(2)}) collective-permute-start(bf16[2,72,512]{2,1,0:T(8,128)(2,1)S(1)} %get-tuple-element.165), channel_id=1, source_target_pairs={{0,2},{2,4},{4,6},{6,0},{1,3},{3,5},{5,7},{7,1},{8,10},{10,12},{12... | collective-permute-start | bytes 442376 | tf_op jit(solution)/shard_map/ppermute | solution.py:31
  133.0 9.1 %collective-permute-start.24 = (bf16[2,72,512]{2,1,0:T(8,128)(2,1)S(1)}, bf16[2,72,512]{2,1,0:T(8,128)(2,1)S(1)}, u32[]{:S(2)}, u32[]{:S(2)}) collective-permute-start(bf16[2,72,512]{2,1,0:T(8,128)(2,1)S(1)} %get-tuple-element.166), channel_id=1, source_target_pairs={{0,4},{2,6},{4,0},{6,2},{1,5},{3,7},{5,1},{7,3},{8,12},{10,14},{12... | collective-permute-start | bytes 442376 | tf_op jit(solution)/shard_map/ppermute | solution.py:31
  135.1 7.0 %collective-permute-start.25 = (bf16[2,72,512]{2,1,0:T(8,128)(2,1)S(1)}, bf16[2,72,512]{2,1,0:T(8,128)(2,1)S(1)}, u32[]{:S(2)}, u32[]{:S(2)}) collective-permute-start(bf16[2,72,512]{2,1,0:T(8,128)(2,1)S(1)} %get-tuple-element.167), channel_id=1, source_target_pairs={{0,6},{2,0},{4,2},{6,4},{1,7},{3,1},{5,3},{7,5},{8,14},{10,8},{12,... | collective-permute-start | bytes 442376 | tf_op jit(solution)/shard_map/ppermute | solution.py:31
  136.3 2.9 %copy-start.9 = (bf16[1280,1024]{1,0:T(8,128)(2,1)S(1)}, bf16[1280,1024]{1,0:T(8,128)(2,1)}, u32[]{:S(2)}) copy-start(bf16[1280,1024]{1,0:T(8,128)(2,1)} %get-tuple-element.103) | copy-start | bytes 7864324
  142.1 3.9 %copy-start.8 = (bf16[1280,1024]{1,0:T(8,128)(2,1)S(1)}, bf16[1280,1024]{1,0:T(8,128)(2,1)}, u32[]{:S(2)}) copy-start(bf16[1280,1024]{1,0:T(8,128)(2,1)} %get-tuple-element.110) | copy-start | bytes 7864324
  142.7 6.0 %copy-start.7 = (bf16[1280,1024]{1,0:T(8,128)(2,1)S(1)}, bf16[1280,1024]{1,0:T(8,128)(2,1)}, u32[]{:S(2)}) copy-start(bf16[1280,1024]{1,0:T(8,128)(2,1)} %get-tuple-element.111) | copy-start | bytes 7864324
  142.8 7.7 %collective-permute-start.27 = (bf16[2,72,512]{2,1,0:T(8,128)(2,1)S(1)}, bf16[2,72,512]{2,1,0:T(8,128)(2,1)S(1)}, u32[]{:S(2)}, u32[]{:S(2)}) collective-permute-start(bf16[2,72,512]{2,1,0:T(8,128)(2,1)S(1)} %pad_maximum_fusion.9), channel_id=1, source_target_pairs={{0,8},{8,16},{16,24},{24,0},{1,9},{9,17},{17,25},{25,1},{2,10},{10... | collective-permute-start | bytes 442376 | tf_op jit(solution)/shard_map/ppermute | solution.py:31
  142.8 7.6 %collective-permute-start.28 = (bf16[2,72,512]{2,1,0:T(8,128)(2,1)S(1)}, bf16[2,72,512]{2,1,0:T(8,128)(2,1)S(1)}, u32[]{:S(2)}, u32[]{:S(2)}) collective-permute-start(bf16[2,72,512]{2,1,0:T(8,128)(2,1)S(1)} %pad_maximum_fusion.9), channel_id=1, source_target_pairs={{0,16},{8,24},{16,0},{24,8},{1,17},{9,25},{17,1},{25,9},{2,18},{10... | collective-permute-start | bytes 442376 | tf_op jit(solution)/shard_map/ppermute | solution.py:31
  144.2 6.2 %collective-permute-start.29 = (bf16[2,72,512]{2,1,0:T(8,128)(2,1)S(1)}, bf16[2,72,512]{2,1,0:T(8,128)(2,1)S(1)}, u32[]{:S(2)}, u32[]{:S(2)}) collective-permute-start(bf16[2,72,512]{2,1,0:T(8,128)(2,1)S(1)} %pad_maximum_fusion.9), channel_id=1, source_target_pairs={{0,24},{8,0},{16,8},{24,16},{1,25},{9,1},{17,9},{25,17},{2,26},{10... | collective-permute-start | bytes 442376 | tf_op jit(solution)/shard_map/ppermute | solution.py:31
  151.6 7.8 %collective-permute-start.32 = (bf16[2,64,512]{2,1,0:T(8,128)(2,1)S(1)}, bf16[2,64,512]{2,1,0:T(8,128)(2,1)S(1)}, u32[]{:S(2)}, u32[]{:S(2)}) collective-permute-start(bf16[2,64,512]{2,1,0:T(8,128)(2,1)S(1)} %get-tuple-element.149), channel_id=1, source_target_pairs={{0,2},{2,4},{4,6},{6,0},{1,3},{3,5},{5,7},{7,1},{8,10},{10,12},{12... | collective-permute-start | bytes 393224 | tf_op jit(solution)/shard_map/ppermute | solution.py:31
  152.4 7.1 %collective-permute-start.33 = (bf16[2,64,512]{2,1,0:T(8,128)(2,1)S(1)}, bf16[2,64,512]{2,1,0:T(8,128)(2,1)S(1)}, u32[]{:S(2)}, u32[]{:S(2)}) collective-permute-start(bf16[2,64,512]{2,1,0:T(8,128)(2,1)S(1)} %get-tuple-element.148), channel_id=1, source_target_pairs={{0,4},{2,6},{4,0},{6,2},{1,5},{3,7},{5,1},{7,3},{8,12},{10,14},{12... | collective-permute-start | bytes 393224 | tf_op jit(solution)/shard_map/ppermute | solution.py:31
  154.6 4.9 %collective-permute-start.34 = (bf16[2,64,512]{2,1,0:T(8,128)(2,1)S(1)}, bf16[2,64,512]{2,1,0:T(8,128)(2,1)S(1)}, u32[]{:S(2)}, u32[]{:S(2)}) collective-permute-start(bf16[2,64,512]{2,1,0:T(8,128)(2,1)S(1)} %get-tuple-element.147), channel_id=1, source_target_pairs={{0,6},{2,0},{4,2},{6,4},{1,7},{3,1},{5,3},{7,5},{8,14},{10,8},{12,... | collective-permute-start | bytes 393224 | tf_op jit(solution)/shard_map/ppermute | solution.py:31
  161.4 20.0 %collective-permute-start.35 = (bf16[640,1024]{1,0:T(8,128)(2,1)S(1)}, bf16[640,1024]{1,0:T(8,128)(2,1)S(1)}, u32[]{:S(2)}, u32[]{:S(2)}) collective-permute-start(bf16[640,1024]{1,0:T(8,128)(2,1)S(1)} %readout.3), channel_id=1, source_target_pairs={{0,1},{1,0},{2,3},{3,2},{4,5},{5,4},{6,7},{7,6},{8,9},{9,8},{10,11... | collective-permute-start | bytes 3932168 | tf_op jit(solution)/shard_map/ppermute | solution.py:27
  (2 other events, 1.2 us)
Sparse Core Ops, SparseCore 0:
  10.8 84.7 all-gather.1
